TPU v7x, 32 devices: a whole 2x2x4 slice. The times are simulated.
32 devices in a mesh: dp: 16 (over z, x, core), mp: 2 (over y).
Axes of the slice: x: 2, y: 2, z: 4, core: 2. Of those that a mesh axis runs over, the one named last changes fastest.
Arguments:
- tokens: bfloat16 [48, 512, 768], P('dp', 'mp'), may hold values from -6 to 6
- segment_ids: int32 [48, 512], P('dp'), may hold values from 0 to 3, never falling along the last dimension, each value on 1 to 256 neighbouring positions
- out_grad: bfloat16 [48, 512, 768], P('dp', 'mp'), may hold values from -6 to 6
- t_qkv: bfloat16 [3, 768, 768], P(None, 'dp', 'mp'), may hold values from -0.21875 to 0.21875
- t_qv_bias: bfloat16 [2, 768], P(None, 'mp'), may hold values from -3 to 3
- t_out: bfloat16 [768, 768], P('mp', 'dp'), may hold values from -2 to 2
- t_up: bfloat16 [768, 3072], P('dp', 'mp'), may hold values from -0.21875 to 0.21875
- t_up_bias: bfloat16 [3072], P('mp'), may hold values from -3 to 3
- t_down: bfloat16 [3072, 768], P('mp', 'dp'), may hold values from -0.21875 to 0.21875
- t_gains: bfloat16 [2, 768], P(None, 'dp'), may hold values from 0.5 to 1.5
- t_shifts: bfloat16 [4, 768], P(None, 'dp'), may hold values from -3 to 3
- s_qkv: bfloat16 [3, 768, 384], P(None, 'dp', 'mp'), may hold values from -0.21875 to 0.21875
- s_qv_bias: bfloat16 [2, 384], P(None, 'mp'), may hold values from -3 to 3
- s_out: bfloat16 [384, 768], P('mp', 'dp'), may hold values from -3 to 3
- s_up: bfloat16 [768, 1536], P('dp', 'mp'), may hold values from -0.21875 to 0.21875
- s_up_bias: bfloat16 [1536], P('mp'), may hold values from -3 to 3
- s_down: bfloat16 [1536, 768], P('mp', 'dp'), may hold values from -0.3125 to 0.3125
- s_gains: bfloat16 [2, 768], P(None, 'dp'), may hold values from 0.5 to 1.5
- s_shifts: bfloat16 [4, 768], P(None, 'dp'), may hold values from -3 to 3
Outputs:
- output: float32 [48, 512, 768], P('dp', 'mp')
- input_grad: float32 [48, 512, 768], P('dp', 'mp')
- grad_t_qkv: float32 [3, 768, 768], P(None, 'dp', 'mp')
- grad_t_qv_bias: float32 [2, 768], P(None, 'mp')
- grad_t_out: float32 [768, 768], P('mp', 'dp')
- grad_t_up: float32 [768, 3072], P('dp', 'mp')
- grad_t_up_bias: float32 [3072], P('mp')
- grad_t_down: float32 [3072, 768], P('mp', 'dp')
- grad_t_gains: float32 [2, 768], P(None, 'dp')
- grad_t_shifts: float32 [4, 768], P(None, 'dp')
- grad_s_qkv: float32 [3, 768, 384], P(None, 'dp', 'mp')
- grad_s_qv_bias: float32 [2, 384], P(None, 'mp')
- grad_s_out: float32 [384, 768], P('mp', 'dp')
- grad_s_up: float32 [768, 1536], P('dp', 'mp')
- grad_s_up_bias: float32 [1536], P('mp')
- grad_s_down: float32 [1536, 768], P('mp', 'dp')
- grad_s_gains: float32 [2, 768], P(None, 'dp')
- grad_s_shifts: float32 [4, 768], P(None, 'dp')
Inputs may be any that keep to these rules, and one draw needn't show every extreme that they name: `segment_ids`: segment numbers never fall along a row; a segment holds at most 256 positions of one row.
All inputs are finite; a program needn't handle non-finite values.
Results may differ from a plain program's by a relative error of at most 0.035.
Values may be sent and summed in bfloat16 or wider, within the bound.
No kernel may reach another device: no remote copies, remote signals or barrier semaphores. Data moves between devices by JAX's collectives and lax.ppermute only.
A program may use at most 256 MiB of HBM per device.

v0:
```python
import jax
import jax.numpy as jnp
from jax import lax
from jax.sharding import PartitionSpec as P

D = 768
HEAD_DIM = 64
LEN = 512
MICRO = 3


def fetch_layer(shards):
    return (
        lax.all_gather(shards[0], "dp", axis=1, tiled=True),
        lax.all_gather(shards[1], "dp", axis=1, tiled=True),
        lax.all_gather(shards[2], "dp", axis=0, tiled=True),
        lax.all_gather(shards[3], "dp", axis=1, tiled=True),
        lax.all_gather(shards[4], "dp", axis=1, tiled=True),
        lax.all_gather(shards[5], "dp", axis=1, tiled=True),
    )


def gather_rows(share_low, rows):
    whole = lax.all_gather(share_low.reshape(rows, -1, D), "mp", axis=1, tiled=True)
    return whole.reshape(-1, D)


def forward_sum(partial_sum, rows):
    share = lax.psum_scatter(
        partial_sum.reshape(rows, LEN, D).astype(jnp.bfloat16),
        "mp",
        scatter_dimension=1,
        tiled=True,
    ).astype(jnp.float32)
    return share.reshape(-1, D)


def backward_sum(partial_sum, rows):
    share = lax.psum_scatter(
        partial_sum.reshape(rows, LEN, D).astype(jnp.bfloat16),
        "mp",
        scatter_dimension=1,
        tiled=True,
    ).astype(jnp.float32)
    return share.reshape(-1, D)


def shard_grads(grads):
    return (
        lax.psum_scatter(grads[0], "dp", scatter_dimension=1, tiled=True),
        lax.psum_scatter(grads[1], "dp", scatter_dimension=1, tiled=True),
        lax.psum_scatter(grads[2], "dp", scatter_dimension=0, tiled=True),
        lax.psum_scatter(grads[3], "dp", scatter_dimension=1, tiled=True),
    )


def norm_layer(value, gain, shift):
    center = value - jnp.mean(value, axis=-1, keepdims=True)
    spread = jnp.mean(center * center, axis=-1, keepdims=True)
    recip = lax.rsqrt(spread + 1e-06)
    normed = center * recip
    return (normed * gain + shift, (normed, recip))


def norm_back(grad, kept, gain):
    normed, recip = kept
    scaled = grad * gain
    d_gain = jnp.sum(grad * normed, axis=0)
    d_shift = jnp.sum(grad, axis=0)
    mean_one = jnp.mean(scaled, axis=-1, keepdims=True)
    mean_two = jnp.mean(scaled * normed, axis=-1, keepdims=True)
    return (recip * (scaled - mean_one - normed * mean_two), d_gain, d_shift)


def masked_scores(query4, keys4, segs):
    scale = HEAD_DIM ** (-0.5)
    same = (segs[:, :, None] == segs[:, None, :])[:, None]
    scores = (
        jnp.einsum("rqhe,rkhe->rhqk", query4, keys4, preferred_element_type=jnp.float32) * scale
    )
    return jnp.where(same, scores, -1000000000.0)


def forward_layer(inputs, segs, full, qv_bias, up_bias):
    qkv_w, out_w, up_w, down_w, gains, shifts = full
    gains = gains.astype(jnp.float32)
    shifts = shifts.astype(jnp.float32)
    qv_bias = qv_bias.astype(jnp.float32)
    rows, length = segs.shape
    width = qkv_w.shape[2]
    heads = width // HEAD_DIM
    inputs_low = gather_rows(inputs.astype(jnp.bfloat16), rows)
    proj = jnp.einsum("nd,kdh->knh", inputs_low, qkv_w, preferred_element_type=jnp.float32)
    query = (proj[0] + qv_bias[0]).astype(jnp.bfloat16)
    keys = proj[1].astype(jnp.bfloat16)
    values = (proj[2] + qv_bias[1]).astype(jnp.bfloat16)
    query4 = query.reshape(rows, length, heads, HEAD_DIM)
    keys4 = keys.reshape(rows, length, heads, HEAD_DIM)
    values4 = values.reshape(rows, length, heads, HEAD_DIM)
    scores = masked_scores(query4, keys4, segs)
    top = jnp.max(scores, axis=-1, keepdims=True)
    expo = jnp.exp(scores - top)
    total = jnp.sum(expo, axis=-1, keepdims=True)
    logsum = top + jnp.log(total)
    probs = (expo / total).astype(jnp.bfloat16)
    context = jnp.einsum("rhqk,rkhe->rqhe", probs, values4, preferred_element_type=jnp.float32)
    context = context.reshape(rows * length, width).astype(jnp.bfloat16)
    attn = forward_sum(jnp.dot(context, out_w, preferred_element_type=jnp.float32), rows)
    mid = inputs + attn + shifts[0]
    hidden, first_norm = norm_layer(mid, gains[0], shifts[1])
    hidden_low = gather_rows(hidden.astype(jnp.bfloat16), rows)
    pre = jnp.dot(hidden_low, up_w, preferred_element_type=jnp.float32) + up_bias.astype(
        jnp.float32
    )
    act = jax.nn.gelu(pre, approximate=False).astype(jnp.bfloat16)
    ffn = forward_sum(jnp.dot(act, down_w, preferred_element_type=jnp.float32), rows)
    final = hidden + ffn + shifts[2]
    output, second_norm = norm_layer(final, gains[1], shifts[3])
    saved = (
        inputs_low,
        query4,
        keys4,
        values4,
        logsum,
        context,
        first_norm,
        hidden_low,
        pre,
        act,
        second_norm,
    )
    return (output, saved)


def backward_layer(grad_out, segs, full, saved):
    qkv_w, out_w, up_w, down_w, gains, shifts = full
    gains = gains.astype(jnp.float32)
    (
        inputs_low,
        query4,
        keys4,
        values4,
        logsum,
        context,
        first_norm,
        hidden_low,
        pre,
        act,
        second_norm,
    ) = saved
    rows, length, heads, _ = query4.shape
    width = heads * HEAD_DIM
    scale = HEAD_DIM ** (-0.5)
    d_final, d_gain_two, d_shift_three = norm_back(grad_out, second_norm, gains[1])
    d_shift_two = jnp.sum(d_final, axis=0)
    d_final_low = gather_rows(d_final.astype(jnp.bfloat16), rows)
    d_down = jnp.einsum("nf,nd->fd", act, d_final_low, preferred_element_type=jnp.float32)
    d_act = jnp.einsum("nd,fd->nf", d_final_low, down_w, preferred_element_type=jnp.float32)
    _, gelu_pull = jax.vjp(lambda value: jax.nn.gelu(value, approximate=False), pre)
    d_pre = gelu_pull(d_act)[0].astype(jnp.bfloat16)
    d_up_bias = jnp.sum(d_pre.astype(jnp.float32), axis=0)
    d_up = jnp.einsum("nd,nf->df", hidden_low, d_pre, preferred_element_type=jnp.float32)
    d_hidden = d_final + backward_sum(
        jnp.einsum("nf,df->nd", d_pre, up_w, preferred_element_type=jnp.float32), rows
    )
    d_mid, d_gain_one, d_shift_one = norm_back(d_hidden, first_norm, gains[0])
    d_shift_zero = jnp.sum(d_mid, axis=0)
    d_mid_low = gather_rows(d_mid.astype(jnp.bfloat16), rows)
    d_out = jnp.einsum("nh,nd->hd", context, d_mid_low, preferred_element_type=jnp.float32)
    d_context = jnp.einsum("nd,hd->nh", d_mid_low, out_w, preferred_element_type=jnp.float32)
    d_context4 = d_context.astype(jnp.bfloat16).reshape(rows, length, heads, HEAD_DIM)
    scores = masked_scores(query4, keys4, segs)
    probs = jnp.exp(scores - logsum)
    d_values = jnp.einsum(
        "rhqk,rqhe->rkhe",
        probs.astype(jnp.bfloat16),
        d_context4,
        preferred_element_type=jnp.float32,
    )
    d_probs = jnp.einsum("rqhe,rkhe->rhqk", d_context4, values4, preferred_element_type=jnp.float32)
    inner = jnp.sum(probs * d_probs, axis=-1, keepdims=True)
    d_scores = (probs * (d_probs - inner)).astype(jnp.bfloat16)
    d_query = (
        jnp.einsum("rhqk,rkhe->rqhe", d_scores, keys4, preferred_element_type=jnp.float32) * scale
    )
    d_keys = (
        jnp.einsum("rhqk,rqhe->rkhe", d_scores, query4, preferred_element_type=jnp.float32) * scale
    )
    d_proj = (
        jnp.stack([d_query, d_keys, d_values]).reshape(3, rows * length, width).astype(jnp.bfloat16)
    )
    d_proj_wide = d_proj.astype(jnp.float32)
    d_qv_bias = jnp.stack([jnp.sum(d_proj_wide[0], axis=0), jnp.sum(d_proj_wide[2], axis=0)])
    d_qkv = jnp.einsum("nd,knh->kdh", inputs_low, d_proj, preferred_element_type=jnp.float32)
    d_inputs = d_mid + backward_sum(
        jnp.einsum("knh,kdh->nd", d_proj, qkv_w, preferred_element_type=jnp.float32), rows
    )
    grads = (d_qkv, d_out, d_up, d_down)
    norm_grads = jnp.stack(
        [d_gain_one, d_gain_two, d_shift_zero, d_shift_one, d_shift_two, d_shift_three]
    )
    return (d_inputs, grads, norm_grads, (d_qv_bias, d_up_bias))


def add_tree(left, right):
    return jax.tree.map(lambda one, two: one + two, left, right)


def on_device(
    tokens,
    segment_ids,
    out_grad,
    t_qkv,
    t_qv_bias,
    t_out,
    t_up,
    t_up_bias,
    t_down,
    t_gains,
    t_shifts,
    s_qkv,
    s_qv_bias,
    s_out,
    s_up,
    s_up_bias,
    s_down,
    s_gains,
    s_shifts,
):
    teacher = (t_qkv, t_out, t_up, t_down, t_gains, t_shifts)
    student = (s_qkv, s_out, s_up, s_down, s_gains, s_shifts)
    per_batch = tokens.shape[0] // MICRO
    outputs = []
    input_grads = []
    teacher_acc = None
    student_acc = None
    bias_acc = None
    norm_acc = None
    for batch in range(MICRO):
        segs = segment_ids[batch * per_batch : (batch + 1) * per_batch]
        inputs = (
            tokens[batch * per_batch : (batch + 1) * per_batch].reshape(-1, D).astype(jnp.float32)
        )
        grad_out = (
            out_grad[batch * per_batch : (batch + 1) * per_batch].reshape(-1, D).astype(jnp.float32)
        )
        teacher_full = fetch_layer(teacher)
        student_full = fetch_layer(student)
        first, teacher_saved = forward_layer(inputs, segs, teacher_full, t_qv_bias, t_up_bias)
        second, student_saved = forward_layer(first, segs, student_full, s_qv_bias, s_up_bias)
        outputs.append(second.reshape(per_batch, -1, D))
        teacher_full = fetch_layer(teacher)
        student_full = fetch_layer(student)
        d_first, student_grads, student_norms, student_bias = backward_layer(
            grad_out, segs, student_full, student_saved
        )
        d_inputs, teacher_grads, teacher_norms, teacher_bias = backward_layer(
            d_first, segs, teacher_full, teacher_saved
        )
        input_grads.append(d_inputs.reshape(per_batch, -1, D))
        teacher_grads = shard_grads(teacher_grads)
        student_grads = shard_grads(student_grads)
        biases = teacher_bias + student_bias
        norms = jnp.concatenate([teacher_norms, student_norms], axis=0)
        if batch == 0:
            teacher_acc, student_acc, bias_acc, norm_acc = (
                teacher_grads,
                student_grads,
                biases,
                norms,
            )
        else:
            teacher_acc = add_tree(teacher_acc, teacher_grads)
            student_acc = add_tree(student_acc, student_grads)
            bias_acc = add_tree(bias_acc, biases)
            norm_acc = norm_acc + norms
    bias_tot = lax.psum((bias_acc[0], bias_acc[1], bias_acc[2], bias_acc[3]), "dp")
    norm_tot = lax.psum(norm_acc, ("dp", "mp"))
    piece = D // lax.axis_size("dp")
    norm_mine = lax.dynamic_slice_in_dim(norm_tot, lax.axis_index("dp") * piece, piece, 1)
    output = jnp.concatenate(outputs, axis=0)
    input_grad = jnp.concatenate(input_grads, axis=0)
    return (
        output,
        input_grad,
        teacher_acc[0],
        bias_tot[0],
        teacher_acc[1],
        teacher_acc[2],
        bias_tot[1],
        teacher_acc[3],
        norm_mine[0:2],
        norm_mine[2:6],
        student_acc[0],
        bias_tot[2],
        student_acc[1],
        student_acc[2],
        bias_tot[3],
        student_acc[3],
        norm_mine[6:8],
        norm_mine[8:12],
    )


def solution(mesh):
    placed = (
        P("dp", "mp", None),
        P("dp", None),
        P("dp", "mp", None),
        P(None, "dp", "mp"),
        P(None, "mp"),
        P("mp", "dp"),
        P("dp", "mp"),
        P("mp"),
        P("mp", "dp"),
        P(None, "dp"),
        P(None, "dp"),
        P(None, "dp", "mp"),
        P(None, "mp"),
        P("mp", "dp"),
        P("dp", "mp"),
        P("mp"),
        P("mp", "dp"),
        P(None, "dp"),
        P(None, "dp"),
    )
    return jax.shard_map(
        on_device,
        mesh=mesh,
        in_specs=placed,
        out_specs=(
            P("dp", "mp", None),
            P("dp", "mp", None),
            P(None, "dp", "mp"),
            P(None, "mp"),
            P("mp", "dp"),
            P("dp", "mp"),
            P("mp"),
            P("mp", "dp"),
            P(None, "dp"),
            P(None, "dp"),
            P(None, "dp", "mp"),
            P(None, "mp"),
            P("mp", "dp"),
            P("dp", "mp"),
            P("mp"),
            P("mp", "dp"),
            P(None, "dp"),
            P(None, "dp"),
        ),
        check_vma=False,
    )
```

profile of v0, /device:TPU:0, one launch (start us, length us, event | category | flops | bytes accessed | tf_op | source)
XLA Modules:
  0.0 1588.1 jit_solution(341464673380209258)
XLA Ops:
  10.2 12.8 all_gather.73
  23.0 11.0 all_gather.182
  34.0 10.3 all_gather.88
  45.6 22.8 %all_gather.74 = bf16[384,768]{0,1:T(8,128)(2,1)S(1)} all-gather(bf16[384,48]{0,1:T(8,128)(2,1)S(1)} %copy-done.350), channel_id=1, replica_groups=mesh['dp'=16,'mp'=2] {'dp'}, dimensions={1}, use_global_device_ids=true | all-gather | bytes 626688 | tf_op jit(solution)/shard_map/all_gather | solution.py:15
  103.9 17.3 %all-gather.1 = bf16[16,48,2]{1,2,0:T(2,128)(2,1)S(1)} all-gather(bf16[1,48,2]{1,2,0:T(2,128)(2,1)S(1)} %bitcast.977), channel_id=1, replica_groups=mesh['dp'=16,'mp'=2] {'dp'}, dimensions={0}, use_global_device_ids=true | all-gather | bytes 3264 | tf_op jit(solution)/shard_map/all_gather | solution.py:18
  121.3 18.8 %all-gather = bf16[16,48,4]{1,2,0:T(4,128)(2,1)S(1)} all-gather(bf16[1,48,4]{1,2,0:T(4,128)(2,1)S(1)} %bitcast.975), channel_id=1, replica_groups=mesh['dp'=16,'mp'=2] {'dp'}, dimensions={0}, use_global_device_ids=true | all-gather | bytes 6528 | tf_op jit(solution)/shard_map/all_gather | solution.py:19
  145.8 12.0 all_gather.77
  157.8 11.5 all_gather.89
  169.3 12.6 all-gather.12.cloned.1.call-done
  181.9 11.2 multiply_convert_fusion.7
  193.1 32.2 %all-gather.14.cloned.1.call-done = bf16[1536,768]{0,1:T(8,128)(2,1)} async-done(((bf16[1536,48]{0,1:T(8,128)(2,1)}), bf16[1536,768]{0,1:T(8,128)(2,1)}) %all-gather.14.cloned.1.call-update) | async-done | bytes 2359312 | tf_op jit(solution)/shard_map/all_gather | solution.py:17
  225.3 4.5 fusion.76
  229.9 10.9 multiply_convert_fusion.8
  245.8 20.3 %all_gather.82 = bf16[192,768]{0,1:T(8,128)(2,1)S(1)} all-gather(bf16[192,48]{0,1:T(8,128)(2,1)S(1)} %copy-done.384), channel_id=1, replica_groups=mesh['dp'=16,'mp'=2] {'dp'}, dimensions={1}, use_global_device_ids=true | all-gather | bytes 313344 | tf_op jit(solution)/shard_map/all_gather | solution.py:15
  266.1 22.8 %all_gather.81 = bf16[3,768,192]{2,1,0:T(8,128)(2,1)} all-gather(bf16[3,48,192]{2,1,0:T(8,128)(2,1)S(1)} %copy-done.302), channel_id=1, replica_groups=mesh['dp'=16,'mp'=2] {'dp'}, dimensions={1}, use_global_device_ids=true | all-gather | bytes 940032 | tf_op jit(solution)/shard_map/all_gather | solution.py:14
  295.1 12.4 all_gather.80
  309.7 11.2 all_gather.183
  321.0 10.0 multiply_convert_fusion.6
  344.7 13.4 all_gather.180
  370.1 14.3 all_gather.184
  393.0 21.4 %all-gather.3 = bf16[16,48,2]{1,2,0:T(2,128)(2,1)S(1)} all-gather(bf16[1,48,2]{1,2,0:T(2,128)(2,1)} %bitcast.978), channel_id=1, replica_groups=mesh['dp'=16,'mp'=2] {'dp'}, dimensions={0}, use_global_device_ids=true | all-gather | bytes 3264 | tf_op jit(solution)/shard_map/all_gather | solution.py:18
  415.0 17.6 %all-gather.2 = bf16[16,48,4]{1,2,0:T(4,128)(2,1)S(1)} all-gather(bf16[1,48,4]{1,2,0:T(4,128)(2,1)} %bitcast.976), channel_id=1, replica_groups=mesh['dp'=16,'mp'=2] {'dp'}, dimensions={0}, use_global_device_ids=true | all-gather | bytes 6528 | tf_op jit(solution)/shard_map/all_gather | solution.py:19
  440.0 12.0 all_gather.185
  452.1 8.1 all-gather.16.cloned.1.call-done
  460.2 6.5 multiply_convert_fusion.9
  466.7 33.1 %all-gather.18.cloned.1.call-done = bf16[768,768]{0,1:T(8,128)(2,1)} async-done(((bf16[768,48]{0,1:T(8,128)(2,1)}), bf16[768,768]{0,1:T(8,128)(2,1)}) %all-gather.18.cloned.1.call-update) | async-done | bytes 1179664 | tf_op jit(solution)/shard_map/all_gather | solution.py:17
  503.1 17.6 %all_gather.181 = bf16[1,512,768]{2,1,0:T(8,128)(2,1)S(1)} all-gather(bf16[1,256,768]{2,1,0:T(8,128)(2,1)S(1)} %copy-done.214), channel_id=1, replica_groups=mesh['dp'=16,'mp'=2] {'mp'}, dimensions={1}, use_global_device_ids=true | all-gather | bytes 1179648 | tf_op jit(solution)/shard_map/all_gather | solution.py:24
  520.7 6.8 multiply_convert_fusion.10
  530.2 18.5 %all_gather.85 = bf16[1,512,768]{2,1,0:T(8,128)(2,1)S(1)} all-gather(bf16[1,256,768]{2,1,0:T(8,128)(2,1)S(1)} %copy-done.213), channel_id=1, replica_groups=mesh['dp'=16,'mp'=2] {'mp'}, dimensions={1}, use_global_device_ids=true | all-gather | bytes 1179648 | tf_op jit(solution)/shard_map/all_gather | solution.py:24
  548.7 6.7 multiply_convert_fusion.11
  560.6 13.3 reduce-scatter.37.cloned.1.call-done
  582.1 11.5 all_gather.186
  603.1 19.1 %all_gather.194 = bf16[1,512,768]{2,1,0:T(8,128)(2,1)S(1)} all-gather(bf16[1,256,768]{2,1,0:T(8,128)(2,1)S(1)} %get-tuple-element.262), channel_id=1, replica_groups=mesh['dp'=16,'mp'=2] {'mp'}, dimensions={1}, use_global_device_ids=true | all-gather | bytes 1179648 | tf_op jit(solution)/shard_map/all_gather | solution.py:24
  631.4 17.7 %all_gather.190 = bf16[1,512,768]{2,1,0:T(8,128)(2,1)S(1)} all-gather(bf16[1,256,768]{2,1,0:T(8,128)(2,1)S(1)} %get-tuple-element.264), channel_id=1, replica_groups=mesh['dp'=16,'mp'=2] {'mp'}, dimensions={1}, use_global_device_ids=true | all-gather | bytes 1179648 | tf_op jit(solution)/shard_map/all_gather | solution.py:24
  659.5 17.1 %all_gather.187 = bf16[1,512,768]{2,1,0:T(8,128)(2,1)S(1)} all-gather(bf16[1,256,768]{2,1,0:T(8,128)(2,1)S(1)} %get-tuple-element.211), channel_id=1, replica_groups=mesh['dp'=16,'mp'=2] {'mp'}, dimensions={1}, use_global_device_ids=true | all-gather | bytes 1179648 | tf_op jit(solution)/shard_map/all_gather | solution.py:24
  698.4 9.2 all_gather.191
  717.0 16.8 %all_gather.195 = bf16[1,512,768]{2,1,0:T(8,128)(2,1)S(1)} all-gather(bf16[1,256,768]{2,1,0:T(8,128)(2,1)S(1)} %get-tuple-element.217), channel_id=1, replica_groups=mesh['dp'=16,'mp'=2] {'mp'}, dimensions={1}, use_global_device_ids=true | all-gather | bytes 1179648 | tf_op jit(solution)/shard_map/all_gather | solution.py:24
  759.6 14.8 reduce-scatter.73.cloned.1.call-done
  774.6 4.0 multiply_reduce_fusion.8
  778.8 4.0 fusion.392
  782.8 11.9 all_gather.188
  802.5 17.0 %all_gather.192 = bf16[1,512,768]{2,1,0:T(8,128)(2,1)S(1)} all-gather(bf16[1,256,768]{2,1,0:T(8,128)(2,1)} %get-tuple-element.304), channel_id=1, replica_groups=mesh['dp'=16,'mp'=2] {'mp'}, dimensions={1}, use_global_device_ids=true | all-gather | bytes 1179648 | tf_op jit(solution)/shard_map/all_gather | solution.py:24
  819.4 6.7 convert_reduce_fusion.1
  833.2 16.2 %all_gather.196 = bf16[1,512,768]{2,1,0:T(8,128)(2,1)S(1)} all-gather(bf16[1,256,768]{2,1,0:T(8,128)(2,1)S(1)} %get-tuple-element.214), channel_id=1, replica_groups=mesh['dp'=16,'mp'=2] {'mp'}, dimensions={1}, use_global_device_ids=true | all-gather | bytes 1179648 | tf_op jit(solution)/shard_map/all_gather | solution.py:24
  849.4 6.1 convert_reduce_fusion
  862.1 4.2 multiply_reduce_fusion.15
  869.8 9.9 all_gather.193
  889.2 4.4 multiply_reduce_fusion.11
  895.0 11.3 all_gather.197
  913.6 8.6 all_gather.189
  926.2 4.1 fusion.94
  930.6 8.2 multiply_convert_fusion
  955.8 7.0 multiply_reduce_fusion.2
  962.9 6.4 multiply_convert_fusion.2
  996.2 6.3 copy.201
  1055.5 58.6 %all-reduce.2 = (f32[2,384]{1,0:T(2,128)}, f32[1536]{0:T(1024)}, f32[2,192]{1,0:T(2,128)}, f32[768]{0:T(1024)}) all-reduce(f32[2,384]{1,0:T(2,128)S(1)} %fusion.356, f32[1536]{0:T(1024)S(1)} %add_add_fusion.5, f32[2,192]{1,0:T(2,128)S(1)} %fusion.357, f32[768]{0:T(1024)S(1)} %add_add_fusion.6), channel_id=1, replica_groups=mesh['dp'=16,'mp'=2] {'dp'}, use_global_device_ids=true, to_apply=%region_99.100 | all-reduce | flops 3456 | bytes 27648 | tf_op jit(solution)/shard_map/psum | solution.py:277
  1114.1 38.3 %psum.37 = f32[12,768]{1,0:T(8,128)S(1)} all-reduce(f32[12,768]{1,0:T(8,128)S(1)} %add_add_fusion.4), channel_id=1, replica_groups=mesh['dp'=16,'mp'=2] {'dp','mp'}, use_global_device_ids=true, to_apply=%region_149.150 | all-reduce | flops 9216 | bytes 73728 | tf_op jit(solution)/shard_map/psum | solution.py:278
  1158.6 8.7 all-reduce.6.cloned.1.call-done
  1170.6 57.8 %reduce-scatter.85.cloned.1.call-done = f32[192,48]{0,1:T(8,128)} async-done(((f32[192,768]{0,1:T(8,128)}), f32[192,48]{0,1:T(8,128)}) %reduce-scatter.85.cloned.1.call-update) | async-done | bytes 36880 | tf_op jit(solution)/shard_map/reduce_scatter | solution.py:51
  1228.4 66.3 %reduce-scatter.89.cloned.1.call-done = f32[768,48]{0,1:T(8,128)} async-done(((f32[768,768]{0,1:T(8,128)}), f32[768,48]{0,1:T(8,128)}) %reduce-scatter.89.cloned.1.call-update) | async-done | bytes 147472 | tf_op jit(solution)/shard_map/reduce_scatter | solution.py:53
  1294.7 66.8 %reduce-scatter.87.cloned.1.call-done = f32[48,768]{1,0:T(8,128)} async-done(((f32[768,768]{1,0:T(8,128)}), f32[48,768]{1,0:T(8,128)}) %reduce-scatter.87.cloned.1.call-update) | async-done | bytes 147472 | tf_op jit(solution)/shard_map/reduce_scatter | solution.py:52
  1361.5 61.5 %reduce-scatter.79.cloned.1.call-done = f32[384,48]{0,1:T(8,128)} async-done(((f32[384,768]{0,1:T(8,128)}), f32[384,48]{0,1:T(8,128)}) %reduce-scatter.79.cloned.1.call-update) | async-done | bytes 73744 | tf_op jit(solution)/shard_map/reduce_scatter | solution.py:51
  1422.9 79.0 %reduce-scatter.81.cloned.1.call-done = f32[48,1536]{1,0:T(8,128)} async-done(((f32[768,1536]{1,0:T(8,128)}), f32[48,1536]{1,0:T(8,128)}) %reduce-scatter.81.cloned.1.call-update) | async-done | bytes 294928 | tf_op jit(solution)/shard_map/reduce_scatter | solution.py:52
  1502.0 79.4 %reduce-scatter.83.cloned.1.call-done = f32[1536,48]{0,1:T(8,128)} async-done(((f32[1536,768]{0,1:T(8,128)}), f32[1536,48]{0,1:T(8,128)}) %reduce-scatter.83.cloned.1.call-update) | async-done | bytes 294928 | tf_op jit(solution)/shard_map/reduce_scatter | solution.py:53
  (1409 shorter events, 353.9 us)
Async XLA Ops:
  7.2 61.2 %all-gather.10.cloned.1.call-start = ((), (), s32[]{:S(2)}) async-start(), calls=%async_computation.30 | async-start | bytes 1880064 | tf_op jit(solution)/shard_map/all_gather | solution.py:14
  7.9 133.0 %reduce-scatter.31.cloned.1.call-start = ((), (), s32[]{:S(2)}) async-start(), calls=%async_computation.31 | async-start | bytes 1179648 | tf_op jit(solution)/shard_map/reduce_scatter | solution.py:29
  8.8 88.1 %copy-start.303 = (f32[6,64]{1,0:T(8,128)}, f32[6,64]{1,0:T(8,128)S(1)}, u32[]{:S(2)}) copy-start(f32[6,64]{1,0:T(8,128)S(1)} %add.1129) | copy-start | bytes 4612
  8.8 85.8 %copy-start.277 = (f32[6,64]{1,0:T(8,128)}, f32[6,64]{1,0:T(8,128)S(1)}, u32[]{:S(2)}) copy-start(f32[6,64]{1,0:T(8,128)S(1)} %add.1132) | copy-start | bytes 4612
  10.2 34.1 %copy-start.451 = (s32[3,512]{1,0:T(4,128)S(1)}, s32[3,512]{1,0:T(4,128)}, u32[]{:S(2)}) copy-start(s32[3,512]{1,0:T(4,128)} %param.20) | copy-start | bytes 18436
  10.2 35.5 %copy-start.350 = (bf16[384,48]{0,1:T(8,128)(2,1)S(1)}, bf16[384,48]{0,1:T(8,128)(2,1)}, u32[]{:S(2)}) copy-start(bf16[384,48]{0,1:T(8,128)(2,1)} %param.24) | copy-start | bytes 110596
  34.0 37.3 %copy-start.111 = (bf16[1,512,768]{2,1,0:T(8,128)(2,1)}, bf16[1,512,768]{2,1,0:T(8,128)(2,1)S(1)}, u32[]{:S(2)}) copy-start(bf16[1,512,768]{2,1,0:T(8,128)(2,1)S(1)} %all_gather.182) | copy-start | bytes 2359300
  44.5 38.0 %copy-start.153 = (pred[512,512]{0,1:T(8,128)(4,1)}, pred[512,512]{0,1:T(8,128)(4,1)S(1)}, u32[]{:S(2)}) copy-start(pred[512,512]{0,1:T(8,128)(4,1)S(1)} %broadcast_compare_fusion) | copy-start | bytes 786436
  45.6 49.0 %copy-start.155 = (pred[512,512]{0,1:T(8,128)(4,1)}, pred[512,512]{0,1:T(8,128)(4,1)S(1)}, u32[]{:S(2)}) copy-start(pred[512,512]{0,1:T(8,128)(4,1)S(1)} %broadcast_compare_fusion.1) | copy-start | bytes 786436
  68.4 31.5 %copy-start.49 = (bf16[384,768]{0,1:T(8,128)(2,1)}, bf16[384,768]{0,1:T(8,128)(2,1)S(1)}, u32[]{:S(2)}) copy-start(bf16[384,768]{0,1:T(8,128)(2,1)S(1)} %all_gather.74) | copy-start | bytes 1769476
  82.3 60.0 %reduce-scatter.47.cloned.1.call-start = ((), (), s32[]{:S(2)}) async-start(), calls=%async_computation.43 | async-start | bytes 1179648 | tf_op jit(solution)/shard_map/reduce_scatter | solution.py:29
  94.5 47.7 %reduce-scatter.39.cloned.1.call-start = ((), (), s32[]{:S(2)}) async-start(), calls=%async_computation.39 | async-start | bytes 1179648 | tf_op jit(solution)/shard_map/reduce_scatter | solution.py:29
  99.9 41.0 %copy-start.3 = (bf16[3,256,768]{2,1,0:T(8,128)(2,1)S(1)}, bf16[3,256,768]{2,1,0:T(8,128)(2,1)}, u32[]{:S(2)}) copy-start(bf16[3,256,768]{2,1,0:T(8,128)(2,1)} %param.19) | copy-start | bytes 3538948
  102.1 79.8 %all-gather.12.cloned.1.call-start = ((), (), s32[]{:S(2)}) async-start(), calls=%async_computation.32 | async-start | bytes 2506752 | tf_op jit(solution)/shard_map/all_gather | solution.py:16
  102.7 122.6 %all-gather.14.cloned.1.call-start = ((), (), s32[]{:S(2)}) async-start(), calls=%async_computation.33 | async-start | bytes 2506752 | tf_op jit(solution)/shard_map/all_gather | solution.py:17
  103.3 186.2 %reduce-scatter.41.cloned.1.call-start = ((), (), s32[]{:S(2)}) async-start(), calls=%async_computation.40 | async-start | bytes 1179648 | tf_op jit(solution)/shard_map/reduce_scatter | solution.py:29
  140.8 227.8 %copy-start.248 = (f32[768]{0:T(1024)}, f32[768]{0:T(1024)S(1)}, u32[]{:S(2)}) copy-start(f32[768]{0:T(1024)S(1)} %get-tuple-element.175) | copy-start | bytes 9220
  157.8 72.2 %copy-start.117 = (bf16[1,512,768]{2,1,0:T(8,128)(2,1)}, bf16[1,512,768]{2,1,0:T(8,128)(2,1)S(1)}, u32[]{:S(2)}) copy-start(bf16[1,512,768]{2,1,0:T(8,128)(2,1)S(1)} %all_gather.77) | copy-start | bytes 2359300
  229.9 59.6 %reduce-scatter.33.cloned.1.call-start = ((), (), s32[]{:S(2)}) async-start(), calls=%async_computation.34 | async-start | bytes 1179648 | tf_op jit(solution)/shard_map/reduce_scatter | solution.py:29
  242.1 24.0 %copy-start.302 = (bf16[3,48,192]{2,1,0:T(8,128)(2,1)S(1)}, bf16[3,48,192]{2,1,0:T(8,128)(2,1)}, u32[]{:S(2)}) copy-start(bf16[3,48,192]{2,1,0:T(8,128)(2,1)} %param.30) | copy-start | bytes 165892
  244.4 44.5 %copy-start.452 = (f32[256]{0:T(256)S(1)}, f32[256]{0:T(256)}, u32[]{:S(2)}) copy-start(f32[256]{0:T(256)} %get-tuple-element.143) | copy-start | bytes 3076
  244.4 121.5 %reduce-scatter.49.cloned.1.call-start = ((), (), s32[]{:S(2)}) async-start(), calls=%async_computation.44 | async-start | bytes 1179648 | tf_op jit(solution)/shard_map/reduce_scatter | solution.py:29
  266.1 122.9 %copy-start.37 = (bf16[192,768]{0,1:T(8,128)(2,1)}, bf16[192,768]{0,1:T(8,128)(2,1)S(1)}, u32[]{:S(2)}) copy-start(bf16[192,768]{0,1:T(8,128)(2,1)S(1)} %all_gather.82) | copy-start | bytes 884740
  309.7 24.8 %copy-start.87 = (f32[1,512,192]{1,2,0:T(8,128)}, f32[1,512,192]{1,2,0:T(8,128)S(1)}, u32[]{:S(2)}) copy-start(f32[1,512,192]{1,2,0:T(8,128)S(1)} %get-tuple-element.276) | copy-start | bytes 1179652
  334.4 98.9 %reduce-scatter.35.cloned.1.call-start = ((), (), s32[]{:S(2)}) async-start(), calls=%async_computation.35 | async-start | bytes 1179648 | tf_op jit(solution)/shard_map/reduce_scatter | solution.py:29
  358.1 75.2 %reduce-scatter.43.cloned.1.call-start = ((), (), s32[]{:S(2)}) async-start(), calls=%async_computation.41 | async-start | bytes 1179648 | tf_op jit(solution)/shard_map/reduce_scatter | solution.py:29
  365.9 67.5 %reduce-scatter.51.cloned.1.call-start = ((), (), s32[]{:S(2)}) async-start(), calls=%async_computation.45 | async-start | bytes 1179648 | tf_op jit(solution)/shard_map/reduce_scatter | solution.py:29
  389.0 44.4 %copy-start.20 = (f32[256,768]{1,0:T(8,128)S(1)}, f32[256,768]{1,0:T(8,128)}, u32[]{:S(2)}) copy-start(f32[256,768]{1,0:T(8,128)} %get-tuple-element.269) | copy-start | bytes 2359300
  391.0 69.2 %all-gather.16.cloned.1.call-start = ((), (), s32[]{:S(2)}) async-start(), calls=%async_computation.36 | async-start | bytes 1253376 | tf_op jit(solution)/shard_map/all_gather | solution.py:16
  391.7 108.1 %all-gather.18.cloned.1.call-start = ((), (), s32[]{:S(2)}) async-start(), calls=%async_computation.37 | async-start | bytes 1253376 | tf_op jit(solution)/shard_map/all_gather | solution.py:17
  392.3 168.3 %reduce-scatter.53.cloned.1.call-start = ((), (), s32[]{:S(2)}) async-start(), calls=%async_computation.46 | async-start | bytes 1179648 | tf_op jit(solution)/shard_map/reduce_scatter | solution.py:29
  466.7 36.4 %copy-start.214 = (bf16[1,256,768]{2,1,0:T(8,128)(2,1)S(1)}, bf16[1,256,768]{2,1,0:T(8,128)(2,1)}, u32[]{:S(2)}) copy-start(bf16[1,256,768]{2,1,0:T(8,128)(2,1)} %get-tuple-element.289) | copy-start | bytes 1179652
  503.0 57.6 %reduce-scatter.45.cloned.1.call-start = ((), (), s32[]{:S(2)}) async-start(), calls=%async_computation.42 | async-start | bytes 1179648 | tf_op jit(solution)/shard_map/reduce_scatter | solution.py:29
  530.1 43.8 %reduce-scatter.37.cloned.1.call-start = ((), (), s32[]{:S(2)}) async-start(), calls=%async_computation.38 | async-start | bytes 1179648 | tf_op jit(solution)/shard_map/reduce_scatter | solution.py:29
  558.1 95.6 %reduce-scatter.55.cloned.1.call-start = ((), (), s32[]{:S(2)}) async-start(), calls=%async_computation.47 | async-start | bytes 1179648 | tf_op jit(solution)/shard_map/reduce_scatter | solution.py:39
  598.1 83.1 %reduce-scatter.71.cloned.1.call-start = ((), (), s32[]{:S(2)}) async-start(), calls=%async_computation.55 | async-start | bytes 1179648 | tf_op jit(solution)/shard_map/reduce_scatter | solution.py:39
  598.2 24.0 %copy-start.478 = (bf16[768,768]{0,1:T(8,128)(2,1)S(1)}, bf16[768,768]{0,1:T(8,128)(2,1)}, u32[]{:S(2)}) copy-start(bf16[768,768]{0,1:T(8,128)(2,1)} %all-gather.18.cloned.1.call-done) | copy-start | bytes 3538948
  598.2 24.0 %copy-start.483 = (f32[512,768]{1,0:T(8,128)S(1)}, f32[512,768]{1,0:T(8,128)}, u32[]{:S(2)}) copy-start(f32[512,768]{1,0:T(8,128)} %get-tuple-element.247) | copy-start | bytes 4718596
  598.2 24.0 %copy-start.484 = (f32[512,768]{1,0:T(8,128)S(1)}, f32[512,768]{1,0:T(8,128)}, u32[]{:S(2)}) copy-start(f32[512,768]{1,0:T(8,128)} %get-tuple-element.323) | copy-start | bytes 4718596
  599.0 23.1 %copy-start.416 = (f32[256]{0:T(256)}, f32[256]{0:T(256)S(1)}, u32[]{:S(2)}) copy-start(f32[256]{0:T(256)S(1)} %broadcast_multiply_fusion.6) | copy-start | bytes 3076
  626.5 66.1 %reduce-scatter.63.cloned.1.call-start = ((), (), s32[]{:S(2)}) async-start(), calls=%async_computation.51 | async-start | bytes 1179648 | tf_op jit(solution)/shard_map/reduce_scatter | solution.py:39
  626.6 22.6 %copy-start.479 = (bf16[768,768]{0,1:T(8,128)(2,1)S(1)}, bf16[768,768]{0,1:T(8,128)(2,1)}, u32[]{:S(2)}) copy-start(bf16[768,768]{0,1:T(8,128)(2,1)} %all-gather.18.cloned.1.call-done) | copy-start | bytes 3538948
  626.6 22.6 %copy-start.481 = (f32[512,768]{1,0:T(8,128)S(1)}, f32[512,768]{1,0:T(8,128)}, u32[]{:S(2)}) copy-start(f32[512,768]{1,0:T(8,128)} %get-tuple-element.235) | copy-start | bytes 4718596
  653.6 94.6 %reduce-scatter.57.cloned.1.call-start = ((), (), s32[]{:S(2)}) async-start(), calls=%async_computation.48 | async-start | bytes 1179648 | tf_op jit(solution)/shard_map/reduce_scatter | solution.py:39
  710.5 44.2 %reduce-scatter.65.cloned.1.call-start = ((), (), s32[]{:S(2)}) async-start(), calls=%async_computation.52 | async-start | bytes 1179648 | tf_op jit(solution)/shard_map/reduce_scatter | solution.py:39
  739.2 35.3 %reduce-scatter.73.cloned.1.call-start = ((), (), s32[]{:S(2)}) async-start(), calls=%async_computation.56 | async-start | bytes 1179648 | tf_op jit(solution)/shard_map/reduce_scatter | solution.py:39
  746.8 112.3 %reduce-scatter.59.cloned.1.call-start = ((), (), s32[]{:S(2)}) async-start(), calls=%async_computation.49 | async-start | bytes 1179648 | tf_op jit(solution)/shard_map/reduce_scatter | solution.py:39
  751.9 22.7 %copy-start.92 = (bf16[1,256,768]{2,1,0:T(8,128)(2,1)S(1)}, bf16[1,256,768]{2,1,0:T(8,128)(2,1)}, u32[]{:S(2)}) copy-start(bf16[1,256,768]{2,1,0:T(8,128)(2,1)} %reduce-scatter.71.cloned.1.call-done) | copy-start | bytes 1179652
  801.1 61.0 %reduce-scatter.67.cloned.1.call-start = ((), (), s32[]{:S(2)}) async-start(), calls=%async_computation.53 | async-start | bytes 1179648 | tf_op jit(solution)/shard_map/reduce_scatter | solution.py:39
  829.8 59.4 %reduce-scatter.75.cloned.1.call-start = ((), (), s32[]{:S(2)}) async-start(), calls=%async_computation.57 | async-start | bytes 1179648 | tf_op jit(solution)/shard_map/reduce_scatter | solution.py:39
  859.0 294.7 %reduce-scatter.69.cloned.1.call-start = ((), (), s32[]{:S(2)}) async-start(), calls=%async_computation.54 | async-start | bytes 1179648 | tf_op jit(solution)/shard_map/reduce_scatter | solution.py:39
  930.4 224.4 %reduce-scatter.77.cloned.1.call-start = ((), (), s32[]{:S(2)}) async-start(), calls=%async_computation.58 | async-start | bytes 1179648 | tf_op jit(solution)/shard_map/reduce_scatter | solution.py:39
  943.8 49.0 %copy-start.103 = (bf16[1,512,384]{2,1,0:T(8,128)(2,1)}, bf16[1,512,384]{2,1,0:T(8,128)(2,1)S(1)}, u32[]{:S(2)}) copy-start(bf16[1,512,384]{2,1,0:T(8,128)(2,1)S(1)} %copy.197) | copy-start | bytes 1179652
  962.8 193.1 %reduce-scatter.61.cloned.1.call-start = ((), (), s32[]{:S(2)}) async-start(), calls=%async_computation.50 | async-start | bytes 1179648 | tf_op jit(solution)/shard_map/reduce_scatter | solution.py:39
  981.9 185.4 %all-reduce.6.cloned.1.call-start = ((), (), s32[]{:S(2)}) async-start(), calls=%async_computation.65 | async-start | bytes 15728640
  1002.5 225.9 %reduce-scatter.85.cloned.1.call-start = ((), (), s32[]{:S(2)}) async-start(), calls=%async_computation.62 | async-start | bytes 835584 | tf_op jit(solution)/shard_map/reduce_scatter | solution.py:51
  1007.9 286.8 %reduce-scatter.89.cloned.1.call-start = ((), (), s32[]{:S(2)}) async-start(), calls=%async_computation.64 | async-start | bytes 2506752 | tf_op jit(solution)/shard_map/reduce_scatter | solution.py:53
  1014.0 347.5 %reduce-scatter.87.cloned.1.call-start = ((), (), s32[]{:S(2)}) async-start(), calls=%async_computation.63 | async-start | bytes 2506752 | tf_op jit(solution)/shard_map/reduce_scatter | solution.py:52
  1020.3 402.6 %reduce-scatter.79.cloned.1.call-start = ((), (), s32[]{:S(2)}) async-start(), calls=%async_computation.59 | async-start | bytes 1253376 | tf_op jit(solution)/shard_map/reduce_scatter | solution.py:51
  1025.1 476.9 %reduce-scatter.81.cloned.1.call-start = ((), (), s32[]{:S(2)}) async-start(), calls=%async_computation.60 | async-start | bytes 5013504 | tf_op jit(solution)/shard_map/reduce_scatter | solution.py:52
  1033.5 547.8 %reduce-scatter.83.cloned.1.call-start = ((), (), s32[]{:S(2)}) async-start(), calls=%async_computation.61 | async-start | bytes 5013504 | tf_op jit(solution)/shard_map/reduce_scatter | solution.py:53
  1054.9 98.8 %copy-start.136 = (f32[1,256,768]{2,1,0:T(8,128)S(1)}, f32[1,256,768]{2,1,0:T(8,128)}, u32[]{:S(2)}) copy-start(f32[1,256,768]{2,1,0:T(8,128)} %get-tuple-element.274) | copy-start | bytes 2359300
  1055.1 99.7 %copy-start.141 = (f32[1,256,768]{2,1,0:T(8,128)S(1)}, f32[1,256,768]{2,1,0:T(8,128)}, u32[]{:S(2)}) copy-start(f32[1,256,768]{2,1,0:T(8,128)} %get-tuple-element.198) | copy-start | bytes 2359300
  1055.2 100.7 %copy-start.135 = (f32[1,256,768]{2,1,0:T(8,128)S(1)}, f32[1,256,768]{2,1,0:T(8,128)}, u32[]{:S(2)}) copy-start(f32[1,256,768]{2,1,0:T(8,128)} %get-tuple-element.194) | copy-start | bytes 2359300
  (467 other events, 2158.3 us)
Sparse Core Ops, SparseCore 0:
  10.3 43.2 all-gather.9
  82.4 14.7 reduce-scatter.30
  99.5 17.4 reduce-scatter.46
  119.7 17.4 reduce-scatter.38
  139.5 42.2 all-gather.11
  184.3 40.9 all-gather.13
  230.0 16.2 reduce-scatter.40
  249.1 17.3 reduce-scatter.32
  334.6 18.4 reduce-scatter.48
  358.2 21.5 reduce-scatter.34
  382.2 17.4 reduce-scatter.42
  401.7 17.4 reduce-scatter.50
  421.7 38.3 all-gather.15
  462.6 37.1 all-gather.17
  503.2 21.3 reduce-scatter.52
  530.3 20.2 reduce-scatter.44
  558.2 15.6 reduce-scatter.36
  598.2 24.6 reduce-scatter.54
  626.6 23.2 reduce-scatter.70
  653.7 23.2 reduce-scatter.62
  710.6 23.5 reduce-scatter.56
  739.3 15.3 reduce-scatter.64
  757.0 17.4 reduce-scatter.72
  801.2 21.5 reduce-scatter.58
  829.9 21.2 reduce-scatter.66
  859.1 17.9 reduce-scatter.74
  930.5 17.3 reduce-scatter.68
  963.0 17.3 reduce-scatter.76
  982.7 17.4 reduce-scatter.60
  1003.7 163.4 all-reduce.5
  1171.8 56.5 reduce-scatter.84
  1232.7 61.9 reduce-scatter.88
  1299.4 62.0 reduce-scatter.86
  1365.7 57.2 reduce-scatter.78
  1427.4 74.5 reduce-scatter.80
  1506.7 74.5 reduce-scatter.82
where the time goes:
time: 1600 us; the launch traced here: 1590 us
  blocking collectives  561 us (35%)
  waiting for transfers between devices  539 us (34%)
  matrix products  248 us (16%)
  other arithmetic  134 us (8%)
  local copies, waits for them, and re-layouts  81.9 us (5%)
  between operations  21.4 us (1%)
    all_gather x24, blocking collectives, gather_rows(): lax.all_gather(share_low.reshape(rows, -1, D), 'mp', axis=1, tiled=True)  323 us
    reduce_scatter x2, waiting for transfers between devices, shard_grads(): lax.psum_scatter(grads[2], 'dp', scatter_dimension=0, tiled=True)  146 us
    reduce_scatter x2, waiting for transfers between devices, shard_grads(): lax.psum_scatter(grads[3], 'dp', scatter_dimension=1, tiled=True)  146 us
    reduce_scatter x2, waiting for transfers between devices, shard_grads(): lax.psum_scatter(grads[1], 'dp', scatter_dimension=1, tiled=True)  119 us
    all_gather x2, waiting for transfers between devices, fetch_layer(): lax.all_gather(shards[3], 'dp', axis=1, tiled=True)  65.3 us
    psum x1, blocking collectives, on_device(): lax.psum((bias_acc[0], bias_acc[1], bias_acc[2], bias_acc[3]), 'dp')  58.6 us
    unnamed x995, local copies, waits for them, and re-layouts  52.2 us
    dot_general x6, matrix products, forward_layer(): jnp.dot(hidden_low, up_w, preferred_element_type=jnp.float32)  52.1 us
  transfers between devices with their start and end apart: 36, of which 14 were waited for; matrix products, arithmetic and copies ran while one was open for 21% of the time, Pallas kernels for 0%

commit v1 on v0

v1 whole, which is shorter than its diff:
```python
import math

import jax
import jax.numpy as jnp
from jax import lax
from jax.sharding import PartitionSpec as P

HEAD_DIM = 64
LOW = jnp.bfloat16
F32 = jnp.float32


def ring_of(count):
    return list(range(0, count, 2)) + list(range(1, count, 2))[::-1]


def swap_y(value):
    return lax.ppermute(value, "mp", [(0, 1), (1, 0)])


def swap_x(value):
    n = lax.axis_size("dp")
    return lax.ppermute(value, "dp", [(i, i ^ 2) for i in range(n)])


def swap_core(value):
    n = lax.axis_size("dp")
    return lax.ppermute(value, "dp", [(i, i ^ 1) for i in range(n)])


def ring_shift(value, step):
    count = lax.axis_size("dp") // 4
    ring = ring_of(count)
    pairs = []
    for place in range(count):
        for low in range(4):
            pairs.append((ring[place] * 4 + low, ring[(place + step) % count] * 4 + low))
    return lax.ppermute(value, "dp", pairs)


def feature_order(width):
    n = lax.axis_size("dp")
    count, rows = n // 4, width // n
    me = lax.axis_index("dp")
    z, x, core = me // 4, (me // 2) % 2, me % 2
    place = jnp.where(z % 2 == 0, z // 2, count - 1 - z // 2)
    at = lax.iota(jnp.int32, width)
    row = at % rows
    back = (at // rows) % count
    x_rel = (at // (rows * count)) % 2
    core_rel = at // (rows * count * 2)
    from_place = (place - back + count) % count
    half = (count + 1) // 2
    z_abs = jnp.where(from_place < half, 2 * from_place, 2 * (count - 1 - from_place) + 1)
    block = z_abs * 4 + (x ^ x_rel) * 2 + (core ^ core_rel)
    return block * rows + row


def gather_pair(parts_a, parts_b):
    count = lax.axis_size("dp") // 4
    a = jnp.concatenate(list(parts_a.values()), axis=1)
    b = jnp.concatenate(list(parts_b.values()), axis=1)
    cut = a.shape[1]
    pieces = [jnp.concatenate([a, b], axis=1)]
    for _ in range(count - 1):
        pieces.append(ring_shift(pieces[-1], 1))
    a = jnp.stack([piece[:, :cut] for piece in pieces])
    b = jnp.stack([piece[:, cut:] for piece in pieces])
    a = jnp.stack([a, swap_x(a)])
    b = jnp.stack([b, swap_y(b)])
    a = jnp.stack([a, swap_y(a)])
    b = jnp.stack([b, swap_x(b)], axis=1)
    a = jnp.stack([a, swap_core(a)], axis=1)
    b = jnp.stack([b, swap_core(b)], axis=1)
    out = {}
    for whole, parts in ((a, parts_a), (b, parts_b)):
        whole = whole.reshape(2, -1, whole.shape[-1])
        start = 0
        for name, part in parts.items():
            out[name] = whole[:, :, start : start + part.shape[1]]
            start += part.shape[1]
    return out


def reduce_pair(parts_a, parts_b):
    count = lax.axis_size("dp") // 4

    def start_of(parts):
        sends = jnp.concatenate([part[0] for part in parts.values()], axis=2)
        keeps = jnp.concatenate([part[1] for part in parts.values()], axis=2)
        return keeps + swap_core(sends).astype(F32)

    def fold_y(value):
        return value[0] + swap_y(value[1].astype(LOW)).astype(F32)

    def fold_x(value):
        half = value.shape[-2] // 2
        return value[..., :half, :] + swap_x(value[..., half:, :].astype(LOW)).astype(F32)

    a = fold_x(fold_y(start_of(parts_a)))
    b = fold_y(fold_x(start_of(parts_b)))
    both = jnp.concatenate([a, b], axis=1)
    both = both.reshape(count, -1, both.shape[1])
    total = both[count - 1]
    for back in range(count - 2, -1, -1):
        total = both[back] + ring_shift(total.astype(LOW), -1).astype(F32)
    out = {}
    start = 0
    for name, part in list(parts_a.items()) + list(parts_b.items()):
        out[name] = total[:, start : start + part[0].shape[2]]
        start += part[0].shape[2]
    return out


def weight_grad(left, right):
    half = left.shape[1] // 2
    send = jnp.einsum("nd,ync->ydc", left[:, half:], right, preferred_element_type=F32).astype(LOW)
    keep = jnp.einsum("nd,ync->ydc", left[:, :half], right, preferred_element_type=F32)
    return (send, keep)


def norm_layer(value, gain, shift):
    center = value - jnp.mean(value, axis=-1, keepdims=True)
    spread = jnp.mean(center * center, axis=-1, keepdims=True)
    recip = lax.rsqrt(spread + 1e-06)
    normed = center * recip
    return (normed * gain + shift, (normed, recip))


def norm_back(grad, kept, gain):
    normed, recip = kept
    scaled = grad * gain
    d_gain = jnp.sum(grad * normed, axis=0)
    d_shift = jnp.sum(grad, axis=0)
    mean_one = jnp.mean(scaled, axis=-1, keepdims=True)
    mean_two = jnp.mean(scaled * normed, axis=-1, keepdims=True)
    return (recip * (scaled - mean_one - normed * mean_two), d_gain, d_shift)


def heads_of(value):
    return value.reshape(value.shape[0], value.shape[1], -1, HEAD_DIM)


def scores_of(query, keys, same):
    scores = jnp.einsum("yqhe,ykhe->yhqk", query, keys, preferred_element_type=F32)
    return jnp.where(same, scores * HEAD_DIM ** (-0.5), -1000000000.0)


def attend(query, keys, values, same):
    query, keys, values = heads_of(query), heads_of(keys), heads_of(values)
    scores = scores_of(query, keys, same)
    top = jnp.max(scores, axis=-1, keepdims=True)
    expo = jnp.exp(scores - top)
    total = jnp.sum(expo, axis=-1, keepdims=True)
    probs = (expo / total).astype(LOW)
    context = jnp.einsum("yhqk,ykhe->yqhe", probs, values, preferred_element_type=F32)
    context = context.reshape(context.shape[0], context.shape[1], -1).astype(LOW)
    return context, top + jnp.log(total)


def attend_back(query, keys, values, same, logsum, d_context):
    flat = lambda value: value.reshape(value.shape[0], value.shape[1], -1).astype(LOW)
    scale = HEAD_DIM ** (-0.5)
    query, keys, values, d_context = (
        heads_of(query), heads_of(keys), heads_of(values), heads_of(d_context)
    )
    probs = jnp.exp(scores_of(query, keys, same) - logsum)
    d_values = jnp.einsum("yhqk,yqhe->ykhe", probs.astype(LOW), d_context, preferred_element_type=F32)
    d_probs = jnp.einsum("yqhe,ykhe->yhqk", d_context, values, preferred_element_type=F32)
    inner = jnp.sum(probs * d_probs, axis=-1, keepdims=True)
    d_scores = (probs * (d_probs - inner)).astype(LOW)
    d_query = jnp.einsum("yhqk,ykhe->yqhe", d_scores, keys, preferred_element_type=F32) * scale
    d_keys = jnp.einsum("yhqk,yqhe->ykhe", d_scores, query, preferred_element_type=F32) * scale
    return flat(d_query), flat(d_keys), flat(d_values)


def forward_layer(inputs, away, masks, full, biases, norms):
    same_own, same_shared = masks
    n = inputs.shape[0]
    own = n - away.shape[0]
    gains, shifts = norms
    inputs_low = jnp.concatenate([inputs.astype(LOW), away], axis=0)
    project = lambda name: jnp.einsum("nd,ydc->ync", inputs_low, full[name], preferred_element_type=F32)
    query = (project("q")[:, :n] + biases["q"][:, None]).astype(LOW)
    keys = project("k").astype(LOW)
    values = (project("v") + biases["v"][:, None]).astype(LOW)
    context_a, logsum_a = attend(query[:, :own], keys[:, :own], values[:, :own], same_own)
    context_b, logsum_b = attend(query[:, own:], keys[:, own:], values[:, own:], same_shared)
    context = jnp.concatenate([context_a, context_b], axis=1)
    attn = jnp.einsum("ynw,ydw->nd", context, full["out"], preferred_element_type=F32)
    hidden, first_norm = norm_layer(inputs + attn + shifts[0], gains[0], shifts[1])
    hidden_low = hidden.astype(LOW)
    pre = jnp.einsum("nd,ydf->ynf", hidden_low, full["up"], preferred_element_type=F32)
    pre = pre + biases["up"][:, None]
    bell = 0.5 * (1.0 + lax.erf(pre * math.sqrt(0.5)))
    act = (pre * bell).astype(LOW)
    slope = (bell + pre * (jnp.exp(-0.5 * pre * pre) * (1.0 / math.sqrt(2.0 * math.pi)))).astype(LOW)
    ffn = jnp.einsum("ynf,ydf->nd", act, full["down"], preferred_element_type=F32)
    output, second_norm = norm_layer(hidden + ffn + shifts[2], gains[1], shifts[3])
    saved = (
        inputs_low, query, keys, values, logsum_a, logsum_b, context, first_norm, hidden_low,
        act, slope, second_norm,
    )
    return output, saved


def backward_ffn(grad_out, full, norms, saved):
    gains, _ = norms
    (_, _, _, _, _, _, _, first_norm, hidden_low, act, slope, second_norm) = saved
    d_final, d_gain_two, d_shift_three = norm_back(grad_out, second_norm, gains[1])
    d_shift_two = jnp.sum(d_final, axis=0)
    d_final_low = d_final.astype(LOW)
    d_down = weight_grad(d_final_low, act)
    d_act = jnp.einsum("nd,ydf->ynf", d_final_low, full["down"], preferred_element_type=F32)
    d_pre = (d_act * slope.astype(F32)).astype(LOW)
    d_up_bias = jnp.sum(d_pre.astype(F32), axis=1)
    d_up = weight_grad(hidden_low, d_pre)
    d_hidden = d_final + jnp.einsum("ynf,ydf->nd", d_pre, full["up"], preferred_element_type=F32)
    d_mid, d_gain_one, d_shift_one = norm_back(d_hidden, first_norm, gains[0])
    d_shift_zero = jnp.sum(d_mid, axis=0)
    norm_grads = [d_gain_one, d_gain_two, d_shift_zero, d_shift_one, d_shift_two, d_shift_three]
    return d_mid, d_up, d_down, d_up_bias, norm_grads


def backward_attn(d_mid, masks, full, saved):
    same_own, same_shared = masks
    (inputs_low, query, keys, values, logsum_a, logsum_b, context, _, _, _, _, _) = saved
    n = d_mid.shape[0]
    own = n - (inputs_low.shape[0] - n)
    d_mid_low = d_mid.astype(LOW)
    d_out = weight_grad(d_mid_low, context)
    d_context = jnp.einsum("nd,ydw->ynw", d_mid_low, full["out"], preferred_element_type=F32).astype(LOW)
    dq_b, dk_b, dv_b = attend_back(
        query[:, own:], keys[:, own:], values[:, own:], same_shared, logsum_b, d_context[:, own:]
    )
    half = n - own
    back = lambda one, name: jnp.einsum("ync,ydc->nd", one, full[name], preferred_element_type=F32)
    away = back(dk_b[:, half:], "k") + back(dv_b[:, half:], "v")
    from_away = swap_y(away.astype(LOW))
    dq_a, dk_a, dv_a = attend_back(
        query[:, :own], keys[:, :own], values[:, :own], same_own, logsum_a, d_context[:, :own]
    )
    d_query = jnp.concatenate([dq_a, dq_b], axis=1)
    d_keys = jnp.concatenate([dk_a, dk_b], axis=1)
    d_values = jnp.concatenate([dv_a, dv_b], axis=1)
    d_qv_bias = (jnp.sum(d_query.astype(F32), axis=1), jnp.sum(d_values.astype(F32), axis=1))
    grads = {
        "q": weight_grad(inputs_low[:n], d_query),
        "k": weight_grad(inputs_low, d_keys),
        "v": weight_grad(inputs_low, d_values),
        "out": d_out,
    }
    d_inputs = d_mid + back(d_query, "q") + back(d_keys[:, :n], "k") + back(d_values[:, :n], "v")
    d_inputs = jnp.concatenate([d_inputs[:own], d_inputs[own:] + from_away.astype(F32)], axis=0)
    return d_inputs, grads, d_qv_bias


def on_device(
    tokens, segment_ids, out_grad,
    t_qkv, t_qv_bias, t_out, t_up, t_up_bias, t_down, t_gains, t_shifts,
    s_qkv, s_qv_bias, s_out, s_up, s_up_bias, s_down, s_gains, s_shifts,
):
    rows, half, width = tokens.shape
    first = lax.axis_index("mp") == 0

    norm_rows = jnp.concatenate([t_gains, t_shifts, s_gains, s_shifts], axis=0).T
    norm_rows = jnp.pad(norm_rows, ((0, 0), (0, 128 - norm_rows.shape[1])))
    t_full = gather_pair(
        {"q": t_qkv[0], "k": t_qkv[1]}, {"v": t_qkv[2], "out": t_out.T, "norm": norm_rows}
    )
    t_full.update(gather_pair({"up": t_up}, {"down": t_down.T}))
    s_full = gather_pair(
        {"up": s_up, "q": s_qkv[0], "out": s_out.T}, {"down": s_down.T, "k": s_qkv[1], "v": s_qkv[2]}
    )
    norm_all = t_full["norm"][0, :, :12].T.astype(F32)
    t_norms = (norm_all[0:2], norm_all[2:6])
    s_norms = (norm_all[6:8], norm_all[8:12])
    bias_parts = [t_qv_bias[0], t_qv_bias[1], t_up_bias, s_qv_bias[0], s_qv_bias[1], s_up_bias]
    bias_own = jnp.concatenate(bias_parts)
    bias_all = jnp.stack([bias_own, swap_y(bias_own)]).astype(F32)
    cuts = [0]
    for part in bias_parts:
        cuts.append(cuts[-1] + part.shape[0])
    pick = [bias_all[:, cuts[i] : cuts[i + 1]] for i in range(6)]
    t_bias = {"q": pick[0], "v": pick[1], "up": pick[2]}
    s_bias = {"q": pick[3], "v": pick[4], "up": pick[5]}

    to_own = feature_order(width)
    into = (lax.iota(jnp.int32, width)[:, None] == to_own[None, :]).astype(LOW)
    own_row = lambda value: jnp.where(first, value[0], value[2])
    far_row = lambda value: jnp.where(first, value[2], value[0])
    got = swap_y(jnp.stack([far_row(tokens), tokens[1]]))
    local = jnp.concatenate([own_row(tokens), got[0], tokens[1], got[1]], axis=0)
    local = jnp.dot(local, into, preferred_element_type=F32).astype(LOW)
    inputs, away = local[: rows * half].astype(F32), local[rows * half :]
    grad_in = jnp.concatenate([own_row(out_grad), swap_y(far_row(out_grad)), out_grad[1]], axis=0)
    grad_in = jnp.dot(grad_in, into, preferred_element_type=F32)
    spin = lambda segs: jnp.where(first, segs, jnp.roll(segs, half))
    seg_own = spin(own_row(segment_ids))
    seg_shared = spin(segment_ids[1])
    same_own = (seg_own[:, None] == seg_own[None, :])[None, None]
    same_shared = (seg_shared[:half, None] == seg_shared[None, :])[None, None]
    masks = (same_own, same_shared)

    middle, t_saved = forward_layer(inputs, away, masks, t_full, t_bias, t_norms)
    away = swap_y(middle[2 * half :].astype(LOW))
    last, s_saved = forward_layer(middle, away, masks, s_full, s_bias, s_norms)

    def to_rows(value):
        far = swap_y(value[half : 2 * half].astype(LOW))
        mine = jnp.concatenate([value[:half], value[2 * half :]], axis=0)
        high = mine.astype(LOW)
        low = (mine - high.astype(F32)).astype(LOW)
        back = lambda part: jnp.einsum("nd,ed->ne", part, into, preferred_element_type=F32)
        mine = back(high) + back(low)
        far = back(far)
        return jnp.stack([jnp.where(first, mine[:half], far), mine[half:], jnp.where(first, far, mine[:half])])

    output = to_rows(last)

    d_mid, d_up, d_down, s_up_grad, s_norm_grads = backward_ffn(grad_in, s_full, s_norms, s_saved)
    d_first, grads, s_qv_grad = backward_attn(d_mid, masks, s_full, s_saved)
    s_sum = reduce_pair(
        {"up": d_up, "q": grads["q"], "out": grads["out"]}, {"down": d_down, "k": grads["k"], "v": grads["v"]}
    )
    d_mid, d_up, d_down, t_up_grad, t_norm_grads = backward_ffn(d_first, t_full, t_norms, t_saved)
    t_sum = reduce_pair({"up": d_up}, {"down": d_down})
    d_tokens, grads, t_qv_grad = backward_attn(d_mid, masks, t_full, t_saved)
    norm_grads = jnp.stack(t_norm_grads + s_norm_grads)
    norm_cols = jnp.pad(norm_grads, ((0, 128 - norm_grads.shape[0]), (0, 0))).T
    core_half = width // 2
    spread = lambda value: jnp.broadcast_to(value[None], (2,) + value.shape)
    norm_pair = (spread(norm_cols[core_half:].astype(LOW)), spread(norm_cols[:core_half]))
    t_sum.update(
        reduce_pair(
            {"q": grads["q"], "k": grads["k"]}, {"v": grads["v"], "out": grads["out"], "norm": norm_pair}
        )
    )
    input_grad = to_rows(d_tokens)

    bias_grads = jnp.concatenate(
        [t_qv_grad[0], t_qv_grad[1], t_up_grad, s_qv_grad[0], s_qv_grad[1], s_up_grad], axis=1
    )
    bias_sum = lax.psum(bias_grads[0] + swap_y(bias_grads[1]), "dp")
    pick = [bias_sum[cuts[i] : cuts[i + 1]] for i in range(6)]
    norm_sum = t_sum["norm"][:, :12].T
    qkv = lambda sums: jnp.stack([sums["q"], sums["k"], sums["v"]])
    return (
        output, input_grad,
        qkv(t_sum), jnp.stack([pick[0], pick[1]]), t_sum["out"].T, t_sum["up"], pick[2], t_sum["down"].T,
        norm_sum[0:2], norm_sum[2:6],
        qkv(s_sum), jnp.stack([pick[3], pick[4]]), s_sum["out"].T, s_sum["up"], pick[5], s_sum["down"].T,
        norm_sum[6:8], norm_sum[8:12],
    )


def solution(mesh):
    layer = (
        P(None, "dp", "mp"), P(None, "mp"), P("mp", "dp"), P("dp", "mp"), P("mp"), P("mp", "dp"),
        P(None, "dp"), P(None, "dp"),
    )
    rows = P("dp", "mp", None)
    return jax.shard_map(
        on_device,
        mesh=mesh,
        in_specs=(rows, P("dp", None), rows) + layer + layer,
        out_specs=(rows, rows) + layer + layer,
        check_vma=False,
    )
```

time: 1600 us -> 685 us (0.43)
  blocking collectives: 561 us -> 61.1 us
  waiting for transfers between devices: 539 us -> 158 us
  starting transfers between devices: 2.58 us -> 52.3 us
  matrix products: 248 us -> 207 us
  other arithmetic: 134 us -> 101 us
  between operations: 21.4 us -> 3.76 us
    all_gather x31 -> x0, blocking collectives: 464 us -> none  [the longest x24 323 us: gather_rows(): lax.all_gather(share_low.reshape(rows, -1, D), 'mp', axis=1, tiled=True)]
    reduce_scatter x30 -> x0, waiting for transfers between devices: 441 us -> none  [the longest x2 146 us: shard_grads(): lax.psum_scatter(grads[2], 'dp', scatter_dimension=0, tiled=True)]
    ppermute x0 -> x63, waiting for transfers between devices: none -> 158 us  [the longest x18 67.7 us: ring_shift(): return lax.ppermute(value, 'dp', pairs)]
    all_gather x5 -> x0, waiting for transfers between devices: 86 us -> none  [the longest x2 65.3 us: fetch_layer(): lax.all_gather(shards[3], 'dp', axis=1, tiled=True)]
    ppermute x0 -> x63, starting transfers between devices: none -> 52.3 us  [the longest x21 24.9 us: swap_y(): return lax.ppermute(value, 'mp', [(0, 1), (1, 0)])]
    dot_general x108 -> x84, matrix products: 248 us -> 207 us  [the longest x12 31.3 us: weight_grad(): jnp.einsum('nd,ync->ydc', left[:, half:], right, preferred_element_type=F32)]
    convert_element_type x34 -> x21, other arithmetic: 52.6 us -> 16.3 us  [the longest x4 11.5 us: attend_back(): d_scores = (probs * (d_probs - inner)).astype(LOW)]
    psum x2 -> x1, blocking collectives: 96.9 us -> 61.1 us  [on_device(): bias_sum = lax.psum(bias_grads[0] + swap_y(bias_grads[1]), 'dp')]
  transfers between devices with their start and end apart: 36 -> 63, of which waited for: 14 -> 23; matrix products, arithmetic and copies ran while one was open for 21% -> 50% of each run, Pallas kernels for 0% -> 0%
where the time goes in v1:
time: 685 us; the launch traced here: 679 us
  matrix products  207 us (30%)
  waiting for transfers between devices  158 us (23%)
  other arithmetic  101 us (15%)
  local copies, waits for them, and re-layouts  95 us (14%)
  blocking collectives  61.1 us (9%)
  starting transfers between devices  52.3 us (8%)
    ppermute x18, waiting for transfers between devices, ring_shift(): return lax.ppermute(value, 'dp', pairs)  67.7 us
    psum x1, blocking collectives, on_device(): bias_sum = lax.psum(bias_grads[0] + swap_y(bias_grads[1]), 'dp')  61.1 us
    ppermute x12, waiting for transfers between devices, swap_x(): return lax.ppermute(value, 'dp', [(i, i ^ 2) for i in range(n)])  60.9 us
    dot_general x12, matrix products, weight_grad(): jnp.einsum('nd,ync->ydc', left[:, half:], right, preferred_element_type=F32)  31.3 us
    ppermute x21, waiting for transfers between devices, swap_y(): return lax.ppermute(value, 'mp', [(0, 1), (1, 0)])  29.8 us
    dot_general x12, matrix products, weight_grad(): jnp.einsum('nd,ync->ydc', left[:, :half], right, preferred_element_type=F32)  28.1 us
    ppermute x21, starting transfers between devices, swap_y(): return lax.ppermute(value, 'mp', [(0, 1), (1, 0)])  24.9 us
    unnamed x315, local copies, waits for them, and re-layouts  22 us
  transfers between devices with their start and end apart: 63, of which 23 were waited for; matrix products, arithmetic and copies ran while one was open for 50% of the time, Pallas kernels for 0%

profile of v1, /device:TPU:0, one launch (start us, length us, event | category | flops | bytes accessed | tf_op | source)
XLA Modules:
  0.0 678.7 jit_solution(14876607063139147103)
XLA Ops:
  4.3 3.0 collective-permute-start.7
  14.3 2.6 collective-permute-start.1
  32.6 3.0 collective-permute-start.21
  39.7 3.9 collective-permute-done.21
  45.2 8.0 %collective-permute-done.3 = bf16[48,1664]{1,0:T(8,128)(2,1)S(1)} collective-permute-done((bf16[48,1664]{1,0:T(8,128)(2,1)S(1)}, bf16[48,1664]{1,0:T(8,128)(2,1)S(1)}, u32[]{:S(2)}, u32[]{:S(2)}) %collective-permute-start.3) | collective-permute-done | bytes 159776 | tf_op jit(solution)/shard_map/ppermute | solution.py:38
  59.2 3.6 collective-permute-done.8
  69.5 6.5 collective-permute-done.27
  79.9 8.2 %collective-permute-done.9 = bf16[2,4,48,768]{3,2,1,0:T(8,128)(2,1)S(1)} collective-permute-done((bf16[2,4,48,768]{3,2,1,0:T(8,128)(2,1)S(1)}, bf16[2,4,48,768]{3,2,1,0:T(8,128)(2,1)S(1)}, u32[]{:S(2)}, u32[]{:S(2)}) %collective-permute-start.9) | collective-permute-done | bytes 589856 | tf_op jit(solution)/shard_map/ppermute | solution.py:18
  88.8 14.6 %collective-permute-done.14 = bf16[4,48,1536]{2,1,0:T(8,128)(2,1)S(1)} collective-permute-done((bf16[4,48,1536]{2,1,0:T(8,128)(2,1)S(1)}, bf16[4,48,1536]{2,1,0:T(8,128)(2,1)S(1)}, u32[]{:S(2)}, u32[]{:S(2)}) %collective-permute-start.14) | collective-permute-done | bytes 589856 | tf_op jit(solution)/shard_map/ppermute | solution.py:23
  111.8 7.9 %collective-permute-done.28 = bf16[2,4,48,1152]{3,2,1,0:T(8,128)(2,1)S(1)} collective-permute-done((bf16[2,4,48,1152]{3,2,1,0:T(8,128)(2,1)S(1)}, bf16[2,4,48,1152]{3,2,1,0:T(8,128)(2,1)S(1)}, u32[]{:S(2)}, u32[]{:S(2)}) %collective-permute-start.28) | collective-permute-done | bytes 884768 | tf_op jit(solution)/shard_map/ppermute | solution.py:18
  130.8 2.8 fusion
  138.1 3.1 collective-permute-done.18
  141.2 3.1 fusion.317
  144.3 3.5 collective-permute-done.15
  147.9 3.9 fusion.318
  156.4 4.3 fusion.104
  160.7 2.8 fusion.131
  174.1 2.5 pad_maximum_fusion.1
  181.9 7.2 %fusion.11 = (bf16[2,768,1536]{2,1,0:T(8,128)(2,1)S(1)}, f32[2,1536,768]{1,2,0:T(8,128)}) fusion(f32[2,1536]{1,0:T(2,128)S(1)} %copy-done.119, bf16[2,768,1536]{2,1,0:T(8,128)(2,1)S(1)} %bitcast.673, bf16[768,768]{1,0:T(8,128)(2,1)S(1)} %fusion.57), kind=kOutput, calls=%fused_computation.21 | convolution fusion | flops 3638034432 | bytes 20066304 | tf_op jit(solution)/shard_map/nd,ydf->ynf/dot_general | solution.py:193
  189.1 4.1 fusion.339
  201.0 4.3 collective-permute-done.26
  218.8 4.1 fusion.29
  226.4 2.7 multiply_reduce_fusion.4
  232.4 6.2 convert_reduce_fusion.1
  238.5 2.7 multiply_reduce_fusion.5
  248.4 2.7 convolution_bitcast_fusion.2
  282.3 3.9 concatenate.160
  286.3 2.6 fusion.135
  290.3 4.0 concatenate.162
  294.8 3.5 fusion.54
  301.3 4.6 concatenate.161
  305.9 4.5 concatenate.159
  313.0 4.0 fusion.93
  322.3 10.1 %convert_reduce_fusion = (f32[2,1536]{1,0:T(2,128)}, bf16[2,768,1536]{2,1,0:T(8,128)(2,1)S(1)}) fusion(f32[2,1536,768]{1,2,0:T(8,128)} %get-tuple-element.275, f32[2,1536]{1,0:T(2,128)S(1)} %copy-done.120, bf16[2,768,1536]{2,1,0:T(8,128)(2,1)S(1)} %bitcast.672, bf16[768,768]{1,0:T(8,128)(2,1)S(1)} %convert_element_type.618), kind=kOutput, calls=%fused_computation.22 | convolution fusion | flops 3659265024 | bytes 20078592 | tf_op jit(solution)/shard_map/nd,ydf->ynf/dot_general | solution.py:214
  332.5 4.4 multiply_reduce_fusion.7
  342.7 2.6 fusion.95
  350.4 8.8 %fusion.101 = bf16[2,6,64,512]{3,2,1,0:T(8,128)(2,1)} fusion(bf16[2,512,6,64]{1,3,2,0:T(8,128)(2,1)} %bitcast.699, f32[2,6,512]{2,1,0:T(8,128)S(1)} %copy-done.107, f32[2,6,512,512]{2,3,1,0:T(8,128)} %copy-done, pred[512,512]{0,1:T(8,128)(4,1)S(1)} %broadcast_compare_fusion), kind=kOutput, calls=%fused_computation.245 | convolution fusion | flops 415629312 | bytes 14442496 | tf_op jit(solution)/shard_map/yhqk,yqhe->ykhe/dot_general | solution.py:168
  363.6 3.3 fusion.122
  369.0 5.9 fusion.39
  374.9 3.6 fusion.40
  386.7 7.0 %multiply_reduce_fusion = (f32[2,6,512]{2,1,0:T(8,128)S(1)}, f32[2,6,512,512]{2,3,1,0:T(8,128)}) fusion(f32[2,6,512]{2,1,0:T(8,128)S(1)} %copy-done.107, f32[2,6,512,512]{2,3,1,0:T(8,128)S(1)} %bitcast.633, pred[512,512]{0,1:T(8,128)(4,1)S(1)} %broadcast_compare_fusion, bf16[2,512,6,64]{1,3,2,0:T(8,128)(2,1)S(1)} %bitcast.700, ...), kind=kOutput, calls=%fused_computation.2 | convolution fusion | flops 418375680 | bytes 27049984 | tf_op jit(solution)/shard_map/yqhe,ykhe->yhqk/dot_general | solution.py:169
  393.7 7.1 %multiply_convert_fusion = bf16[2,6,512,512]{2,3,1,0:T(8,128)(2,1)S(1)} fusion(f32[2,6,512,512]{2,3,1,0:T(8,128)} %get-tuple-element.298, f32[2,6,512]{2,1,0:T(8,128)S(1)} %get-tuple-element.297, f32[2,6,512]{2,1,0:T(8,128)S(1)} %copy-done.107, f32[2,6,512,512]{2,3,1,0:T(8,128)S(1)} %bitcast.633, pred[512,512]{0,1:T(8,128)(4,1)S(1)} %broadcast_compare_fusion), kind=kLoop, calls=%fused_computation.1 | loop fusion | flops 18874368 | bytes 31768576 | tf_op jit(solution)/shard_map/convert_element_type | solution.py:171
  400.8 2.9 multiply_convert_fusion.5
  411.4 3.1 fusion.120
  416.7 2.8 convolution_bitcast_fusion.13
  421.9 2.8 fusion.121
  428.5 2.5 fusion.141
  432.7 2.6 fusion.115
  437.7 2.9 fusion.171
  444.2 3.8 bitcast_add_fusion.2
  450.3 61.1 %psum.7 = f32[3456]{0:T(1024)S(1)} all-reduce(f32[3456]{0:T(1024)S(1)} %add.551), channel_id=1, replica_groups=mesh['dp'=16,'mp'=2] {'dp'}, use_global_device_ids=true, to_apply=%region_47.48 | all-reduce | flops 3456 | bytes 27648 | tf_op jit(solution)/shard_map/psum | solution.py:344
  542.4 7.7 %collective-permute-done.39 = bf16[2,192,896]{2,1,0:T(8,128)(2,1)S(1)} collective-permute-done((bf16[2,192,896]{2,1,0:T(8,128)(2,1)}, bf16[2,192,896]{2,1,0:T(8,128)(2,1)S(1)}, u32[]{:S(2)}, u32[]{:S(2)}) %collective-permute-start.39) | collective-permute-done | bytes 688160 | tf_op jit(solution)/shard_map/ppermute | solution.py:23
  554.7 22.2 %collective-permute-done.37 = bf16[192,768]{0,1:T(8,128)(2,1)S(1)} collective-permute-done((bf16[192,768]{0,1:T(8,128)(2,1)S(1)}, bf16[192,768]{0,1:T(8,128)(2,1)S(1)}, u32[]{:S(2)}, u32[]{:S(2)}) %collective-permute-start.37) | collective-permute-done | bytes 294944 | tf_op jit(solution)/shard_map/ppermute | solution.py:23
  582.9 5.3 bitcast_add_fusion
  590.9 3.9 bitcast_add_fusion.1
  598.5 8.2 %collective-permute-done.41 = bf16[48,1664]{0,1:T(8,128)(2,1)S(1)} collective-permute-done((bf16[48,1664]{0,1:T(8,128)(2,1)S(1)}, bf16[48,1664]{0,1:T(8,128)(2,1)S(1)}, u32[]{:S(2)}, u32[]{:S(2)}) %collective-permute-start.41) | collective-permute-done | bytes 159776 | tf_op jit(solution)/shard_map/ppermute | solution.py:38
  607.3 10.2 %collective-permute-done.42 = bf16[48,1664]{0,1:T(8,128)(2,1)S(1)} collective-permute-done((bf16[48,1664]{0,1:T(8,128)(2,1)S(1)}, bf16[48,1664]{0,1:T(8,128)(2,1)S(1)}, u32[]{:S(2)}, u32[]{:S(2)}) %collective-permute-start.42) | collective-permute-done | bytes 159776 | tf_op jit(solution)/shard_map/ppermute | solution.py:38
  618.6 11.1 %collective-permute-done.43 = bf16[48,1664]{0,1:T(8,128)(2,1)S(1)} collective-permute-done((bf16[48,1664]{0,1:T(8,128)(2,1)S(1)}, bf16[48,1664]{0,1:T(8,128)(2,1)S(1)}, u32[]{:S(2)}, u32[]{:S(2)}) %collective-permute-start.43) | collective-permute-done | bytes 159776 | tf_op jit(solution)/shard_map/ppermute | solution.py:38
  640.7 4.4 collective-permute-done.50
  645.2 3.2 collective-permute-done.47
  649.9 9.1 %collective-permute-done.51 = bf16[48,3072]{1,0:T(8,128)(2,1)S(1)} collective-permute-done((bf16[48,3072]{1,0:T(8,128)(2,1)S(1)}, bf16[48,3072]{1,0:T(8,128)(2,1)S(1)}, u32[]{:S(2)}, u32[]{:S(2)}) %collective-permute-start.51) | collective-permute-done | bytes 294944 | tf_op jit(solution)/shard_map/ppermute | solution.py:38
  659.2 2.6 collective-permute-done.62
  662.5 7.3 %collective-permute-done.52 = bf16[48,3072]{1,0:T(8,128)(2,1)S(1)} collective-permute-done((bf16[48,3072]{1,0:T(8,128)(2,1)S(1)}, bf16[48,3072]{1,0:T(8,128)(2,1)S(1)}, u32[]{:S(2)}, u32[]{:S(2)}) %collective-permute-start.52) | collective-permute-done | bytes 294944 | tf_op jit(solution)/shard_map/ppermute | solution.py:38
  671.3 6.2 collective-permute-done.53
  (715 shorter events, 287.8 us)
Async XLA Ops:
  4.3 23.8 %collective-permute-start.7 = (bf16[3456]{0:T(1024)(128)(2,1)}, bf16[3456]{0:T(1024)(128)(2,1)}, u32[]{:S(2)}, u32[]{:S(2)}) collective-permute-start(bf16[3456]{0:T(1024)(128)(2,1)} %concatenate.129), channel_id=1, source_target_pairs={{0,1},{1,0},{2,3},{3,2},{4,5},{5,4},{6,7},{7,6},{8,9},{9,8},{10,11... | collective-permute-start | bytes 20744 | tf_op jit(solution)/shard_map/ppermute | solution.py:18
  14.3 16.5 %collective-permute-start.1 = (bf16[48,1664]{1,0:T(8,128)(2,1)}, bf16[48,1664]{1,0:T(8,128)(2,1)}, u32[]{:S(2)}, u32[]{:S(2)}) collective-permute-start(bf16[48,1664]{1,0:T(8,128)(2,1)} %get-tuple-element.256), channel_id=1, source_target_pairs={{0,16},{2,18},{4,20},{6,22},{16,24},{18,26},{20,28},{22,30},{24,8}... | collective-permute-start | bytes 479240 | tf_op jit(solution)/shard_map/ppermute | solution.py:38
  19.3 13.3 %collective-permute-start.20 = (bf16[48,2304]{1,0:T(8,128)(2,1)}, bf16[48,2304]{1,0:T(8,128)(2,1)}, u32[]{:S(2)}, u32[]{:S(2)}) collective-permute-start(bf16[48,2304]{1,0:T(8,128)(2,1)} %concatenate.138), channel_id=1, source_target_pairs={{0,16},{2,18},{4,20},{6,22},{16,24},{18,26},{20,28},{22,30},{24,8}... | collective-permute-start | bytes 663560 | tf_op jit(solution)/shard_map/ppermute | solution.py:38
  22.0 14.7 %collective-permute-start.11 = (bf16[48,3072]{1,0:T(8,128)(2,1)S(1)}, bf16[48,3072]{1,0:T(8,128)(2,1)}, u32[]{:S(2)}, u32[]{:S(2)}) collective-permute-start(bf16[48,3072]{1,0:T(8,128)(2,1)S(1)} %pad_maximum_fusion.53), channel_id=1, source_target_pairs={{0,16},{2,18},{4,20},{6,22},{16,24},{18,26},{20,28},{22,30},{24,8}... | collective-permute-start | bytes 884744 | tf_op jit(solution)/shard_map/ppermute | solution.py:38
  24.3 40.1 %collective-permute-start = (bf16[2,256,768]{2,1,0:T(8,128)(2,1)}, bf16[2,256,768]{2,1,0:T(8,128)(2,1)S(1)}, u32[]{:S(2)}, u32[]{:S(2)}) collective-permute-start(bf16[2,256,768]{2,1,0:T(8,128)(2,1)} %pad_maximum_fusion.32), channel_id=1, source_target_pairs={{0,1},{1,0},{2,3},{3,2},{4,5},{5,4},{6,7},{7,6},{8,9},{9,8},{10,11... | collective-permute-start | bytes 2359304 | tf_op jit(solution)/shard_map/ppermute | solution.py:18
  27.2 285.9 %copy-start.110 = (s32[768]{0:T(1024)}, s32[768]{0:T(1024)S(1)}, u32[]{:S(2)}) copy-start(s32[768]{0:T(1024)S(1)} %fusion.256) | copy-start | bytes 9220
  31.7 7.6 %collective-permute-start.2 = (bf16[48,1664]{1,0:T(8,128)(2,1)}, bf16[48,1664]{1,0:T(8,128)(2,1)S(1)}, u32[]{:S(2)}, u32[]{:S(2)}) collective-permute-start(bf16[48,1664]{1,0:T(8,128)(2,1)} %collective-permute-done.1), channel_id=1, source_target_pairs={{0,16},{2,18},{4,20},{6,22},{16,24},{18,26},{20,28},{22,30},{24,8}... | collective-permute-start | bytes 479240 | tf_op jit(solution)/shard_map/ppermute | solution.py:38
  32.6 11.0 %collective-permute-start.21 = (bf16[48,2304]{1,0:T(8,128)(2,1)}, bf16[48,2304]{1,0:T(8,128)(2,1)S(1)}, u32[]{:S(2)}, u32[]{:S(2)}) collective-permute-start(bf16[48,2304]{1,0:T(8,128)(2,1)} %collective-permute-done.20), channel_id=1, source_target_pairs={{0,16},{2,18},{4,20},{6,22},{16,24},{18,26},{20,28},{22,30},{24,8}... | collective-permute-start | bytes 663560 | tf_op jit(solution)/shard_map/ppermute | solution.py:38
  37.7 19.0 %collective-permute-start.12 = (bf16[48,3072]{1,0:T(8,128)(2,1)}, bf16[48,3072]{1,0:T(8,128)(2,1)S(1)}, u32[]{:S(2)}, u32[]{:S(2)}) collective-permute-start(bf16[48,3072]{1,0:T(8,128)(2,1)} %collective-permute-done.11), channel_id=1, source_target_pairs={{0,16},{2,18},{4,20},{6,22},{16,24},{18,26},{20,28},{22,30},{24,8}... | collective-permute-start | bytes 884744 | tf_op jit(solution)/shard_map/ppermute | solution.py:38
  39.3 13.9 %collective-permute-start.3 = (bf16[48,1664]{1,0:T(8,128)(2,1)S(1)}, bf16[48,1664]{1,0:T(8,128)(2,1)S(1)}, u32[]{:S(2)}, u32[]{:S(2)}) collective-permute-start(bf16[48,1664]{1,0:T(8,128)(2,1)S(1)} %collective-permute-done.2), channel_id=1, source_target_pairs={{0,16},{2,18},{4,20},{6,22},{16,24},{18,26},{20,28},{22,30},{24,8}... | collective-permute-start | bytes 479240 | tf_op jit(solution)/shard_map/ppermute | solution.py:38
  43.7 14.7 %collective-permute-start.22 = (bf16[48,2304]{1,0:T(8,128)(2,1)S(1)}, bf16[48,2304]{1,0:T(8,128)(2,1)S(1)}, u32[]{:S(2)}, u32[]{:S(2)}) collective-permute-start(bf16[48,2304]{1,0:T(8,128)(2,1)S(1)} %collective-permute-done.21), channel_id=1, source_target_pairs={{0,16},{2,18},{4,20},{6,22},{16,24},{18,26},{20,28},{22,30},{24,8}... | collective-permute-start | bytes 663560 | tf_op jit(solution)/shard_map/ppermute | solution.py:38
  53.2 9.6 %collective-permute-start.8 = (bf16[4,48,768]{2,1,0:T(8,128)(2,1)S(1)}, bf16[4,48,768]{2,1,0:T(8,128)(2,1)S(1)}, u32[]{:S(2)}, u32[]{:S(2)}) collective-permute-start(bf16[4,48,768]{2,1,0:T(8,128)(2,1)S(1)} %get-tuple-element.234), channel_id=1, source_target_pairs={{0,4},{2,6},{4,0},{6,2},{8,12},{10,14},{12,8},{14,10},{16,20},{18,... | collective-permute-start | bytes 884744 | tf_op jit(solution)/shard_map/ppermute | solution.py:23
  54.9 13.3 %collective-permute-start.4 = (bf16[4,48,896]{2,1,0:T(8,128)(2,1)S(1)}, bf16[4,48,896]{2,1,0:T(8,128)(2,1)S(1)}, u32[]{:S(2)}, u32[]{:S(2)}) collective-permute-start(bf16[4,48,896]{2,1,0:T(8,128)(2,1)S(1)} %get-tuple-element.226), channel_id=1, source_target_pairs={{0,1},{1,0},{2,3},{3,2},{4,5},{5,4},{6,7},{7,6},{8,9},{9,8},{10,11... | collective-permute-start | bytes 1032200 | tf_op jit(solution)/shard_map/ppermute | solution.py:18
  56.7 11.8 %collective-permute-start.13 = (bf16[48,3072]{1,0:T(8,128)(2,1)S(1)}, bf16[48,3072]{1,0:T(8,128)(2,1)S(1)}, u32[]{:S(2)}, u32[]{:S(2)}) collective-permute-start(bf16[48,3072]{1,0:T(8,128)(2,1)S(1)} %collective-permute-done.12), channel_id=1, source_target_pairs={{0,16},{2,18},{4,20},{6,22},{16,24},{18,26},{20,28},{22,30},{24,8}... | collective-permute-start | bytes 884744 | tf_op jit(solution)/shard_map/ppermute | solution.py:38
  58.6 19.1 %collective-permute-start.23 = (bf16[4,48,1152]{2,1,0:T(8,128)(2,1)S(1)}, bf16[4,48,1152]{2,1,0:T(8,128)(2,1)S(1)}, u32[]{:S(2)}, u32[]{:S(2)}) collective-permute-start(bf16[4,48,1152]{2,1,0:T(8,128)(2,1)S(1)} %get-tuple-element.222), channel_id=1, source_target_pairs={{0,1},{1,0},{2,3},{3,2},{4,5},{5,4},{6,7},{7,6},{8,9},{9,8},{10,11... | collective-permute-start | bytes 1327112 | tf_op jit(solution)/shard_map/ppermute | solution.py:18
  62.9 13.1 %collective-permute-start.27 = (bf16[4,48,1152]{2,1,0:T(8,128)(2,1)S(1)}, bf16[4,48,1152]{2,1,0:T(8,128)(2,1)S(1)}, u32[]{:S(2)}, u32[]{:S(2)}) collective-permute-start(bf16[4,48,1152]{2,1,0:T(8,128)(2,1)S(1)} %get-tuple-element.224), channel_id=1, source_target_pairs={{0,4},{2,6},{4,0},{6,2},{8,12},{10,14},{12,8},{14,10},{16,20},{18,... | collective-permute-start | bytes 1327112 | tf_op jit(solution)/shard_map/ppermute | solution.py:23
  64.4 23.6 %collective-permute-start.9 = (bf16[2,4,48,768]{3,2,1,0:T(8,128)(2,1)S(1)}, bf16[2,4,48,768]{3,2,1,0:T(8,128)(2,1)S(1)}, u32[]{:S(2)}, u32[]{:S(2)}) collective-permute-start(bf16[2,4,48,768]{3,2,1,0:T(8,128)(2,1)S(1)} %get-tuple-element.212), channel_id=1, source_target_pairs={{0,1},{1,0},{2,3},{3,2},{4,5},{5,4},{6,7},{7,6},{8,9},{9,8},{10,11... | collective-permute-start | bytes 1769480 | tf_op jit(solution)/shard_map/ppermute | solution.py:18
  68.3 39.9 %collective-permute-start.5 = (bf16[2,4,48,896]{3,2,1,0:T(8,128)(2,1)S(1)}, bf16[2,4,48,896]{3,2,1,0:T(8,128)(2,1)S(1)}, u32[]{:S(2)}, u32[]{:S(2)}) collective-permute-start(bf16[2,4,48,896]{3,2,1,0:T(8,128)(2,1)S(1)} %get-tuple-element.206), channel_id=1, source_target_pairs={{0,4},{2,6},{4,0},{6,2},{8,12},{10,14},{12,8},{14,10},{16,20},{18,... | collective-permute-start | bytes 2064392 | tf_op jit(solution)/shard_map/ppermute | solution.py:23
  69.3 35.6 %collective-permute-start.17 = (bf16[4,48,1536]{2,1,0:T(8,128)(2,1)S(1)}, bf16[4,48,1536]{2,1,0:T(8,128)(2,1)S(1)}, u32[]{:S(2)}, u32[]{:S(2)}) collective-permute-start(bf16[4,48,1536]{2,1,0:T(8,128)(2,1)S(1)} %get-tuple-element.210), channel_id=1, source_target_pairs={{0,1},{1,0},{2,3},{3,2},{4,5},{5,4},{6,7},{7,6},{8,9},{9,8},{10,11... | collective-permute-start | bytes 1769480 | tf_op jit(solution)/shard_map/ppermute | solution.py:18
  76.0 27.4 %collective-permute-start.14 = (bf16[4,48,1536]{2,1,0:T(8,128)(2,1)S(1)}, bf16[4,48,1536]{2,1,0:T(8,128)(2,1)S(1)}, u32[]{:S(2)}, u32[]{:S(2)}) collective-permute-start(bf16[4,48,1536]{2,1,0:T(8,128)(2,1)S(1)} %get-tuple-element.214), channel_id=1, source_target_pairs={{0,4},{2,6},{4,0},{6,2},{8,12},{10,14},{12,8},{14,10},{16,20},{18,... | collective-permute-start | bytes 1769480 | tf_op jit(solution)/shard_map/ppermute | solution.py:23
  77.6 42.0 %collective-permute-start.28 = (bf16[2,4,48,1152]{3,2,1,0:T(8,128)(2,1)S(1)}, bf16[2,4,48,1152]{3,2,1,0:T(8,128)(2,1)S(1)}, u32[]{:S(2)}, u32[]{:S(2)}) collective-permute-start(bf16[2,4,48,1152]{3,2,1,0:T(8,128)(2,1)S(1)} %get-tuple-element.194), channel_id=1, source_target_pairs={{0,1},{1,0},{2,3},{3,2},{4,5},{5,4},{6,7},{7,6},{8,9},{9,8},{10,11... | collective-permute-start | bytes 2654216 | tf_op jit(solution)/shard_map/ppermute | solution.py:18
  88.1 34.3 %collective-permute-start.24 = (bf16[2,4,48,1152]{3,2,1,0:T(8,128)(2,1)S(1)}, bf16[2,4,48,1152]{3,2,1,0:T(8,128)(2,1)S(1)}, u32[]{:S(2)}, u32[]{:S(2)}) collective-permute-start(bf16[2,4,48,1152]{3,2,1,0:T(8,128)(2,1)S(1)} %get-tuple-element.192), channel_id=1, source_target_pairs={{0,4},{2,6},{4,0},{6,2},{8,12},{10,14},{12,8},{14,10},{16,20},{18,... | collective-permute-start | bytes 2654216 | tf_op jit(solution)/shard_map/ppermute | solution.py:23
  103.4 21.0 %collective-permute-start.10 = (bf16[2,2,4,48,768]{4,3,2,1,0:T(8,128)(2,1)S(1)}, bf16[2,2,4,48,768]{4,3,2,1,0:T(8,128)(2,1)S(1)}, u32[]{:S(2)}, u32[]{:S(2)}) collective-permute-start(bf16[2,2,4,48,768]{4,3,2,1,0:T(8,128)(2,1)S(1)} %get-tuple-element.184), channel_id=1, source_target_pairs={{0,2},{2,0},{4,6},{6,4},{8,10},{10,8},{12,14},{14,12},{16,18},{18,... | collective-permute-start | bytes 3538952 | tf_op jit(solution)/shard_map/ppermute | solution.py:28
  104.9 120.8 %collective-permute-start.31 = (bf16[256,768]{1,0:T(8,128)(2,1)S(1)}, bf16[256,768]{1,0:T(8,128)(2,1)}, u32[]{:S(2)}, u32[]{:S(2)}) collective-permute-start(bf16[256,768]{1,0:T(8,128)(2,1)S(1)} %get-tuple-element.180), channel_id=1, source_target_pairs={{0,1},{1,0},{2,3},{3,2},{4,5},{5,4},{6,7},{7,6},{8,9},{9,8},{10,11... | collective-permute-start | bytes 1179656 | tf_op jit(solution)/shard_map/ppermute | solution.py:18
  108.1 33.1 %collective-permute-start.18 = (bf16[2,4,48,1536]{3,2,1,0:T(8,128)(2,1)}, bf16[2,4,48,1536]{3,2,1,0:T(8,128)(2,1)}, u32[]{:S(2)}, u32[]{:S(2)}) collective-permute-start(bf16[2,4,48,1536]{3,2,1,0:T(8,128)(2,1)} %get-tuple-element.182), channel_id=1, source_target_pairs={{0,4},{2,6},{4,0},{6,2},{8,12},{10,14},{12,8},{14,10},{16,20},{18,... | collective-permute-start | bytes 3538952 | tf_op jit(solution)/shard_map/ppermute | solution.py:23
  119.7 28.2 %collective-permute-start.15 = (bf16[2,4,48,1536]{3,2,1,0:T(8,128)(2,1)}, bf16[2,4,48,1536]{3,2,1,0:T(8,128)(2,1)}, u32[]{:S(2)}, u32[]{:S(2)}) collective-permute-start(bf16[2,4,48,1536]{3,2,1,0:T(8,128)(2,1)} %get-tuple-element.190), channel_id=1, source_target_pairs={{0,1},{1,0},{2,3},{3,2},{4,5},{5,4},{6,7},{7,6},{8,9},{9,8},{10,11... | collective-permute-start | bytes 3538952 | tf_op jit(solution)/shard_map/ppermute | solution.py:18
  122.3 29.4 %collective-permute-start.6 = (bf16[2,2,4,48,896]{4,3,2,1,0:T(8,128)(2,1)}, bf16[2,2,4,48,896]{4,3,2,1,0:T(8,128)(2,1)}, u32[]{:S(2)}, u32[]{:S(2)}) collective-permute-start(bf16[2,2,4,48,896]{4,3,2,1,0:T(8,128)(2,1)} %get-tuple-element.177), channel_id=1, source_target_pairs={{0,2},{2,0},{4,6},{6,4},{8,10},{10,8},{12,14},{14,12},{16,18},{18,... | collective-permute-start | bytes 4128776 | tf_op jit(solution)/shard_map/ppermute | solution.py:28
  124.4 73.0 %collective-permute-start.25 = (bf16[2,2,4,48,1152]{4,3,2,1,0:T(8,128)(2,1)}, bf16[2,2,4,48,1152]{4,3,2,1,0:T(8,128)(2,1)}, u32[]{:S(2)}, u32[]{:S(2)}) collective-permute-start(bf16[2,2,4,48,1152]{4,3,2,1,0:T(8,128)(2,1)} %get-tuple-element.167), channel_id=1, source_target_pairs={{0,2},{2,0},{4,6},{6,4},{8,10},{10,8},{12,14},{14,12},{16,18},{18,... | collective-permute-start | bytes 5308424 | tf_op jit(solution)/shard_map/ppermute | solution.py:28
  141.2 54.0 %collective-permute-start.29 = (bf16[2,2,4,48,1152]{4,3,2,1,0:T(8,128)(2,1)}, bf16[2,2,4,48,1152]{4,3,2,1,0:T(8,128)(2,1)}, u32[]{:S(2)}, u32[]{:S(2)}) collective-permute-start(bf16[2,2,4,48,1152]{4,3,2,1,0:T(8,128)(2,1)} %get-tuple-element.169), channel_id=1, source_target_pairs={{0,2},{2,0},{4,6},{6,4},{8,10},{10,8},{12,14},{14,12},{16,18},{18,... | collective-permute-start | bytes 5308424 | tf_op jit(solution)/shard_map/ppermute | solution.py:28
  147.9 26.2 %collective-permute-start.19 = (bf16[2,2,4,48,1536]{4,3,2,0,1:T(8,128)(2,1)}, bf16[2,2,4,48,1536]{4,3,2,0,1:T(8,128)(2,1)}, u32[]{:S(2)}, u32[]{:S(2)}) collective-permute-start(bf16[2,2,4,48,1536]{4,3,2,0,1:T(8,128)(2,1)} %get-tuple-element.163), channel_id=1, source_target_pairs={{0,2},{2,0},{4,6},{6,4},{8,10},{10,8},{12,14},{14,12},{16,18},{18,... | collective-permute-start | bytes 7077896 | tf_op jit(solution)/shard_map/ppermute | solution.py:28
  151.8 25.3 %collective-permute-start.16 = (bf16[2,2,4,48,1536]{4,3,2,1,0:T(8,128)(2,1)}, bf16[2,2,4,48,1536]{4,3,2,1,0:T(8,128)(2,1)}, u32[]{:S(2)}, u32[]{:S(2)}) collective-permute-start(bf16[2,2,4,48,1536]{4,3,2,1,0:T(8,128)(2,1)} %get-tuple-element.165), channel_id=1, source_target_pairs={{0,2},{2,0},{4,6},{6,4},{8,10},{10,8},{12,14},{14,12},{16,18},{18,... | collective-permute-start | bytes 7077896 | tf_op jit(solution)/shard_map/ppermute | solution.py:28
  194.2 11.1 %collective-permute-start.26 = (bf16[256,768]{1,0:T(8,128)(2,1)S(1)}, bf16[256,768]{1,0:T(8,128)(2,1)S(1)}, u32[]{:S(2)}, u32[]{:S(2)}) collective-permute-start(bf16[256,768]{1,0:T(8,128)(2,1)S(1)} %slice.929), channel_id=1, source_target_pairs={{0,1},{1,0},{2,3},{3,2},{4,5},{5,4},{6,7},{7,6},{8,9},{9,8},{10,11... | collective-permute-start | bytes 1179656 | tf_op jit(solution)/shard_map/ppermute | solution.py:18
  273.6 167.0 %collective-permute-start.30 = (bf16[256,768]{1,0:T(8,128)(2,1)}, bf16[256,768]{1,0:T(8,128)(2,1)}, u32[]{:S(2)}, u32[]{:S(2)}) collective-permute-start(bf16[256,768]{1,0:T(8,128)(2,1)} %slice.1439), channel_id=1, source_target_pairs={{0,1},{1,0},{2,3},{3,2},{4,5},{5,4},{6,7},{7,6},{8,9},{9,8},{10,11... | collective-permute-start | bytes 1179656 | tf_op jit(solution)/shard_map/ppermute | solution.py:18
  276.5 40.6 %collective-permute-start.32 = (bf16[256,768]{1,0:T(8,128)(2,1)}, bf16[256,768]{1,0:T(8,128)(2,1)}, u32[]{:S(2)}, u32[]{:S(2)}) collective-permute-start(bf16[256,768]{1,0:T(8,128)(2,1)} %fusion.113), channel_id=1, source_target_pairs={{0,1},{1,0},{2,3},{3,2},{4,5},{5,4},{6,7},{7,6},{8,9},{9,8},{10,11... | collective-permute-start | bytes 1179656 | tf_op jit(solution)/shard_map/ppermute | solution.py:18
  286.2 245.4 %collective-permute-start.54 = (bf16[2,384,1152]{2,1,0:T(8,128)(2,1)}, bf16[2,384,1152]{2,1,0:T(8,128)(2,1)}, u32[]{:S(2)}, u32[]{:S(2)}) collective-permute-start(bf16[2,384,1152]{2,1,0:T(8,128)(2,1)} %concatenate.160), channel_id=1, source_target_pairs={{0,2},{2,0},{4,6},{6,4},{8,10},{10,8},{12,14},{14,12},{16,18},{18,... | collective-permute-start | bytes 5308424 | tf_op jit(solution)/shard_map/ppermute | solution.py:28
  294.4 240.3 %collective-permute-start.57 = (bf16[2,384,1152]{2,1,0:T(8,128)(2,1)}, bf16[2,384,1152]{2,1,0:T(8,128)(2,1)}, u32[]{:S(2)}, u32[]{:S(2)}) collective-permute-start(bf16[2,384,1152]{2,1,0:T(8,128)(2,1)} %concatenate.162), channel_id=1, source_target_pairs={{0,2},{2,0},{4,6},{6,4},{8,10},{10,8},{12,14},{14,12},{16,18},{18,... | collective-permute-start | bytes 5308424 | tf_op jit(solution)/shard_map/ppermute | solution.py:28
  432.4 91.6 %collective-permute-start.38 = (bf16[2,384,896]{1,2,0:T(8,128)(2,1)}, bf16[2,384,896]{1,2,0:T(8,128)(2,1)}, u32[]{:S(2)}, u32[]{:S(2)}) collective-permute-start(bf16[2,384,896]{1,2,0:T(8,128)(2,1)} %pad_maximum_fusion.19), channel_id=1, source_target_pairs={{0,2},{2,0},{4,6},{6,4},{8,10},{10,8},{12,14},{14,12},{16,18},{18,... | collective-permute-start | bytes 4128776 | tf_op jit(solution)/shard_map/ppermute | solution.py:28
  435.3 78.6 %collective-permute-start.33 = (bf16[256,768]{1,0:T(8,128)(2,1)}, bf16[256,768]{1,0:T(8,128)(2,1)}, u32[]{:S(2)}, u32[]{:S(2)}) collective-permute-start(bf16[256,768]{1,0:T(8,128)(2,1)} %fusion.115), channel_id=1, source_target_pairs={{0,1},{1,0},{2,3},{3,2},{4,5},{5,4},{6,7},{7,6},{8,9},{9,8},{10,11... | collective-permute-start | bytes 1179656 | tf_op jit(solution)/shard_map/ppermute | solution.py:18
  440.6 8.6 %collective-permute-start.44 = (f32[3456]{0:T(1024)S(1)}, f32[3456]{0:T(1024)S(1)}, u32[]{:S(2)}, u32[]{:S(2)}) collective-permute-start(f32[3456]{0:T(1024)S(1)} %get-tuple-element.135), channel_id=1, source_target_pairs={{0,1},{1,0},{2,3},{3,2},{4,5},{5,4},{6,7},{7,6},{8,9},{9,8},{10,11... | collective-permute-start | bytes 41480 | tf_op jit(solution)/shard_map/ppermute | solution.py:18
  449.2 68.0 %collective-permute-start.34 = (bf16[256,768]{1,0:T(8,128)(2,1)S(1)}, bf16[256,768]{1,0:T(8,128)(2,1)S(1)}, u32[]{:S(2)}, u32[]{:S(2)}) collective-permute-start(bf16[256,768]{1,0:T(8,128)(2,1)S(1)} %slice.1438), channel_id=1, source_target_pairs={{0,1},{1,0},{2,3},{3,2},{4,5},{5,4},{6,7},{7,6},{8,9},{9,8},{10,11... | collective-permute-start | bytes 1179656 | tf_op jit(solution)/shard_map/ppermute | solution.py:18
  513.9 7.9 %collective-permute-start.35 = (bf16[2,384,768]{1,2,0:T(8,128)(2,1)}, bf16[2,384,768]{1,2,0:T(8,128)(2,1)S(1)}, u32[]{:S(2)}, u32[]{:S(2)}) collective-permute-start(bf16[2,384,768]{1,2,0:T(8,128)(2,1)} %pad_maximum_fusion.25), channel_id=1, source_target_pairs={{0,2},{2,0},{4,6},{6,4},{8,10},{10,8},{12,14},{14,12},{16,18},{18,... | collective-permute-start | bytes 3538952 | tf_op jit(solution)/shard_map/ppermute | solution.py:28
  517.3 65.7 %collective-permute-start.48 = (bf16[2,384,1536]{2,1,0:T(8,128)(2,1)}, bf16[2,384,1536]{2,1,0:T(8,128)(2,1)}, u32[]{:S(2)}, u32[]{:S(2)}) collective-permute-start(bf16[2,384,1536]{2,1,0:T(8,128)(2,1)} %fusion.40), channel_id=1, source_target_pairs={{0,2},{2,0},{4,6},{6,4},{8,10},{10,8},{12,14},{14,12},{16,18},{18,... | collective-permute-start | bytes 7077896 | tf_op jit(solution)/shard_map/ppermute | solution.py:28
  521.8 69.0 %collective-permute-start.45 = (bf16[2,384,1536]{2,1,0:T(8,128)(2,1)}, bf16[2,384,1536]{2,1,0:T(8,128)(2,1)}, u32[]{:S(2)}, u32[]{:S(2)}) collective-permute-start(bf16[2,384,1536]{2,1,0:T(8,128)(2,1)} %fusion.39), channel_id=1, source_target_pairs={{0,2},{2,0},{4,6},{6,4},{8,10},{10,8},{12,14},{14,12},{16,18},{18,... | collective-permute-start | bytes 7077896 | tf_op jit(solution)/shard_map/ppermute | solution.py:28
  524.0 16.4 %collective-permute-start.36 = (bf16[384,768]{0,1:T(8,128)(2,1)}, bf16[384,768]{0,1:T(8,128)(2,1)}, u32[]{:S(2)}, u32[]{:S(2)}) collective-permute-start(bf16[384,768]{0,1:T(8,128)(2,1)} %fusion.211), channel_id=1, source_target_pairs={{0,1},{1,0},{2,3},{3,2},{4,5},{5,4},{6,7},{7,6},{8,9},{9,8},{10,11... | collective-permute-start | bytes 1769480 | tf_op jit(solution)/shard_map/ppermute | solution.py:18
  531.7 18.5 %collective-permute-start.39 = (bf16[2,192,896]{2,1,0:T(8,128)(2,1)}, bf16[2,192,896]{2,1,0:T(8,128)(2,1)S(1)}, u32[]{:S(2)}, u32[]{:S(2)}) collective-permute-start(bf16[2,192,896]{2,1,0:T(8,128)(2,1)} %copy.359), channel_id=1, source_target_pairs={{0,4},{2,6},{4,0},{6,2},{8,12},{10,14},{12,8},{14,10},{16,20},{18,... | collective-permute-start | bytes 2064392 | tf_op jit(solution)/shard_map/ppermute | solution.py:23
  534.7 43.4 %collective-permute-start.55 = (bf16[384,1152]{1,0:T(8,128)(2,1)}, bf16[384,1152]{1,0:T(8,128)(2,1)}, u32[]{:S(2)}, u32[]{:S(2)}) collective-permute-start(bf16[384,1152]{1,0:T(8,128)(2,1)} %fusion.182), channel_id=1, source_target_pairs={{0,1},{1,0},{2,3},{3,2},{4,5},{5,4},{6,7},{7,6},{8,9},{9,8},{10,11... | collective-permute-start | bytes 2654216 | tf_op jit(solution)/shard_map/ppermute | solution.py:18
  540.4 39.7 %collective-permute-start.58 = (bf16[2,192,1152]{2,1,0:T(8,128)(2,1)}, bf16[2,192,1152]{2,1,0:T(8,128)(2,1)}, u32[]{:S(2)}, u32[]{:S(2)}) collective-permute-start(bf16[2,192,1152]{2,1,0:T(8,128)(2,1)} %slice.1434), channel_id=1, source_target_pairs={{0,4},{2,6},{4,0},{6,2},{8,12},{10,14},{12,8},{14,10},{16,20},{18,... | collective-permute-start | bytes 2654216 | tf_op jit(solution)/shard_map/ppermute | solution.py:23
  551.0 25.9 %collective-permute-start.37 = (bf16[192,768]{0,1:T(8,128)(2,1)S(1)}, bf16[192,768]{0,1:T(8,128)(2,1)S(1)}, u32[]{:S(2)}, u32[]{:S(2)}) collective-permute-start(bf16[192,768]{0,1:T(8,128)(2,1)S(1)} %slice.1437), channel_id=1, source_target_pairs={{0,4},{2,6},{4,0},{6,2},{8,12},{10,14},{12,8},{14,10},{16,20},{18,... | collective-permute-start | bytes 884744 | tf_op jit(solution)/shard_map/ppermute | solution.py:23
  576.9 17.9 %collective-permute-start.40 = (bf16[192,896]{0,1:T(8,128)(2,1)S(1)}, bf16[192,896]{0,1:T(8,128)(2,1)S(1)}, u32[]{:S(2)}, u32[]{:S(2)}) collective-permute-start(bf16[192,896]{0,1:T(8,128)(2,1)S(1)} %fusion.225), channel_id=1, source_target_pairs={{0,1},{1,0},{2,3},{3,2},{4,5},{5,4},{6,7},{7,6},{8,9},{9,8},{10,11... | collective-permute-start | bytes 1032200 | tf_op jit(solution)/shard_map/ppermute | solution.py:18
  579.8 27.3 %collective-permute-start.56 = (bf16[192,1152]{1,0:T(8,128)(2,1)S(1)}, bf16[192,1152]{1,0:T(8,128)(2,1)S(1)}, u32[]{:S(2)}, u32[]{:S(2)}) collective-permute-start(bf16[192,1152]{1,0:T(8,128)(2,1)S(1)} %slice.1436), channel_id=1, source_target_pairs={{0,4},{2,6},{4,0},{6,2},{8,12},{10,14},{12,8},{14,10},{16,20},{18,... | collective-permute-start | bytes 1327112 | tf_op jit(solution)/shard_map/ppermute | solution.py:23
  582.0 25.2 %collective-permute-start.59 = (bf16[192,1152]{1,0:T(8,128)(2,1)S(1)}, bf16[192,1152]{1,0:T(8,128)(2,1)S(1)}, u32[]{:S(2)}, u32[]{:S(2)}) collective-permute-start(bf16[192,1152]{1,0:T(8,128)(2,1)S(1)} %fusion.229), channel_id=1, source_target_pairs={{0,1},{1,0},{2,3},{3,2},{4,5},{5,4},{6,7},{7,6},{8,9},{9,8},{10,11... | collective-permute-start | bytes 1327112 | tf_op jit(solution)/shard_map/ppermute | solution.py:18
  589.4 43.3 %collective-permute-start.49 = (bf16[2,192,1536]{2,1,0:T(8,128)(2,1)}, bf16[2,192,1536]{2,1,0:T(8,128)(2,1)}, u32[]{:S(2)}, u32[]{:S(2)}) collective-permute-start(bf16[2,192,1536]{2,1,0:T(8,128)(2,1)} %slice.1432), channel_id=1, source_target_pairs={{0,4},{2,6},{4,0},{6,2},{8,12},{10,14},{12,8},{14,10},{16,20},{18,... | collective-permute-start | bytes 3538952 | tf_op jit(solution)/shard_map/ppermute | solution.py:23
  595.1 11.6 %collective-permute-start.41 = (bf16[48,1664]{0,1:T(8,128)(2,1)S(1)}, bf16[48,1664]{0,1:T(8,128)(2,1)S(1)}, u32[]{:S(2)}, u32[]{:S(2)}) collective-permute-start(bf16[48,1664]{0,1:T(8,128)(2,1)S(1)} %fusion.192), channel_id=1, source_target_pairs={{0,8},{2,10},{4,12},{6,14},{16,0},{18,2},{20,4},{22,6},{24,16},{26... | collective-permute-start | bytes 479240 | tf_op jit(solution)/shard_map/ppermute | solution.py:38
  597.3 38.7 %collective-permute-start.46 = (bf16[384,1536]{1,0:T(8,128)(2,1)}, bf16[384,1536]{1,0:T(8,128)(2,1)}, u32[]{:S(2)}, u32[]{:S(2)}) collective-permute-start(bf16[384,1536]{1,0:T(8,128)(2,1)} %fusion.138), channel_id=1, source_target_pairs={{0,1},{1,0},{2,3},{3,2},{4,5},{5,4},{6,7},{7,6},{8,9},{9,8},{10,11... | collective-permute-start | bytes 3538952 | tf_op jit(solution)/shard_map/ppermute | solution.py:18
  607.0 10.4 %collective-permute-start.42 = (bf16[48,1664]{0,1:T(8,128)(2,1)S(1)}, bf16[48,1664]{0,1:T(8,128)(2,1)S(1)}, u32[]{:S(2)}, u32[]{:S(2)}) collective-permute-start(bf16[48,1664]{0,1:T(8,128)(2,1)S(1)} %fusion.186), channel_id=1, source_target_pairs={{0,8},{2,10},{4,12},{6,14},{16,0},{18,2},{20,4},{22,6},{24,16},{26... | collective-permute-start | bytes 479240 | tf_op jit(solution)/shard_map/ppermute | solution.py:38
  617.8 11.9 %collective-permute-start.43 = (bf16[48,1664]{0,1:T(8,128)(2,1)S(1)}, bf16[48,1664]{0,1:T(8,128)(2,1)S(1)}, u32[]{:S(2)}, u32[]{:S(2)}) collective-permute-start(bf16[48,1664]{0,1:T(8,128)(2,1)S(1)} %fusion.191), channel_id=1, source_target_pairs={{0,8},{2,10},{4,12},{6,14},{16,0},{18,2},{20,4},{22,6},{24,16},{26... | collective-permute-start | bytes 479240 | tf_op jit(solution)/shard_map/ppermute | solution.py:38
  618.5 21.1 %collective-permute-start.60 = (bf16[48,2304]{1,0:T(8,128)(2,1)}, bf16[48,2304]{1,0:T(8,128)(2,1)}, u32[]{:S(2)}, u32[]{:S(2)}) collective-permute-start(bf16[48,2304]{1,0:T(8,128)(2,1)} %fusion.238), channel_id=1, source_target_pairs={{0,8},{2,10},{4,12},{6,14},{16,0},{18,2},{20,4},{22,6},{24,16},{26... | collective-permute-start | bytes 663560 | tf_op jit(solution)/shard_map/ppermute | solution.py:38
  635.1 9.9 %collective-permute-start.50 = (bf16[192,1536]{1,0:T(8,128)(2,1)S(1)}, bf16[192,1536]{1,0:T(8,128)(2,1)S(1)}, u32[]{:S(2)}, u32[]{:S(2)}) collective-permute-start(bf16[192,1536]{1,0:T(8,128)(2,1)S(1)} %fusion.212), channel_id=1, source_target_pairs={{0,1},{1,0},{2,3},{3,2},{4,5},{5,4},{6,7},{7,6},{8,9},{9,8},{10,11... | collective-permute-start | bytes 1769480 | tf_op jit(solution)/shard_map/ppermute | solution.py:18
  638.4 9.9 %collective-permute-start.47 = (bf16[192,1536]{1,0:T(8,128)(2,1)S(1)}, bf16[192,1536]{1,0:T(8,128)(2,1)S(1)}, u32[]{:S(2)}, u32[]{:S(2)}) collective-permute-start(bf16[192,1536]{1,0:T(8,128)(2,1)S(1)} %slice.1435), channel_id=1, source_target_pairs={{0,4},{2,6},{4,0},{6,2},{8,12},{10,14},{12,8},{14,10},{16,20},{18,... | collective-permute-start | bytes 1769480 | tf_op jit(solution)/shard_map/ppermute | solution.py:23
  640.6 9.2 %collective-permute-start.61 = (bf16[48,2304]{1,0:T(8,128)(2,1)S(1)}, bf16[48,2304]{1,0:T(8,128)(2,1)S(1)}, u32[]{:S(2)}, u32[]{:S(2)}) collective-permute-start(bf16[48,2304]{1,0:T(8,128)(2,1)S(1)} %fusion.232), channel_id=1, source_target_pairs={{0,8},{2,10},{4,12},{6,14},{16,0},{18,2},{20,4},{22,6},{24,16},{26... | collective-permute-start | bytes 663560 | tf_op jit(solution)/shard_map/ppermute | solution.py:38
  648.6 10.5 %collective-permute-start.51 = (bf16[48,3072]{1,0:T(8,128)(2,1)S(1)}, bf16[48,3072]{1,0:T(8,128)(2,1)S(1)}, u32[]{:S(2)}, u32[]{:S(2)}) collective-permute-start(bf16[48,3072]{1,0:T(8,128)(2,1)S(1)} %fusion.221), channel_id=1, source_target_pairs={{0,8},{2,10},{4,12},{6,14},{16,0},{18,2},{20,4},{22,6},{24,16},{26... | collective-permute-start | bytes 884744 | tf_op jit(solution)/shard_map/ppermute | solution.py:38
  649.9 11.9 %collective-permute-start.62 = (bf16[48,2304]{1,0:T(8,128)(2,1)S(1)}, bf16[48,2304]{1,0:T(8,128)(2,1)S(1)}, u32[]{:S(2)}, u32[]{:S(2)}) collective-permute-start(bf16[48,2304]{1,0:T(8,128)(2,1)S(1)} %fusion.237), channel_id=1, source_target_pairs={{0,8},{2,10},{4,12},{6,14},{16,0},{18,2},{20,4},{22,6},{24,16},{26... | collective-permute-start | bytes 663560 | tf_op jit(solution)/shard_map/ppermute | solution.py:38
  659.1 10.7 %collective-permute-start.52 = (bf16[48,3072]{1,0:T(8,128)(2,1)S(1)}, bf16[48,3072]{1,0:T(8,128)(2,1)S(1)}, u32[]{:S(2)}, u32[]{:S(2)}) collective-permute-start(bf16[48,3072]{1,0:T(8,128)(2,1)S(1)} %fusion.215), channel_id=1, source_target_pairs={{0,8},{2,10},{4,12},{6,14},{16,0},{18,2},{20,4},{22,6},{24,16},{26... | collective-permute-start | bytes 884744 | tf_op jit(solution)/shard_map/ppermute | solution.py:38
  669.8 7.7 %collective-permute-start.53 = (bf16[48,3072]{1,0:T(8,128)(2,1)S(1)}, bf16[48,3072]{1,0:T(8,128)(2,1)S(1)}, u32[]{:S(2)}, u32[]{:S(2)}) collective-permute-start(bf16[48,3072]{1,0:T(8,128)(2,1)S(1)} %fusion.220), channel_id=1, source_target_pairs={{0,8},{2,10},{4,12},{6,14},{16,0},{18,2},{20,4},{22,6},{24,16},{26... | collective-permute-start | bytes 884744 | tf_op jit(solution)/shard_map/ppermute | solution.py:38
  (154 other events, 928.0 us)

commit v2 on v1

v2 whole, which is shorter than its diff:
```python
import functools
import math

import jax
import jax.numpy as jnp
from jax import lax
from jax.experimental import pallas as pl
from jax.experimental.pallas import tpu as pltpu
from jax.sharding import PartitionSpec as P

HEAD_DIM = 64
LOW = jnp.bfloat16
F32 = jnp.float32


def ring_of(count):
    return list(range(0, count, 2)) + list(range(1, count, 2))[::-1]


def swap_y(value):
    return lax.ppermute(value, "mp", [(0, 1), (1, 0)])


def swap_x(value):
    n = lax.axis_size("dp")
    return lax.ppermute(value, "dp", [(i, i ^ 2) for i in range(n)])


def swap_core(value):
    n = lax.axis_size("dp")
    return lax.ppermute(value, "dp", [(i, i ^ 1) for i in range(n)])


def ring_shift(value, step):
    count = lax.axis_size("dp") // 4
    ring = ring_of(count)
    pairs = []
    for place in range(count):
        for low in range(4):
            pairs.append((ring[place] * 4 + low, ring[(place + step) % count] * 4 + low))
    return lax.ppermute(value, "dp", pairs)


def feature_order(width):
    n = lax.axis_size("dp")
    count, rows = n // 4, width // n
    me = lax.axis_index("dp")
    z, x, core = me // 4, (me // 2) % 2, me % 2
    place = jnp.where(z % 2 == 0, z // 2, count - 1 - z // 2)
    at = lax.iota(jnp.int32, width)
    row = at % rows
    back = (at // rows) % count
    x_rel = (at // (rows * count)) % 2
    core_rel = at // (rows * count * 2)
    from_place = (place - back + count) % count
    half = (count + 1) // 2
    z_abs = jnp.where(from_place < half, 2 * from_place, 2 * (count - 1 - from_place) + 1)
    block = z_abs * 4 + (x ^ x_rel) * 2 + (core ^ core_rel)
    return block * rows + row


def after(value, *others):
    return lax.optimization_barrier((value, others))[0]


VMEM_BYTES = 48 << 20
TILE = 256


def dot(left, right, left_at, right_at):
    return lax.dot_general(
        left, right, (((left_at,), (right_at,)), ((), ())), preferred_element_type=F32
    )


def call(body, steps, inputs, outputs, scratch, flops, exps=0):
    size = lambda shape, dtype: math.prod(shape) * jnp.dtype(dtype).itemsize
    moved = sum(size(array.shape, array.dtype) for array, _, _ in inputs)
    moved += sum(size(shape, dtype) for shape, dtype, _, _ in outputs)
    return pl.pallas_call(
        body,
        grid=(steps,),
        in_specs=[pl.BlockSpec(block, index) for _, block, index in inputs],
        out_specs=[pl.BlockSpec(block, index) for _, _, block, index in outputs],
        out_shape=[jax.ShapeDtypeStruct(shape, dtype) for shape, dtype, _, _ in outputs],
        scratch_shapes=scratch,
        compiler_params=pltpu.CompilerParams(
            dimension_semantics=("arbitrary",), vmem_limit_bytes=VMEM_BYTES
        ),
        cost_estimate=pl.CostEstimate(
            flops=flops, bytes_accessed=moved, transcendentals=exps
        ),
    )(*[array for array, _, _ in inputs])


def whole(array):
    rank = array.ndim
    return (array, array.shape, lambda i: (0,) * rank)


def per_group(array, at=lambda i: i):
    return (array, (1,) + array.shape[1:], lambda i: (at(i),) + (0,) * (array.ndim - 1))


def out_whole(shape, dtype):
    return (shape, dtype, shape, lambda i: (0,) * len(shape))


def out_group(shape, dtype, at=lambda i: i):
    return (shape, dtype, (1,) + shape[1:], lambda i: (at(i),) + (0,) * (len(shape) - 1))


class Layer:
    def __init__(self, every, width, up, down, qkv, out, out_from, norms, bias_qkv, bias_up):
        self.every = every
        self.width, self.up_at, self.down_at = width, up, down
        self.qkv_blocks, self.out_block, self.out_from = qkv, out, out_from
        self.norms, self.bias_qkv, self.bias_up = norms, bias_qkv, bias_up

    def columns(self, block, at):
        size, place = block
        depth = self.every.shape[1]
        return (self.every, (1, depth, size), lambda i: (at(i), 0, place))

    def qkv(self, at=lambda i: i):
        return [self.columns(block, at) for block in self.qkv_blocks]

    def out(self, at=lambda i: i):
        return self.columns(self.out_block, at)

    def ffn(self, base, first):
        size, per = self.bias_up.shape[2], self.bias_up.shape[0] // 2
        depth = self.every.shape[1]

        def index(i):
            step = jnp.maximum(i - first, 0)
            return (step // per, 0, base + step % per)

        return (self.every, (1, depth, size), index)


def put_projection(rows, weights, bias, target):
    start = 0
    wide = target.shape[1]
    for weight in weights:
        cols = min(weight.shape[2], wide - start)
        part = dot(rows, weight[0, :, :cols], 1, 0) + bias[0, :, start : start + cols]
        target[:, start : start + cols] = part.astype(LOW)
        start += cols


def through_projection(grads, weights):
    start = 0
    total = None
    for weight in weights:
        cols = min(weight.shape[2], grads.shape[1] - start)
        part = dot(grads[:, start : start + cols], weight[0, :, :cols], 1, 1)
        total = part if total is None else total + part
        start += cols
    return total


def head_at(width, part, head):
    return slice(part * width + head * HEAD_DIM, part * width + (head + 1) * HEAD_DIM)


def join(parts, cols):
    picked = [part[:, cols] for part in parts]
    return picked[0] if len(picked) == 1 else jnp.concatenate(picked, axis=0)


def attend(width, kept, mask, logsum):
    scale = jnp.asarray(HEAD_DIM**-0.5, LOW)
    out = []
    for head in range(width // HEAD_DIM):
        query = kept[0][:, head_at(width, 0, head)] * scale
        scores = dot(join(kept, head_at(width, 1, head)), query, 1, 1) + mask[...]
        top = jnp.max(scores, axis=0, keepdims=True)
        expo = jnp.exp(scores - top)
        total = jnp.sum(expo, axis=0, keepdims=True)
        out.append(dot(join(kept, head_at(width, 2, head)), expo.astype(LOW), 0, 0) * (1.0 / total))
        logsum[head : head + 1, :] = top + jnp.log(total)
    return jnp.concatenate(out, axis=0).T.astype(LOW)


def attend_back(width, kept, mask, logsum, d_context, grads, sums):
    scale = jnp.asarray(HEAD_DIM**-0.5, LOW)
    for head in range(width // HEAD_DIM):
        at_q, at_k, at_v = (head_at(width, part, head) for part in range(3))
        query = kept[0][:, at_q] * scale
        keys = join(kept, at_k)
        d_ctx = d_context[:, head * HEAD_DIM : (head + 1) * HEAD_DIM]
        probs = jnp.exp(dot(keys, query, 1, 1) + mask[...] - logsum[head : head + 1, :])
        d_probs = dot(join(kept, at_v), d_ctx, 1, 1)
        both = probs * d_probs
        inner = jnp.sum(both, axis=0, keepdims=True)
        d_scores = (both - probs * inner).astype(LOW)
        d_values = dot(probs.astype(LOW), d_ctx, 1, 0).astype(LOW)
        d_keys = dot(d_scores, query, 1, 0).astype(LOW)
        d_query = dot(keys * scale, d_scores, 0, 0).T.astype(LOW)
        grads[0][:, at_q] = d_query
        start = 0
        for grad in grads:
            rows = grad.shape[0]
            grad[:, at_k] = d_keys[start : start + rows]
            grad[:, at_v] = d_values[start : start + rows]
            start += rows
        for grad in grads[1:]:
            grad[:, at_q] = jnp.zeros((grad.shape[0], HEAD_DIM), LOW)
        sums[0:1, at_q] = jnp.sum(d_query.astype(F32), axis=0, keepdims=True)
        sums[0:1, at_k] = jnp.zeros((1, HEAD_DIM), F32)
        sums[0:1, at_v] = jnp.sum(d_values.astype(F32), axis=0, keepdims=True)


def make_mask(segs_q, segs_k, mask):
    @pl.when(pl.program_id(0) == 0)
    def _():
        mask[...] = jnp.where(segs_k[...] == segs_q[...], 0.0, -1e9)


def normalize(value, gain, shift):
    center = value - jnp.mean(value, axis=-1, keepdims=True)
    recip = lax.rsqrt(jnp.mean(center * center, axis=-1, keepdims=True) + 1e-06)
    normed = center * recip
    return normed * gain + shift, normed, recip


def normalize_back(grad, normed, recip, gain):
    scaled = grad * gain
    mean_one = jnp.mean(scaled, axis=-1, keepdims=True)
    mean_two = jnp.mean(scaled * normed, axis=-1, keepdims=True)
    return recip * (scaled - mean_one - normed * mean_two)


def row_tiles(rows):
    return [slice(start, start + TILE) for start in range(0, rows, TILE)]


def project_call(layer, rows_low, segs, half):
    n, depth = rows_low.shape
    width, wide, own = layer.width, 3 * layer.width, 2 * half
    count = len(layer.qkv_blocks)

    def body(rows, *refs):
        weights = refs[:count]
        bias, segs_q, segs_k, proj, context, logsum, mask = refs[count:]
        make_mask(segs_q, segs_k, mask)
        put_projection(rows[...], weights, bias, proj.at[0])
        context[0] = attend(width, [proj.at[0, :own]], mask, logsum.at[0])

    return call(
        body, 2,
        [whole(rows_low)] + layer.qkv() + [
            per_group(layer.bias_qkv), whole(segs[None, :]), whole(segs[:, None])
        ],
        [
            out_group((2, n, wide), LOW), out_group((2, own, width), LOW), out_group((2, 8, own), F32),
        ],
        [pltpu.VMEM((own, own), F32)],
        flops=4 * n * depth * wide + 8 * own * own * width,
        exps=2 * own * own * width // HEAD_DIM,
    )


def rest_call(layer, rows, proj, away_low, context_own, segs, half):
    n, depth = rows.shape
    width, wide, own = layer.width, 3 * layer.width, 2 * half
    count = len(layer.qkv_blocks)
    steps, _, size = layer.bias_up.shape
    per = steps // 2
    group = lambda i: jnp.minimum(i, 1)
    block = lambda i: jnp.maximum(i - 2, 0)

    def body(rows, proj, away, *refs):
        weights = refs[:count]
        (
            out_w, bias, segs_q, segs_k, context_own, norms, up, bias_up, down,
            proj_away, context, logsum, hidden_low, normed_one, recip_one, act, slope,
            output, output_low, normed_two, recip_two,
            mask, hidden, total,
        ) = refs[count:]
        i = pl.program_id(0)
        make_mask(segs_q, segs_k, mask)
        gain = lambda at: norms[at : at + 1, :]

        @pl.when(i < 2)
        def _():
            put_projection(away[...], weights, bias, proj_away.at[0])
            context[0, :own] = context_own[0]
            context[0, own:] = attend(width, [proj.at[0], proj_away.at[0]], mask, logsum.at[0])
            out_cols = out_w[0, :, layer.out_from : layer.out_from + width]
            part = dot(context[0], out_cols, 1, 1)

            @pl.when(i == 0)
            def _():
                total[...] = part

            @pl.when(i == 1)
            def _():
                total[...] += part
                for at in row_tiles(n):
                    value = rows[at, :].astype(F32) + total[at, :] + gain(2)
                    value, normed, recip = normalize(value, gain(0), gain(3))
                    hidden[at, :] = value
                    hidden_low[at, :] = value.astype(LOW)
                    normed_one[at, :] = normed.astype(LOW)
                    recip_one[at, :] = recip

        @pl.when(i >= 2)
        def _():
            for at in row_tiles(n):
                pre = dot(hidden_low[at, :], up[0], 1, 0) + bias_up[0]
                bell = 0.5 + 0.5 * lax.erf(pre * math.sqrt(0.5))
                low = (pre * bell).astype(LOW)
                act[0, at, :] = low
                slope[0, at, :] = (
                    bell + pre * (jnp.exp(-0.5 * pre * pre) * (1.0 / math.sqrt(2.0 * math.pi)))
                ).astype(LOW)
                part = dot(low, down[0], 1, 1)

                @pl.when(i == 2)
                def _():
                    total[at, :] = part

                @pl.when(i > 2)
                def _():
                    total[at, :] += part

        @pl.when(i == steps + 1)
        def _():
            for at in row_tiles(n):
                value = hidden[at, :] + total[at, :] + gain(4)
                value, normed, recip = normalize(value, gain(1), gain(5))
                output[at, :] = value
                output_low[at, :] = value.astype(LOW)
                normed_two[at, :] = normed.astype(LOW)
                recip_two[at, :] = recip

    neurons = per * size
    ffn_out = ((2, n, neurons), LOW, (1, n, size), lambda i: (block(i) // per, 0, block(i) % per))
    return call(
        body, steps + 2,
        [
            whole(rows), (proj, (1, half, wide), lambda i: (group(i), 2, 0)), whole(away_low),
        ] + layer.qkv(group) + [
            layer.out(group), per_group(layer.bias_qkv, group), whole(segs[None, :half]),
            whole(segs[:, None]), per_group(context_own, group), whole(layer.norms),
            layer.ffn(layer.up_at, 2), per_group(layer.bias_up, block), layer.ffn(layer.down_at, 2),
        ],
        [
            out_group((2, half, wide), LOW, group), out_group((2, n, width), LOW, group),
            out_group((2, 8, half), F32, group), out_whole((n, depth), LOW), out_whole((n, depth), LOW),
            out_whole((n, 1), F32), ffn_out, ffn_out, out_whole((n, depth), F32), out_whole((n, depth), LOW),
            out_whole((n, depth), LOW), out_whole((n, 1), F32),
        ],
        [pltpu.VMEM((own, half), F32), pltpu.VMEM((n, depth), F32), pltpu.VMEM((n, depth), F32)],
        flops=4 * depth * (n * width + half * wide + 2 * n * neurons) + 8 * own * half * width,
        exps=2 * own * half * width // HEAD_DIM + 4 * n * neurons,
    )


def add_rows(sums, row, value, at):
    value = jnp.sum(value, axis=0, keepdims=True)
    if at.start == 0:
        sums[row : row + 1, :] = value
    else:
        sums[row : row + 1, :] += value


def ffn_back_call(layer, grad, extra, kept, half):
    n, depth = grad.shape
    steps, _, size = layer.bias_up.shape
    per = steps // 2
    has_extra = extra is not None

    def body(grad, *refs):
        extra = refs[0] if has_extra else None
        (
            normed_one, recip_one, normed_two, recip_two, norms, slope, up, down,
            d_final_low, d_pre, d_mid, d_mid_low, sums, bias_sums, d_final, total,
        ) = refs[1:] if has_extra else refs
        i = pl.program_id(0)
        gain = lambda at: norms[at : at + 1, :]

        @pl.when(i == 0)
        def _():
            sums[...] = jnp.zeros_like(sums)
            for at in row_tiles(n):
                value = grad[at, :].astype(F32)
                if has_extra and at.start >= 2 * half:
                    value = value + extra[at.start - 2 * half : at.stop - 2 * half, :].astype(F32)
                normed = normed_two[at, :].astype(F32)
                back = normalize_back(value, normed, recip_two[at, :], gain(1))
                d_final[at, :] = back
                d_final_low[at, :] = back.astype(LOW)
                add_rows(sums, 1, value * normed, at)
                add_rows(sums, 5, value, at)
                add_rows(sums, 4, back, at)

        bias = None
        for at in row_tiles(n):
            d_act = dot(d_final_low[at, :], down[0], 1, 0)
            low = (d_act * slope[0, at, :].astype(F32)).astype(LOW)
            d_pre[0, at, :] = low
            one = jnp.sum(low.astype(F32), axis=0, keepdims=True)
            bias = one if bias is None else bias + one
            part = dot(low, up[0], 1, 1)

            @pl.when(i == 0)
            def _():
                total[at, :] = part

            @pl.when(i > 0)
            def _():
                total[at, :] += part

        bias_sums[0] = bias

        @pl.when(i == steps - 1)
        def _():
            for at in row_tiles(n):
                value = d_final[at, :] + total[at, :]
                normed = normed_one[at, :].astype(F32)
                back = normalize_back(value, normed, recip_one[at, :], gain(0))
                d_mid[at, :] = back
                d_mid_low[at, :] = back.astype(LOW)
                add_rows(sums, 0, value * normed, at)
                add_rows(sums, 3, value, at)
                add_rows(sums, 2, back, at)

    neurons = per * size
    blocks = ((1, n, size), lambda i: (i // per, 0, i % per))
    return call(
        body, steps,
        [whole(grad)] + ([whole(extra)] if has_extra else []) + [
            whole(kept["normed_one"]), whole(kept["recip_one"]), whole(kept["normed_two"]),
            whole(kept["recip_two"]), whole(layer.norms), (kept["slope"],) + blocks,
            layer.ffn(layer.up_at, 0), layer.ffn(layer.down_at, 0),
        ],
        [
            out_whole((n, depth), LOW), ((2, n, neurons), LOW) + blocks, out_whole((n, depth), F32),
            out_whole((n, depth), LOW), out_whole((8, depth), F32), out_group((steps, 1, size), F32),
        ],
        [pltpu.VMEM((n, depth), F32), pltpu.VMEM((n, depth), F32)],
        flops=8 * n * depth * neurons,
    )


def ffn_back_first_call(layer, grad, extra, kept, half):
    n, depth = grad.shape
    steps, _, size = layer.bias_up.shape
    per = steps // 2

    def body(
        grad, extra, normed_two, recip_two, norms, slope, down,
        d_final, d_final_low, d_pre, sums, bias_sums,
    ):
        i = pl.program_id(0)

        @pl.when(i == 0)
        def _():
            sums[...] = jnp.zeros_like(sums)
            for at in row_tiles(n):
                value = grad[at, :]
                if at.start >= 2 * half:
                    value = value + extra[at.start - 2 * half : at.stop - 2 * half, :].astype(F32)
                normed = normed_two[at, :].astype(F32)
                back = normalize_back(value, normed, recip_two[at, :], norms[1:2, :])
                d_final[at, :] = back
                d_final_low[at, :] = back.astype(LOW)
                add_rows(sums, 1, value * normed, at)
                add_rows(sums, 5, value, at)
                add_rows(sums, 4, back, at)

        bias = None
        for at in row_tiles(n):
            d_act = dot(d_final_low[at, :], down[0], 1, 0)
            low = (d_act * slope[0, at, :].astype(F32)).astype(LOW)
            d_pre[0, at, :] = low
            one = jnp.sum(low.astype(F32), axis=0, keepdims=True)
            bias = one if bias is None else bias + one
        bias_sums[0] = bias

    neurons = per * size
    blocks = ((1, n, size), lambda i: (i // per, 0, i % per))
    return call(
        body, steps,
        [
            whole(grad), whole(extra), whole(kept["normed_two"]), whole(kept["recip_two"]),
            whole(layer.norms), (kept["slope"],) + blocks, layer.ffn(layer.down_at, 0),
        ],
        [
            out_whole((n, depth), F32), out_whole((n, depth), LOW), ((2, n, neurons), LOW) + blocks,
            out_whole((8, depth), F32), out_group((steps, 1, size), F32),
        ],
        [],
        flops=4 * n * depth * neurons,
    )


def ffn_back_second_call(layer, d_final, d_pre, kept):
    n, depth = d_final.shape
    steps, _, size = layer.bias_up.shape
    per = steps // 2

    def body(d_final, d_pre, normed_one, recip_one, norms, up, d_mid, d_mid_low, sums):
        i = pl.program_id(0)
        for at in row_tiles(n):
            part = dot(d_pre[0, at, :], up[0], 1, 1)

            @pl.when(i == 0)
            def _():
                d_mid[at, :] = d_final[at, :] + part

            @pl.when(i > 0)
            def _():
                d_mid[at, :] += part

        @pl.when(i == steps - 1)
        def _():
            sums[...] = jnp.zeros_like(sums)
            for at in row_tiles(n):
                value = d_mid[at, :]
                normed = normed_one[at, :].astype(F32)
                back = normalize_back(value, normed, recip_one[at, :], norms[0:1, :])
                d_mid[at, :] = back
                d_mid_low[at, :] = back.astype(LOW)
                add_rows(sums, 0, value * normed, at)
                add_rows(sums, 3, value, at)
                add_rows(sums, 2, back, at)

    blocks = ((1, n, size), lambda i: (i // per, 0, i % per))
    return call(
        body, steps,
        [
            whole(d_final), (d_pre,) + blocks, whole(kept["normed_one"]), whole(kept["recip_one"]),
            whole(layer.norms), layer.ffn(layer.up_at, 0),
        ],
        [out_whole((n, depth), F32), out_whole((n, depth), LOW), out_whole((8, depth), F32)],
        [],
        flops=4 * n * depth * per * size,
    )


def shared_back_call(layer, d_mid_low, kept, segs, half):
    n, depth = d_mid_low.shape
    width, wide, own = layer.width, 3 * layer.width, 2 * half
    count = len(layer.qkv_blocks)

    def body(d_mid, proj, away, logsum, *refs):
        weights = refs[:count]
        out_w, segs_q, segs_k, d_proj, d_away, sums, back, mask, total = refs[count:]
        i = pl.program_id(0)
        make_mask(segs_q, segs_k, mask)
        out_cols = out_w[0, :, layer.out_from : layer.out_from + width]
        d_context = dot(d_mid[...], out_cols, 1, 0).astype(LOW)
        attend_back(
            width, [proj.at[0], away.at[0]], mask, logsum.at[0], d_context,
            [d_proj.at[0], d_away.at[0]], sums.at[0],
        )
        part = through_projection(d_away[0], weights)

        @pl.when(i == 0)
        def _():
            total[...] = part

        @pl.when(i == 1)
        def _():
            back[...] = (total[...] + part).astype(LOW)

    return call(
        body, 2,
        [
            (d_mid_low, (half, depth), lambda i: (2, 0)), (kept["proj"], (1, half, wide), lambda i: (i, 2, 0)),
            per_group(kept["proj_away"]), per_group(kept["logsum_shared"]),
        ] + layer.qkv() + [layer.out(), whole(segs[None, :half]), whole(segs[:, None])],
        [
            out_group((2, half, wide), LOW), out_group((2, half, wide), LOW), out_group((2, 8, wide), F32),
            out_whole((half, depth), LOW),
        ],
        [pltpu.VMEM((own, half), F32), pltpu.VMEM((half, depth), F32)],
        flops=4 * half * depth * (wide + width) + 20 * own * half * width,
        exps=2 * own * half * width // HEAD_DIM,
    )


def own_back_call(layer, d_mid, d_mid_low, d_shared, kept, segs, half):
    n, depth = d_mid_low.shape
    width, wide, own = layer.width, 3 * layer.width, 2 * half
    count = len(layer.qkv_blocks)

    def body(d_mid, d_mid_low, d_shared, proj, logsum, *refs):
        weights = refs[:count]
        out_w, segs_q, segs_k, d_proj, sums, d_rows, mask = refs[count:]
        i = pl.program_id(0)
        make_mask(segs_q, segs_k, mask)
        out_cols = out_w[0, :, layer.out_from : layer.out_from + width]
        d_context = dot(d_mid_low[...], out_cols, 1, 0).astype(LOW)
        attend_back(
            width, [proj.at[0]], mask, logsum.at[0], d_context, [d_proj.at[0, :own]], sums.at[0]
        )
        d_proj[0, own:] = d_shared[0]
        part = through_projection(d_proj[0], weights)

        @pl.when(i == 0)
        def _():
            d_rows[...] = d_mid[...] + part

        @pl.when(i == 1)
        def _():
            d_rows[...] += part

    return call(
        body, 2,
        [
            whole(d_mid), (d_mid_low, (own, depth), lambda i: (0, 0)), per_group(d_shared),
            (kept["proj"], (1, own, wide), lambda i: (i, 0, 0)), per_group(kept["logsum_own"]),
        ] + layer.qkv() + [layer.out(), whole(segs[None, :]), whole(segs[:, None])],
        [
            out_group((2, n, wide), LOW), out_group((2, 8, wide), F32), out_whole((n, depth), F32),
        ],
        [pltpu.VMEM((own, own), F32)],
        flops=4 * depth * (n * wide + own * width) + 20 * own * own * width,
        exps=2 * own * own * width // HEAD_DIM,
    )


class Grads:
    def __init__(self, entries, columns, cut):
        self.entries, self.columns, self.cut = entries, columns, cut
        sizes = [end - start for _, start, end in columns]
        self.size_a, self.size_b = sum(sizes[:cut]), sum(sizes[cut:])

    def inputs(self, at):
        out = []
        for pairs in self.entries:
            for left, right in pairs:
                out += [whole(left), per_group(right, at)]
        return out

    def scratch(self, rows):
        return [pltpu.VMEM((rows, left.shape[0]), LOW) for pairs in self.entries for left, _ in pairs]

    def flops(self, rows):
        depth = self.entries[0][0][0].shape[1]
        return sum(
            2 * rows * left.shape[0] * (2 * right.shape[2] + depth)
            for pairs in self.entries for left, right in pairs
        )

    def turn(self, pick, refs, turned):
        @pl.when(pl.program_id(0) == 0)
        def _():
            for at in range(len(turned)):
                turned[at][...] = dot(pick[...], refs[2 * at][...], 1, 1).astype(LOW)

    def product(self, refs, turned, entry, start, end):
        first = sum(len(pairs) for pairs in self.entries[:entry])
        total = None
        for at in range(first, first + len(self.entries[entry])):
            one = dot(turned[at][...], refs[2 * at + 1][0, :, start:end], 1, 0)
            total = one if total is None else total + one
        return total

    def send(self, pick):
        rows = pick.shape[0]
        size = self.size_a + self.size_b

        def body(pick, *refs):
            count = 2 * sum(len(pairs) for pairs in self.entries)
            out, turned = refs[count], refs[count + 1 :]
            self.turn(pick, refs, turned)
            col = 0
            for entry, start, end in self.columns:
                part = self.product(refs, turned, entry, start, end)
                out[0, :, col : col + end - start] = part.astype(LOW)
                col += end - start

        return call(
            body, 2, [whole(pick)] + self.inputs(lambda i: i), [out_group((2, rows, size), LOW)],
            self.scratch(rows), self.flops(rows),
        )[0]

    def keep(self, pick, got, group):
        rows = pick.shape[0]
        half = rows // 2
        size = self.size_a + self.size_b
        order = jnp.stack([1 - group, group]).astype(jnp.int32)

        def body(order, pick, got, *refs):
            count = 2 * sum(len(pairs) for pairs in self.entries)
            send_a, keep_a, send_b, keep_b = refs[count : count + 4]
            turned = refs[count + 4 :]
            i = pl.program_id(0)
            self.turn(pick, refs, turned)
            col = 0
            for at, (entry, start, end) in enumerate(self.columns):
                part = self.product(refs, turned, entry, start, end)
                part = part + got[0, :, col : col + end - start].astype(F32)
                if at < self.cut:
                    place = slice(col, col + end - start)

                    @pl.when(i == 0)
                    def _():
                        send_a[:, place] = part.astype(LOW)

                    @pl.when(i == 1)
                    def _():
                        keep_a[:, place] = part
                else:
                    place = slice(col - self.size_a, col - self.size_a + end - start)
                    keep_b[0, :, place] = part[:half]
                    send_b[0, :, place] = part[half:].astype(LOW)
                col += end - start

        inputs = [whole(pick), per_group(got, None)] + self.inputs(None)
        specs = []
        for array, block, index in inputs:
            rank = array.ndim
            if rank == 3:
                specs.append(pl.BlockSpec(block, lambda i, order: (order[i], 0, 0)))
            else:
                specs.append(pl.BlockSpec(block, lambda i, order: (0, 0)))
        flat = lambda shape: pl.BlockSpec(shape, lambda i, order: (0, 0))
        each = lambda shape: pl.BlockSpec((1,) + shape, lambda i, order: (i, 0, 0))
        return pl.pallas_call(
            body,
            grid_spec=pltpu.PrefetchScalarGridSpec(
                num_scalar_prefetch=1,
                grid=(2,),
                in_specs=specs,
                out_specs=[
                    flat((rows, self.size_a)), flat((rows, self.size_a)),
                    each((half, self.size_b)), each((half, self.size_b)),
                ],
                scratch_shapes=self.scratch(rows),
            ),
            out_shape=[
                jax.ShapeDtypeStruct((rows, self.size_a), LOW), jax.ShapeDtypeStruct((rows, self.size_a), F32),
                jax.ShapeDtypeStruct((2, half, self.size_b), LOW),
                jax.ShapeDtypeStruct((2, half, self.size_b), F32),
            ],
            compiler_params=pltpu.CompilerParams(
                dimension_semantics=("arbitrary",), vmem_limit_bytes=VMEM_BYTES
            ),
            cost_estimate=pl.CostEstimate(
                flops=self.flops(rows), bytes_accessed=10 * rows * size, transcendentals=0
            ),
        )(order, *[array for array, _, _ in inputs])


class Reduce:
    def __init__(self, grads, pick_send, pick_keep):
        self.grads, self.pick_keep = grads, pick_keep
        self.sends = (grads.send(pick_send),)
        self.got = (swap_core(self.sends[0]),)
        self.work = self._run()

    def _run(self):
        count = lax.axis_size("dp") // 4
        send_a, keep_a, send_b, keep_b = self.grads.keep(self.pick_keep, self.got[0], lax.axis_index("mp"))
        fourth = keep_a.shape[0] // 2
        self.sends = (send_a, send_b)
        self.got = (swap_y(send_a), swap_x(send_b))
        yield
        a = keep_a + self.got[0].astype(F32)
        b = keep_b + self.got[1].astype(F32)
        self.sends = (a[fourth:].astype(LOW), b[0].astype(LOW))
        self.got = (swap_x(self.sends[0]), swap_y(self.sends[1]))
        a, b = a[:fourth], b[1]
        yield
        both = jnp.concatenate([a + self.got[0].astype(F32), b + self.got[1].astype(F32)], axis=1)
        both = both.reshape((count, -1) + both.shape[1:])
        total = both[count - 1]
        for back in range(count - 2, -1, -1):
            self.sends = (total.astype(LOW),)
            self.got = (ring_shift(self.sends[0], -1),)
            yield
            total = both[back] + self.got[0].astype(F32)
        self.total = total
        self.got = self.sends = ()

    def step(self):
        next(self.work, None)


class Total:
    def __init__(self, value):
        self.total = value
        self.work = self._run()
        self.step()

    def _run(self):
        n = lax.axis_size("dp")
        self.sends = (self.total,)
        self.got = (swap_y(self.total),)
        yield
        self.total = self.total + self.got[0]
        step = 1
        while step < n:
            self.sends = (self.total,)
            self.got = (lax.ppermute(self.total, "dp", [(i, i ^ step) for i in range(n)]),)
            yield
            self.total = self.total + self.got[0]
            step *= 2
        self.got = self.sends = ()

    def step(self):
        next(self.work, None)


def round_of(*works):
    ended = lax.optimization_barrier(tuple(work.got for work in works))
    for work, got in zip(works, ended):
        work.got = got
    for work in works:
        work.step()


def before(value, *works):
    value, ended = lax.optimization_barrier((value, tuple(work.got for work in works)))
    for work, got in zip(works, ended):
        work.got = got
    return value


def forward_layer(layer, rows, rows_low, away_low, segs, half):
    proj, context_own, logsum_own = project_call(layer, rows_low, segs[0], half)
    away_low = away_low()
    (
        proj_away, context, logsum_shared, hidden_low, normed_one, recip_one, act, slope, output,
        output_low, normed_two, recip_two,
    ) = rest_call(layer, rows, proj, away_low, context_own, segs[1], half)
    kept = dict(
        rows_low=rows_low, away_low=away_low, proj=proj, proj_away=proj_away, context=context,
        logsum_own=logsum_own, logsum_shared=logsum_shared, hidden_low=hidden_low,
        normed_one=normed_one, recip_one=recip_one, act=act, slope=slope, normed_two=normed_two,
        recip_two=recip_two,
    )
    return output, output_low, kept


def backward_ffn(layer, grad, extra, kept, half):
    d_final_low, d_pre, d_mid, d_mid_low, sums, bias_sums = ffn_back_call(layer, grad, extra, kept, half)
    per = bias_sums.shape[0] // 2
    entries = [[(kept["hidden_low"], d_pre)], [(d_final_low, kept["act"])]]
    return d_mid, d_mid_low, sums[:6], bias_sums.reshape(2, per * bias_sums.shape[2]), entries


def attn_entries(kept, d_proj, d_away, d_mid_low):
    return [[(kept["rows_low"], d_proj), (kept["away_low"], d_away)], [(d_mid_low, kept["context"])]]


def on_device(
    tokens, segment_ids, out_grad,
    t_qkv, t_qv_bias, t_out, t_up, t_up_bias, t_down, t_gains, t_shifts,
    s_qkv, s_qv_bias, s_out, s_up, s_up_bias, s_down, s_gains, s_shifts,
):
    rows, half, width = tokens.shape
    group = lax.axis_index("mp")
    first = group == 0
    own_row = lambda value: jnp.where(first, value[0], value[2])
    far_row = lambda value: jnp.where(first, value[2], value[0])

    norm_rows = jnp.concatenate([t_gains, t_shifts, s_gains, s_shifts], axis=0).T
    norm_rows = jnp.pad(norm_rows, ((0, 0), (0, 128 - norm_rows.shape[1])))
    t_width, s_width = t_qkv.shape[2], s_qkv.shape[2]
    weight_parts = [
        t_up, t_down.T, t_qkv[0], t_qkv[1], t_qkv[2], t_out.T,
        s_up, s_down.T, s_qkv[0], s_qkv[1], s_qkv[2], s_out.T, norm_rows,
    ]
    every = lax.all_gather(jnp.concatenate(weight_parts, axis=1), ("mp", "dp"), axis=0, tiled=True)
    every = every.reshape(2, width, -1)
    norms = every[0, :, -128:-116].T.astype(F32)
    norms_of = lambda at: jnp.pad(norms[at : at + 6], ((0, 2), (0, 0)))

    bias_parts = [t_qv_bias[0], t_qv_bias[1], t_up_bias, s_qv_bias[0], s_qv_bias[1], s_up_bias]
    bias_own = jnp.concatenate(bias_parts)
    bias_far = swap_y(bias_own)
    bias_all = jnp.where(first, jnp.stack([bias_own, bias_far]), jnp.stack([bias_far, bias_own])).astype(F32)
    cuts = [0]
    for part in bias_parts:
        cuts.append(cuts[-1] + part.shape[0])
    pick = [bias_all[:, cuts[i] : cuts[i + 1]] for i in range(6)]
    bias_qkv = lambda q, v: jnp.concatenate([q, jnp.zeros_like(q), v], axis=1)[:, None, :]

    size = s_up.shape[1]
    per = t_up.shape[1] // size
    t_end = t_up.shape[1] + t_down.shape[0] + 4 * t_width
    t_ffn = t_up.shape[1] + t_down.shape[0]
    s_ffn = t_end + s_up.shape[1] + s_down.shape[0]
    teacher = Layer(
        every, t_width, 0, per, [(t_width, t_ffn // t_width + i) for i in range(3)],
        (t_width, t_ffn // t_width + 3), 0, norms_of(0), bias_qkv(pick[0], pick[1]),
        pick[2].reshape(2 * per, 1, size),
    )
    student = Layer(
        every, s_width, t_end // size, t_end // size + 1, [(4 * s_width, s_ffn // (4 * s_width))],
        (4 * s_width, s_ffn // (4 * s_width)), 3 * s_width, norms_of(6), bias_qkv(pick[3], pick[4]),
        pick[5].reshape(2, 1, size),
    )

    to_own = feature_order(width)
    pick_all = (lax.iota(jnp.int32, width)[None, :] == to_own[:, None]).astype(LOW)
    pick_keep, pick_send = pick_all[: width // 2], pick_all[width // 2 :]

    got = swap_y(jnp.stack([far_row(tokens), tokens[1]]))
    inputs = jnp.concatenate([own_row(tokens), got[0], tokens[1]], axis=0)
    grad_in = jnp.concatenate([own_row(out_grad), swap_y(far_row(out_grad)), out_grad[1]], axis=0)
    spin = lambda segs: jnp.where(first, segs, jnp.roll(segs, half))
    segs = (spin(own_row(segment_ids)), spin(segment_ids[1]))

    middle, middle_low, t_kept = forward_layer(teacher, inputs, inputs, lambda: got[1], segs, half)
    last, _, s_kept = forward_layer(
        student, middle, middle_low, lambda: swap_y(middle_low[2 * half :]), segs, half
    )

    def to_rows(value):
        far = swap_y(value[half : 2 * half].astype(LOW)).astype(F32)
        near = value[:half]
        return jnp.stack([jnp.where(first, near, far), value[2 * half :], jnp.where(first, far, near)])

    output = to_rows(last)

    d_mid, d_mid_low, s_norm_grads, s_up_grad, s_entries = backward_ffn(student, grad_in, None, s_kept, half)
    d_shared, d_away, s_sums_b, back = shared_back_call(student, d_mid_low, s_kept, segs[1], half)
    extra = swap_y(back)
    d_proj, s_sums_a, d_rows = own_back_call(student, d_mid, d_mid_low, d_shared, s_kept, segs[0], half)
    d_proj, extra = lax.optimization_barrier((d_proj, extra))
    s_entries += attn_entries(s_kept, d_proj, d_away, d_mid_low)
    s_columns = [(0, 0, size), (2, 0, s_width), (3, 0, s_width), (1, 0, size), (2, s_width, 3 * s_width)]
    reduce_s = Reduce(Grads(s_entries, s_columns, 3), pick_send, pick_keep)

    d_rows = after(d_rows, reduce_s.sends)
    d_final, d_final_low, d_pre, t_sums_two, t_up_grad = ffn_back_first_call(
        teacher, d_rows, extra, t_kept, half
    )
    t_up_grad = t_up_grad.reshape(2, -1)
    d_pre = before(d_pre, reduce_s)
    reduce_s.step()
    d_pre = after(d_pre, reduce_s.sends)
    f_entries = [[(t_kept["hidden_low"], d_pre)], [(d_final_low, t_kept["act"])]]
    reduce_f = Reduce(
        Grads(f_entries, [(0, 0, per * size), (1, 0, per * size)], 1), pick_send, pick_keep
    )
    d_pre = after(d_pre, reduce_f.sends)
    d_mid, d_mid_low, t_sums_one = ffn_back_second_call(teacher, d_final, d_pre, t_kept)
    t_norm_grads = (t_sums_one + t_sums_two)[:6]
    d_mid_low = before(d_mid_low, reduce_s)
    reduce_s.step()
    d_mid_low = after(before(d_mid_low, reduce_f), reduce_s.sends)
    reduce_f.step()
    d_mid_low = after(d_mid_low, reduce_f.sends)
    d_shared, d_away, t_sums_b, back = shared_back_call(teacher, d_mid_low, t_kept, segs[1], half)
    extra = swap_y(back)
    d_shared = before(d_shared, reduce_s)
    reduce_s.step()
    d_shared = after(d_shared, reduce_s.sends)
    d_proj, t_sums_a, d_rows = own_back_call(teacher, d_mid, d_mid_low, d_shared, t_kept, segs[0], half)
    d_proj = before(d_proj, reduce_f, reduce_s)
    reduce_f.step()
    reduce_s.step()
    d_proj = after(d_proj, reduce_f.sends)
    t_entries = attn_entries(t_kept, d_proj, d_away, d_mid_low)
    reduce_t = Reduce(
        Grads(t_entries, [(0, 0, 2 * t_width), (0, 2 * t_width, 3 * t_width), (1, 0, t_width)], 1),
        pick_send, pick_keep,
    )
    d_rows = jnp.concatenate([d_rows[: 2 * half], d_rows[2 * half :] + extra.astype(F32)], axis=0)
    input_grad = to_rows(d_rows)

    def qv_grad(first, second, wide):
        sums = first[:, 0] + second[:, 0]
        return [sums[:, :wide], sums[:, 2 * wide :]]

    small = jnp.concatenate([t_norm_grads, s_norm_grads], axis=0).reshape(-1)
    bias_grads = jnp.concatenate(
        qv_grad(t_sums_a, t_sums_b, t_width) + [t_up_grad]
        + qv_grad(s_sums_a, s_sums_b, s_width) + [s_up_grad], axis=1,
    )
    small = Total(jnp.concatenate([small, bias_grads.reshape(-1)]))
    for _ in range(6):
        round_of(reduce_t, reduce_f, reduce_s, small)
    for work in (reduce_t, reduce_f, reduce_s, small):
        while work.got:
            work.step()
    s_sum, f_sum, t_sum, small = reduce_s.total, reduce_f.total, reduce_t.total, small.total

    piece = width // lax.axis_size("dp")
    norm_sum = small[: 12 * width].reshape(12, width)
    norm_sum = lax.dynamic_slice_in_dim(norm_sum, lax.axis_index("dp") * piece, piece, 1)
    bias_sum = small[12 * width :].reshape(2, -1)
    bias_sum = jnp.where(first, bias_sum[0], bias_sum[1])
    pick = [bias_sum[cuts[i] : cuts[i + 1]] for i in range(6)]

    def cut(value, *sizes):
        out = []
        for one in sizes:
            out.append(value[:, :one])
            value = value[:, one:]
        return out

    tq, tk, tv, to = cut(t_sum, t_width, t_width, t_width, t_width)
    t_up_sum, t_down_sum = cut(f_sum, per * size, per * size)
    s_up_sum, sq, so, s_down_sum, sk, sv = cut(s_sum, size, s_width, s_width, size, s_width, s_width)
    return (
        output, input_grad,
        jnp.stack([tq, tk, tv]), jnp.stack([pick[0], pick[1]]), to.T, t_up_sum, pick[2], t_down_sum.T,
        norm_sum[0:2], norm_sum[2:6],
        jnp.stack([sq, sk, sv]), jnp.stack([pick[3], pick[4]]), so.T, s_up_sum, pick[5], s_down_sum.T,
        norm_sum[6:8], norm_sum[8:12],
    )


def solution(mesh):
    layer = (
        P(None, "dp", "mp"), P(None, "mp"), P("mp", "dp"), P("dp", "mp"), P("mp"), P("mp", "dp"),
        P(None, "dp"), P(None, "dp"),
    )
    rows = P("dp", "mp", None)
    return jax.shard_map(
        on_device,
        mesh=mesh,
        in_specs=(rows, P("dp", None), rows) + layer + layer,
        out_specs=(rows, rows) + layer + layer,
        check_vma=False,
    )
```

time: 685 us -> 526 us (0.77)
  Pallas kernels: 0 us -> 218 us
  matrix products: 207 us -> 0 us
  other arithmetic: 101 us -> 26.4 us
  blocking collectives: 61.1 us -> 0 us
  local copies, waits for them, and re-layouts: 95 us -> 49.6 us
  starting transfers between devices: 52.3 us -> 37.1 us
  waiting for transfers between devices: 158 us -> 173 us
  between operations: 3.76 us -> 15.7 us
    pallas_call x0 -> x17, Pallas kernels: none -> 218 us  [the longest x14 183 us: call(): pl.pallas_call(body, grid=(steps,), in_specs=[pl.BlockSpec(block, index)...]
    dot_general x84 -> x0, matrix products: 207 us -> none  [the longest x12 31.3 us: weight_grad(): jnp.einsum('nd,ync->ydc', left[:, half:], right, preferred_element_type=F32)]
    all_gather x0 -> x1, waiting for transfers between devices: none -> 107 us  [on_device(): lax.all_gather(jnp.concatenate(weight_parts, axis=1), ('mp', 'dp'), axis=...]
    psum x1 -> x0, blocking collectives: 61.1 us -> none  [on_device(): bias_sum = lax.psum(bias_grads[0] + swap_y(bias_grads[1]), 'dp')]
    ppermute x12 -> x6, waiting for transfers between devices: 60.9 us -> 0.26 us  [swap_x(): return lax.ppermute(value, 'dp', [(i, i ^ 2) for i in range(n)])]
    ppermute x18 -> x9, waiting for transfers between devices: 67.7 us -> 10.3 us  [ring_shift(): return lax.ppermute(value, 'dp', pairs)]
    another operation x33 -> x10, other arithmetic: 33.4 us -> 7.37 us  [the longest x4 5.85 us: to_rows(): jnp.stack([jnp.where(first, near, far), value[2 * half:], jnp.where(first...]
    reduce_sum x20 -> x0, other arithmetic: 21.4 us -> none  [the longest x4 6.07 us: attend(): total = jnp.sum(expo, axis=-1, keepdims=True)]
  transfers between devices with their start and end apart: 63 -> 38, of which waited for: 23 -> 14; matrix products, arithmetic and copies ran while one was open for 50% -> 8% of each run, Pallas kernels for 0% -> 27%
where the time goes in v2:
time: 526 us; the launch traced here: 520 us
  Pallas kernels  218 us (41%)
  waiting for transfers between devices  173 us (33%)
  local copies, waits for them, and re-layouts  49.6 us (9%)
  starting transfers between devices  37.1 us (7%)
  other arithmetic  26.4 us (5%)
  between operations  15.7 us (3%)
    pallas_call x14, Pallas kernels, call(): pl.pallas_call(body, grid=(steps,), in_specs=[pl.BlockSpec(block, index)...  183 us
    all_gather x1, waiting for transfers between devices, on_device(): lax.all_gather(jnp.concatenate(weight_parts, axis=1), ('mp', 'dp'), axis=...  107 us
    ppermute x15, waiting for transfers between devices, swap_y(): return lax.ppermute(value, 'mp', [(0, 1), (1, 0)])  42.1 us
    pallas_call x3, Pallas kernels, keep(): pl.pallas_call(body, grid_spec=pltpu.PrefetchScalarGridSpec(num_scalar_pr...  34.5 us
    unnamed x188, local copies, waits for them, and re-layouts  29.3 us
    ppermute x15, starting transfers between devices, swap_y(): return lax.ppermute(value, 'mp', [(0, 1), (1, 0)])  17.9 us
    ppermute x4, waiting for transfers between devices, _run(): lax.ppermute(self.total, 'dp', [(i, i ^ step) for i in range(n)])  13.9 us
  transfers between devices with their start and end apart: 38, of which 14 were waited for; matrix products, arithmetic and copies ran while one was open for 8% of the time, Pallas kernels for 27%

profile of v2, /device:TPU:0, one launch (start us, length us, event | category | flops | bytes accessed | tf_op | source)
XLA Modules:
  0.0 519.7 jit_solution(16896121707033907324)
XLA Ops:
  9.8 1.9 concatenate.75
  12.0 3.0 collective-permute-start.1
  16.0 1.3 select_bitcast_fusion.2
  18.3 2.0 collective-permute-start
  21.2 1.3 fusion
  22.8 25.7 %collective-permute-done = bf16[2,256,768]{2,1,0:T(8,128)(2,1)S(1)} collective-permute-done((bf16[2,256,768]{2,1,0:T(8,128)(2,1)}, bf16[2,256,768]{2,1,0:T(8,128)(2,1)S(1)}, u32[]{:S(2)}, u32[]{:S(2)}) %collective-permute-start) | collective-permute-done | bytes 786464 | tf_op jit(solution)/shard_map/ppermute | solution.py:21
  48.7 106.7 %all-gather.2.cloned.1.call-done = bf16[1536,7040]{1,0:T(8,128)(2,1)} async-done(((bf16[48,7040]{1,0:T(8,128)(2,1)}), bf16[1536,7040]{1,0:T(8,128)(2,1)}) %all-gather.2.cloned.1.call-update) | async-done | bytes 21626896 | tf_op jit(solution)/shard_map/all_gather | solution.py:872
  157.2 12.1 %shard_map.322 = (bf16[2,768,1152]{2,1,0:T(8,128)(2,1)S(1)}, bf16[2,512,384]{2,1,0:T(8,128)(2,1)S(1)}, f32[2,8,512]{2,1,0:T(8,128)S(1)}) custom-call(bf16[768,768]{1,0:T(8,128)(2,1)S(1)} %pad_maximum_fusion.2.rows.refs_0_, bf16[2,768,7040]{2,1,0:T(8,128)(2,1)} %bitcast.129, bf16[2,768,7040]{2,1,0:T(8,128)(2,1)} %bitcast.130, ...), custom_call_target="tpu_custom_call" | custom-call | flops 3523215360 | bytes 70431744 | tf_op jit(solution)/shard_map/pallas_call | solution.py:80
  169.4 1.9 copy-done
  171.2 30.4 %shard_map.323 = (bf16[2,256,1152]{2,1,0:T(8,128)(2,1)S(1)}, bf16[2,768,384]{2,1,0:T(8,128)(2,1)S(1)}, f32[2,8,256]{2,1,0:T(8,128)S(1)}, bf16[768,768]{1,0:T(8,1...) custom-call(bf16[768,768]{1,0:T(8,128)(2,1)} %copy-done.3, ...), custom_call_target="tpu_custom_call" | custom-call | flops 9462349824 | bytes 154605568 | tf_op jit(solution)/shard_map/pallas_call | solution.py:80
  202.7 2.1 slice.421
  204.8 1.5 collective-permute-start.2
  209.1 1.1 copy.84
  210.3 1.3 copy-done.12
  211.6 6.7 %shard_map.324 = (bf16[2,768,576]{2,1,0:T(8,128)(2,1)S(1)}, bf16[2,512,192]{2,1,0:T(8,128)(2,1)S(1)}, f32[2,8,512]{2,1,0:T(8,128)S(1)}) custom-call(bf16[768,768]{1,0:T(8,128)(2,1)S(1)} %copy-done.12, bf16[2,768,7040]{2,1,0:T(8,128)(2,1)} %bitcast.138, f32[2,1,576]{2,1,0:T(1,128)S(1)} %copy.74.refs_1_.refs_2_, ...), custom_call_target="tpu_custom_call" | custom-call | flops 1761607680 | bytes 25010688 | tf_op jit(solution)/shard_map/pallas_call | solution.py:80
  218.3 1.2 copy-done.1
  219.5 20.3 %shard_map.325 = (bf16[2,256,576]{2,1,0:T(8,128)(2,1)S(1)}, bf16[2,768,192]{2,1,0:T(8,128)(2,1)S(1)}, f32[2,8,256]{2,1,0:T(8,128)S(1)}, bf16[768,768]{1,0:T(8,12...) custom-call(f32[768,768]{1,0:T(8,128)} %get-tuple-element.131.rows, ...), custom_call_target="tpu_custom_call" | custom-call | flops 4731174912 | bytes 104459776 | tf_op jit(solution)/shard_map/pallas_call | solution.py:80
  239.9 14.2 %shard_map.326 = (bf16[768,768]{1,0:T(8,128)(2,1)S(1)}, bf16[2,768,768]{2,1,0:T(8,128)(2,1)}, f32[768,768]{1,0:T(8,128)}, bf16[768,768]{1,0:T(8,128)(2,1)S(1)}, ...) custom-call(bf16[768,768]{1,0:T(8,128)(2,1)S(1)} %pad_maximum_fusion.3.grad, ...), custom_call_target="tpu_custom_call" | custom-call | flops 3623878656 | bytes 56291328 | tf_op jit(solution)/shard_map/pallas_call | solution.py:80
  254.1 7.7 %shard_map.327 = (bf16[2,256,576]{2,1,0:T(8,128)(2,1)S(1)}, bf16[2,256,576]{2,1,0:T(8,128)(2,1)S(1)}, f32[2,8,576]{2,1,0:T(8,128)S(1)}, bf16[256,768]{1,0:T(8,128)(2,1)S(1)}) custom-call(bf16[768,768]{1,0:T(8,128)(2,1)S(1)} %get-tuple-element.142.d_mid.d_mid_low.refs_8_, bf16[2,768,576]{2,1,0:T(8,128)(2,1)S(1)} %copy-done.2, ...), custom_call_target="tpu_custom_call" | custom-call | flops 1107296256 | bytes 48421888 | tf_op jit(solution)/shard_map/pallas_call | solution.py:80
  263.1 12.9 %shard_map.328 = (bf16[2,768,576]{2,1,0:T(8,128)(2,1)S(1)}, f32[2,8,576]{2,1,0:T(8,128)S(1)}, f32[768,768]{1,0:T(8,128)}) custom-call(f32[768,768]{1,0:T(8,128)} %get-tuple-element.141.d_mid, bf16[768,768]{1,0:T(8,128)(2,1)S(1)} %get-tuple-element.142.d_mid.d_mid_low.refs_8_, bf16[2,256,576]{2,1,0:T(8,128)(2,1)S(1)} %get-tuple-element.145.d_shared, ...), custom_call_target="tpu_custom_call" | custom-call | flops 2667577344 | bytes 53354496 | tf_op jit(solution)/shard_map/pallas_call | solution.py:80
  276.6 1.2 copy-done.45
  278.7 9.8 %shard_map.329 = bf16[2,384,2304]{2,1,0:T(8,128)(2,1)} custom-call(bf16[384,768]{1,0:T(8,128)(2,1)S(1)} %get-tuple-element.251.pick, bf16[768,768]{1,0:T(8,128)(2,1)S(1)} %get-tuple-element.148.refs_0_, bf16[2,768,768]{2,1,0:T(8,128)(2,1)} %get-tuple-element.149.refs_1_, bf16[768,768]{1,0:T(8,128)(2,1)S(1)} %get-tuple-element.150.refs_2_, ...), custom_call_target="tpu_custom_call" | custom-call | flops 4907335680 | bytes 16908288 | tf_op jit(solution)/shard_map/pallas_call | solution.py:80
  288.6 1.3 copy-done.19
  291.8 10.9 %shard_map.330 = (f32[768,768]{1,0:T(8,128)S(1)}, bf16[768,768]{1,0:T(8,128)(2,1)S(1)}, bf16[2,768,1536]{2,1,0:T(8,128)(2,1)}, f32[8,768]{1,0:T(8,128)S(1)}, f32[4,1,768]{2,1,0:T(1,128)S(1)}) custom-call(f32[768,768]{1,0:T(8,128)} %get-tuple-element.157.grad, bf16[256,768]{1,0:T(8,128)(2,1)S(1)} %copy-done.30, bf16[768,768]{1,0:T(8,128)(2,1)S(1)} %copy-done.19, ...), custom_call_target="tpu_custom_call" | custom-call | flops 3623878656 | bytes 38599680 | tf_op jit(solution)/shard_map/pallas_call | solution.py:80
  302.8 1.4 copy-done.11
  304.9 14.2 %shard_map.331 = (bf16[384,1152]{1,0:T(8,128)(2,1)}, f32[384,1152]{1,0:T(8,128)}, bf16[2,192,1152]{2,1,0:T(8,128)(2,1)}, f32[2,192,1152]{2,1,0:T(8,128)}) custom-call(s32[2]{0:T(128)S(1)} %pad_add_fusion.2.order, bf16[384,768]{1,0:T(8,128)(2,1)S(1)} %get-tuple-element.250.pick, bf16[2,384,2304]{2,1,0:T(8,128)(2,1)} %collective-permute-done.6.got, ...), custom_call_target="tpu_custom_call" | custom-call | flops 4907335680 | bytes 8847360 | tf_op jit(solution)/shard_map/pallas_call | solution.py:726
  319.1 9.4 %shard_map.332 = bf16[2,384,3072]{2,1,0:T(8,128)(2,1)} custom-call(bf16[384,768]{1,0:T(8,128)(2,1)S(1)} %copy-done.9, bf16[768,768]{1,0:T(8,128)(2,1)S(1)} %get-tuple-element.169.refs_0_, bf16[2,768,1536]{2,1,0:T(8,128)(2,1)} %get-tuple-element.172.refs_1_.d_pre, bf16[768,768]{1,0:T(8,128)(2,1)S(1)} %get-tuple-element.170.refs_2_, ...), custom_call_target="tpu_custom_call" | custom-call | flops 4529848320 | bytes 17104896 | tf_op jit(solution)/shard_map/pallas_call | solution.py:80
  328.9 1.5 collective-permute-start.7
  331.0 1.9 slice.739
  332.9 1.3 copy.89
  334.2 1.4 collective-permute-start.3
  337.0 1.3 copy-done.18
  339.3 11.8 %shard_map.333 = (f32[768,768]{1,0:T(8,128)S(1)}, bf16[768,768]{1,0:T(8,128)(2,1)S(1)}, f32[8,768]{1,0:T(8,128)S(1)}) custom-call(f32[768,768]{1,0:T(8,128)} %copy-done.11, bf16[2,768,1536]{2,1,0:T(8,128)(2,1)} %get-tuple-element.172.refs_1_.d_pre, bf16[768,768]{1,0:T(8,128)(2,1)S(1)} %copy-done.18, f32[768,1]{1,0:T(8,128)S(1)} %copy-done.23, ...), custom_call_target="tpu_custom_call" | custom-call | flops 3623878656 | bytes 33475584 | tf_op jit(solution)/shard_map/pallas_call | solution.py:80
  352.0 1.7 convert_add_fusion.3
  354.6 1.4 convert_add_fusion.2
  357.8 1.1 collective-permute-start.10
  358.9 10.9 %shard_map.334 = (bf16[384,1536]{1,0:T(8,128)(2,1)S(1)}, f32[384,1536]{1,0:T(8,128)}, bf16[2,192,1536]{2,1,0:T(8,128)(2,1)S(1)}, f32[2,192,1536]{2,1,0:T(8,128)}) custom-call(s32[2]{0:T(128)S(1)} %copy-done.43, bf16[384,768]{1,0:T(8,128)(2,1)S(1)} %get-tuple-element.250.pick, bf16[2,384,3072]{2,1,0:T(8,128)(2,1)} %collective-permute-done.9.got, ...), custom_call_target="tpu_custom_call" | custom-call | flops 4529848320 | bytes 11796480 | tf_op jit(solution)/shard_map/pallas_call | solution.py:726
  371.7 10.3 %shard_map.335 = (bf16[2,256,1152]{2,1,0:T(8,128)(2,1)S(1)}, bf16[2,256,1152]{2,1,0:T(8,128)(2,1)S(1)}, f32[2,8,1152]{2,1,0:T(8,128)S(1)}, bf16[256,768]{1,0:T(8,128)(2,1)S(1)}) custom-call(bf16[768,768]{1,0:T(8,128)(2,1)S(1)} %get-tuple-element.187.d_mid.d_mid_low.refs_4_, bf16[2,768,1152]{2,1,0:T(8,128)(2,1)} %copy-done, ...), custom_call_target="tpu_custom_call" | custom-call | flops 2214592512 | bytes 95251456 | tf_op jit(solution)/shard_map/pallas_call | solution.py:80
  382.9 1.2 fusion.2
  385.4 19.7 %shard_map.336 = (bf16[2,768,1152]{2,1,0:T(8,128)(2,1)}, f32[2,8,1152]{2,1,0:T(8,128)S(1)}, f32[768,768]{1,0:T(8,128)S(1)}) custom-call(f32[768,768]{1,0:T(8,128)} %copy-done.7, bf16[768,768]{1,0:T(8,128)(2,1)S(1)} %get-tuple-element.187.d_mid.d_mid_low.refs_4_, bf16[2,256,1152]{2,1,0:T(8,128)(2,1)S(1)} %get-tuple-element.194.d_shared, ...), custom_call_target="tpu_custom_call" | custom-call | flops 5335154688 | bytes 100773888 | tf_op jit(solution)/shard_map/pallas_call | solution.py:80
  406.2 2.5 convert_add_fusion
  413.0 6.9 %shard_map.337 = bf16[2,384,1536]{2,1,0:T(8,128)(2,1)} custom-call(bf16[384,768]{1,0:T(8,128)(2,1)S(1)} %copy-done.10, bf16[768,768]{1,0:T(8,128)(2,1)S(1)} %copy-done.4, bf16[2,768,1152]{2,1,0:T(8,128)(2,1)} %get-tuple-element.204.refs_1_, bf16[256,768]{1,0:T(8,128)(2,1)S(1)} %copy-done.17, bf16[2,256,1152]{2,1,0:T(8,128)(2,1)S(1)} %get-tuple-element.205.refs_3_, ...), custom_call_target="tpu_custom_call" | custom-call | flops 3321888768 | bytes 11599872 | tf_op jit(solution)/shard_map/pallas_call | solution.py:80
  420.1 2.5 fusion.3
  424.7 1.1 collective-permute-start.18
  425.8 1.2 fusion.26
  428.7 1.6 pad_maximum_fusion
  432.0 9.0 %collective-permute-done.21 = f32[16128]{0:T(1024)S(1)} collective-permute-done((f32[16128]{0:T(1024)S(1)}, f32[16128]{0:T(1024)S(1)}, u32[]{:S(2)}, u32[]{:S(2)}) %collective-permute-start.21) | collective-permute-done | bytes 64544 | tf_op jit(solution)/shard_map/ppermute | solution.py:21
  445.3 9.5 %shard_map.338 = (bf16[384,768]{1,0:T(8,128)(2,1)S(1)}, f32[384,768]{1,0:T(8,128)S(1)}, bf16[2,192,768]{2,1,0:T(8,128)(2,1)S(1)}, f32[2,192,768]{2,1,0:T(8,128)S(1)}) custom-call(s32[2]{0:T(128)S(1)} %copy-done.44, bf16[384,768]{1,0:T(8,128)(2,1)S(1)} %get-tuple-element.250.pick, bf16[2,384,1536]{2,1,0:T(8,128)(2,1)} %collective-permute-done.17.got, ...), custom_call_target="tpu_custom_call" | custom-call | flops 3321888768 | bytes 5898240 | tf_op jit(solution)/shard_map/pallas_call | solution.py:726
  457.8 1.6 collective-permute-start.24
  459.4 2.3 collective-permute-done.13
  462.0 1.6 pad_maximum_fusion.1
  464.1 4.4 collective-permute-done.24
  468.5 4.5 collective-permute-done.22
  475.2 1.1 collective-permute-start.28
  478.1 5.0 collective-permute-done.30
  483.2 1.6 collective-permute-start.31
  484.9 1.5 collective-permute-start.32
  487.1 1.2 collective-permute-start.33
  489.0 6.3 %collective-permute-done.33 = f32[16128]{0:T(1024)S(1)} collective-permute-done((f32[16128]{0:T(1024)S(1)}, f32[16128]{0:T(1024)S(1)}, u32[]{:S(2)}, u32[]{:S(2)}) %collective-permute-start.33) | collective-permute-done | bytes 64544 | tf_op jit(solution)/shard_map/ppermute | solution.py:802
  495.4 1.3 collective-permute-start.35
  496.7 1.8 collective-permute-start.34
  499.3 2.7 collective-permute-done.35
  502.0 2.7 collective-permute-done.34
  508.6 2.6 collective-permute-done.36
  (344 shorter events, 58.7 us)
Async XLA Ops:
  7.2 148.1 %all-gather.2.cloned.1.call-start = ((), (), s32[]{:S(2)}) async-start(), calls=%async_computation | async-start | bytes 22302720 | tf_op jit(solution)/shard_map/all_gather | solution.py:872
  12.0 10.6 %collective-permute-start.1 = (bf16[3456]{0:T(1024)(128)(2,1)S(1)}, bf16[3456]{0:T(1024)(128)(2,1)S(1)}, u32[]{:S(2)}, u32[]{:S(2)}) collective-permute-start(bf16[3456]{0:T(1024)(128)(2,1)S(1)} %concatenate.76), channel_id=1, source_target_pairs={{0,1},{1,0},{2,3},{3,2},{4,5},{5,4},{6,7},{7,6},{8,9},{9,8},{10,11... | collective-permute-start | bytes 20744 | tf_op jit(solution)/shard_map/ppermute | solution.py:21
  16.0 190.3 %collective-permute-start.4 = (bf16[256,768]{1,0:T(8,128)(2,1)}, bf16[256,768]{1,0:T(8,128)(2,1)S(1)}, u32[]{:S(2)}, u32[]{:S(2)}) collective-permute-start(bf16[256,768]{1,0:T(8,128)(2,1)} %get-tuple-element.254), channel_id=1, source_target_pairs={{0,1},{1,0},{2,3},{3,2},{4,5},{5,4},{6,7},{7,6},{8,9},{9,8},{10,11... | collective-permute-start | bytes 1179656 | tf_op jit(solution)/shard_map/ppermute | solution.py:21
  18.3 30.1 %collective-permute-start = (bf16[2,256,768]{2,1,0:T(8,128)(2,1)}, bf16[2,256,768]{2,1,0:T(8,128)(2,1)S(1)}, u32[]{:S(2)}, u32[]{:S(2)}) collective-permute-start(bf16[2,256,768]{2,1,0:T(8,128)(2,1)} %pad_maximum_fusion.4), channel_id=1, source_target_pairs={{0,1},{1,0},{2,3},{3,2},{4,5},{5,4},{6,7},{7,6},{8,9},{9,8},{10,11... | collective-permute-start | bytes 2359304 | tf_op jit(solution)/shard_map/ppermute | solution.py:21
  48.5 122.7 %copy-start.16 = (bf16[256,768]{1,0:T(8,128)(2,1)}, bf16[256,768]{1,0:T(8,128)(2,1)S(1)}, u32[]{:S(2)}) copy-start(bf16[256,768]{1,0:T(8,128)(2,1)S(1)} %get-tuple-element.259.away.refs_2_) | copy-start | bytes 1179652
  48.5 108.5 %copy-start.90 = (pred[8]{0:T(512)(128)(4,1)S(1)}, pred[8]{0:T(512)(128)(4,1)}, u32[]{:S(2)}) copy-start(pred[8]{0:T(512)(128)(4,1)} %constant.114.clone.1) | copy-start | bytes 28
  48.6 120.7 %copy-start.3 = (bf16[768,768]{1,0:T(8,128)(2,1)}, bf16[768,768]{1,0:T(8,128)(2,1)S(1)}, u32[]{:S(2)}) copy-start(bf16[768,768]{1,0:T(8,128)(2,1)S(1)} %pad_maximum_fusion.2.rows.refs_0_) | copy-start | bytes 3538948
  171.2 35.9 %copy-start.74 = (bf16[256,768]{1,0:T(8,128)(2,1)S(1)}, bf16[256,768]{1,0:T(8,128)(2,1)}, u32[]{:S(2)}) copy-start(bf16[256,768]{1,0:T(8,128)(2,1)} %get-tuple-element.252) | copy-start | bytes 1179652
  171.2 35.9 %copy-start.75 = (bf16[256,768]{1,0:T(8,128)(2,1)S(1)}, bf16[256,768]{1,0:T(8,128)(2,1)}, u32[]{:S(2)}) copy-start(bf16[256,768]{1,0:T(8,128)(2,1)} %get-tuple-element.253) | copy-start | bytes 1179652
  204.8 14.7 %collective-permute-start.2 = (bf16[256,768]{1,0:T(8,128)(2,1)}, bf16[256,768]{1,0:T(8,128)(2,1)S(1)}, u32[]{:S(2)}, u32[]{:S(2)}) collective-permute-start(bf16[256,768]{1,0:T(8,128)(2,1)} %slice.421), channel_id=1, source_target_pairs={{0,1},{1,0},{2,3},{3,2},{4,5},{5,4},{6,7},{7,6},{8,9},{9,8},{10,11... | collective-permute-start | bytes 1179656 | tf_op jit(solution)/shard_map/ppermute | solution.py:21
  219.5 20.3 %copy-start.26 = (bf16[256,768]{1,0:T(8,128)(2,1)}, bf16[256,768]{1,0:T(8,128)(2,1)S(1)}, u32[]{:S(2)}) copy-start(bf16[256,768]{1,0:T(8,128)(2,1)S(1)} %collective-permute-done.2.away.refs_6_) | copy-start | bytes 1179652
  239.9 38.8 %copy-start.49 = (bf16[768,768]{1,0:T(8,128)(2,1)}, bf16[768,768]{1,0:T(8,128)(2,1)S(1)}, u32[]{:S(2)}) copy-start(bf16[768,768]{1,0:T(8,128)(2,1)S(1)} %get-tuple-element.148.refs_0_) | copy-start | bytes 3538948
  239.9 38.8 %copy-start.52 = (bf16[2,768,192]{2,1,0:T(8,128)(2,1)}, bf16[2,768,192]{2,1,0:T(8,128)(2,1)S(1)}, u32[]{:S(2)}) copy-start(bf16[2,768,192]{2,1,0:T(8,128)(2,1)S(1)} %get-tuple-element.156.refs_9_) | copy-start | bytes 1769476
  239.9 14.2 %copy-start.2 = (bf16[2,768,576]{2,1,0:T(8,128)(2,1)S(1)}, bf16[2,768,576]{2,1,0:T(8,128)(2,1)}, u32[]{:S(2)}) copy-start(bf16[2,768,576]{2,1,0:T(8,128)(2,1)} %copy-done.1) | copy-start | bytes 5308420
  254.1 24.6 %copy-start.51 = (bf16[768,768]{1,0:T(8,128)(2,1)}, bf16[768,768]{1,0:T(8,128)(2,1)S(1)}, u32[]{:S(2)}) copy-start(bf16[768,768]{1,0:T(8,128)(2,1)S(1)} %get-tuple-element.150.refs_2_) | copy-start | bytes 3538948
  262.4 16.2 %copy-start.54 = (bf16[2,256,576]{2,1,0:T(8,128)(2,1)}, bf16[2,256,576]{2,1,0:T(8,128)(2,1)S(1)}, u32[]{:S(2)}) copy-start(bf16[2,256,576]{2,1,0:T(8,128)(2,1)S(1)} %get-tuple-element.155.refs_7_) | copy-start | bytes 1769476
  262.5 15.4 %collective-permute-start.5 = (bf16[256,768]{1,0:T(8,128)(2,1)S(1)}, bf16[256,768]{1,0:T(8,128)(2,1)S(1)}, u32[]{:S(2)}, u32[]{:S(2)}) collective-permute-start(bf16[256,768]{1,0:T(8,128)(2,1)S(1)} %get-tuple-element.153), channel_id=1, source_target_pairs={{0,1},{1,0},{2,3},{3,2},{4,5},{5,4},{6,7},{7,6},{8,9},{9,8},{10,11... | collective-permute-start | bytes 1179656 | tf_op jit(solution)/shard_map/ppermute | solution.py:21
  263.1 15.6 %copy-start.8 = (bf16[384,768]{1,0:T(8,128)(2,1)}, bf16[384,768]{1,0:T(8,128)(2,1)S(1)}, u32[]{:S(2)}) copy-start(bf16[384,768]{1,0:T(8,128)(2,1)S(1)} %get-tuple-element.251.pick) | copy-start | bytes 1769476
  263.1 15.5 %copy-start.13 = (bf16[768,768]{1,0:T(8,128)(2,1)S(1)}, bf16[768,768]{1,0:T(8,128)(2,1)}, u32[]{:S(2)}) copy-start(bf16[768,768]{1,0:T(8,128)(2,1)} %get-tuple-element.132.rows.refs_4_) | copy-start | bytes 3538948
  263.1 15.5 %copy-start.27 = (bf16[256,768]{1,0:T(8,128)(2,1)S(1)}, bf16[256,768]{1,0:T(8,128)(2,1)}, u32[]{:S(2)}) copy-start(bf16[256,768]{1,0:T(8,128)(2,1)} %copy-done.26) | copy-start | bytes 1179652
  288.5 16.4 %collective-permute-start.6 = (bf16[2,384,2304]{2,1,0:T(8,128)(2,1)}, bf16[2,384,2304]{2,1,0:T(8,128)(2,1)}, u32[]{:S(2)}, u32[]{:S(2)}) collective-permute-start(bf16[2,384,2304]{2,1,0:T(8,128)(2,1)} %shard_map.329), channel_id=1, source_target_pairs={{0,2},{2,0},{4,6},{6,4},{8,10},{10,8},{12,14},{14,12},{16,18},{18,... | collective-permute-start | bytes 10616840 | tf_op jit(solution)/shard_map/ppermute | solution.py:31
  288.5 16.3 %copy-start.42 = (s32[2]{0:T(128)}, s32[2]{0:T(128)S(1)}, u32[]{:S(2)}) copy-start(s32[2]{0:T(128)S(1)} %pad_add_fusion.2.order) | copy-start | bytes 28
  291.8 13.0 %copy-start.28 = (bf16[256,768]{1,0:T(8,128)(2,1)S(1)}, bf16[256,768]{1,0:T(8,128)(2,1)}, u32[]{:S(2)}) copy-start(bf16[256,768]{1,0:T(8,128)(2,1)} %copy-done.26) | copy-start | bytes 1179652
  291.8 13.0 %copy-start.50 = (bf16[768,768]{1,0:T(8,128)(2,1)S(1)}, bf16[768,768]{1,0:T(8,128)(2,1)}, u32[]{:S(2)}) copy-start(bf16[768,768]{1,0:T(8,128)(2,1)} %copy-done.49) | copy-start | bytes 3538948
  291.8 13.0 %copy-start.53 = (bf16[2,768,192]{2,1,0:T(8,128)(2,1)S(1)}, bf16[2,768,192]{2,1,0:T(8,128)(2,1)}, u32[]{:S(2)}) copy-start(bf16[2,768,192]{2,1,0:T(8,128)(2,1)} %copy-done.52) | copy-start | bytes 1769476
  291.8 13.0 %copy-start.55 = (bf16[2,256,576]{2,1,0:T(8,128)(2,1)S(1)}, bf16[2,256,576]{2,1,0:T(8,128)(2,1)}, u32[]{:S(2)}) copy-start(bf16[2,256,576]{2,1,0:T(8,128)(2,1)} %copy-done.54) | copy-start | bytes 1769476
  304.8 14.2 %copy-start.33 = (f32[8,768]{1,0:T(8,128)}, f32[8,768]{1,0:T(8,128)S(1)}, u32[]{:S(2)}) copy-start(f32[8,768]{1,0:T(8,128)S(1)} %get-tuple-element.209) | copy-start | bytes 73732
  304.9 14.2 %copy-start.9 = (bf16[384,768]{1,0:T(8,128)(2,1)S(1)}, bf16[384,768]{1,0:T(8,128)(2,1)}, u32[]{:S(2)}) copy-start(bf16[384,768]{1,0:T(8,128)(2,1)} %copy-done.8) | copy-start | bytes 1769476
  328.4 30.4 %collective-permute-start.9 = (bf16[2,384,3072]{2,1,0:T(8,128)(2,1)}, bf16[2,384,3072]{2,1,0:T(8,128)(2,1)}, u32[]{:S(2)}, u32[]{:S(2)}) collective-permute-start(bf16[2,384,3072]{2,1,0:T(8,128)(2,1)} %shard_map.332), channel_id=1, source_target_pairs={{0,2},{2,0},{4,6},{6,4},{8,10},{10,8},{12,14},{14,12},{16,18},{18,... | collective-permute-start | bytes 14155784 | tf_op jit(solution)/shard_map/ppermute | solution.py:31
  328.9 22.8 %collective-permute-start.7 = (bf16[384,1152]{1,0:T(8,128)(2,1)}, bf16[384,1152]{1,0:T(8,128)(2,1)}, u32[]{:S(2)}, u32[]{:S(2)}) collective-permute-start(bf16[384,1152]{1,0:T(8,128)(2,1)} %get-tuple-element.166), channel_id=1, source_target_pairs={{0,1},{1,0},{2,3},{3,2},{4,5},{5,4},{6,7},{7,6},{8,9},{9,8},{10,11... | collective-permute-start | bytes 2654216 | tf_op jit(solution)/shard_map/ppermute | solution.py:21
  330.4 21.6 %collective-permute-start.8 = (bf16[2,192,1152]{2,1,0:T(8,128)(2,1)}, bf16[2,192,1152]{2,1,0:T(8,128)(2,1)}, u32[]{:S(2)}, u32[]{:S(2)}) collective-permute-start(bf16[2,192,1152]{2,1,0:T(8,128)(2,1)} %get-tuple-element.167), channel_id=1, source_target_pairs={{0,4},{2,6},{4,0},{6,2},{8,12},{10,14},{12,8},{14,10},{16,20},{18,... | collective-permute-start | bytes 2654216 | tf_op jit(solution)/shard_map/ppermute | solution.py:26
  334.2 85.9 %collective-permute-start.3 = (bf16[256,768]{1,0:T(8,128)(2,1)}, bf16[256,768]{1,0:T(8,128)(2,1)}, u32[]{:S(2)}, u32[]{:S(2)}) collective-permute-start(bf16[256,768]{1,0:T(8,128)(2,1)} %slice.739), channel_id=1, source_target_pairs={{0,1},{1,0},{2,3},{3,2},{4,5},{5,4},{6,7},{7,6},{8,9},{9,8},{10,11... | collective-permute-start | bytes 1179656 | tf_op jit(solution)/shard_map/ppermute | solution.py:21
  339.3 12.7 %copy-start.72 = (f32[384,1152]{1,0:T(8,128)S(1)}, f32[384,1152]{1,0:T(8,128)}, u32[]{:S(2)}) copy-start(f32[384,1152]{1,0:T(8,128)} %get-tuple-element.179) | copy-start | bytes 5308420
  351.2 60.7 %copy-start.6 = (bf16[768,768]{1,0:T(8,128)(2,1)}, bf16[768,768]{1,0:T(8,128)(2,1)S(1)}, u32[]{:S(2)}) copy-start(bf16[768,768]{1,0:T(8,128)(2,1)S(1)} %get-tuple-element.187.d_mid.d_mid_low.refs_4_) | copy-start | bytes 3538948
  356.8 15.0 %copy-start.21 = (bf16[2,256,1152]{2,1,0:T(8,128)(2,1)S(1)}, bf16[2,256,1152]{2,1,0:T(8,128)(2,1)}, u32[]{:S(2)}) copy-start(bf16[2,256,1152]{2,1,0:T(8,128)(2,1)} %copy-done.20) | copy-start | bytes 3538948
  356.8 25.3 %collective-permute-start.11 = (bf16[192,1152]{1,0:T(8,128)(2,1)}, bf16[192,1152]{1,0:T(8,128)(2,1)S(1)}, u32[]{:S(2)}, u32[]{:S(2)}) collective-permute-start(bf16[192,1152]{1,0:T(8,128)(2,1)} %fusion.18), channel_id=1, source_target_pairs={{0,1},{1,0},{2,3},{3,2},{4,5},{5,4},{6,7},{7,6},{8,9},{9,8},{10,11... | collective-permute-start | bytes 1327112 | tf_op jit(solution)/shard_map/ppermute | solution.py:21
  357.8 24.3 %collective-permute-start.10 = (bf16[192,1152]{1,0:T(8,128)(2,1)}, bf16[192,1152]{1,0:T(8,128)(2,1)S(1)}, u32[]{:S(2)}, u32[]{:S(2)}) collective-permute-start(bf16[192,1152]{1,0:T(8,128)(2,1)} %slice.737), channel_id=1, source_target_pairs={{0,4},{2,6},{4,0},{6,2},{8,12},{10,14},{12,8},{14,10},{16,20},{18,... | collective-permute-start | bytes 1327112 | tf_op jit(solution)/shard_map/ppermute | solution.py:26
  369.8 35.3 %collective-permute-start.14 = (bf16[384,1536]{1,0:T(8,128)(2,1)S(1)}, bf16[384,1536]{1,0:T(8,128)(2,1)S(1)}, u32[]{:S(2)}, u32[]{:S(2)}) collective-permute-start(bf16[384,1536]{1,0:T(8,128)(2,1)S(1)} %get-tuple-element.185), channel_id=1, source_target_pairs={{0,1},{1,0},{2,3},{3,2},{4,5},{5,4},{6,7},{7,6},{8,9},{9,8},{10,11... | collective-permute-start | bytes 3538952 | tf_op jit(solution)/shard_map/ppermute | solution.py:21
  370.6 34.4 %collective-permute-start.15 = (bf16[2,192,1536]{2,1,0:T(8,128)(2,1)S(1)}, bf16[2,192,1536]{2,1,0:T(8,128)(2,1)S(1)}, u32[]{:S(2)}, u32[]{:S(2)}) collective-permute-start(bf16[2,192,1536]{2,1,0:T(8,128)(2,1)S(1)} %get-tuple-element.186), channel_id=1, source_target_pairs={{0,4},{2,6},{4,0},{6,2},{8,12},{10,14},{12,8},{14,10},{16,20},{18,... | collective-permute-start | bytes 3538952 | tf_op jit(solution)/shard_map/ppermute | solution.py:26
  382.1 29.8 %copy-start.48 = (bf16[2,256,1152]{2,1,0:T(8,128)(2,1)}, bf16[2,256,1152]{2,1,0:T(8,128)(2,1)S(1)}, u32[]{:S(2)}) copy-start(bf16[2,256,1152]{2,1,0:T(8,128)(2,1)S(1)} %get-tuple-element.205.refs_3_) | copy-start | bytes 3538948
  384.2 20.9 %collective-permute-start.16 = (bf16[48,2304]{1,0:T(8,128)(2,1)S(1)}, bf16[48,2304]{1,0:T(8,128)(2,1)S(1)}, u32[]{:S(2)}, u32[]{:S(2)}) collective-permute-start(bf16[48,2304]{1,0:T(8,128)(2,1)S(1)} %fusion.23), channel_id=1, source_target_pairs={{0,8},{2,10},{4,12},{6,14},{16,0},{18,2},{20,4},{22,6},{24,16},{26... | collective-permute-start | bytes 663560 | tf_op jit(solution)/shard_map/ppermute | solution.py:41
  420.0 23.1 %collective-permute-start.17 = (bf16[2,384,1536]{2,1,0:T(8,128)(2,1)}, bf16[2,384,1536]{2,1,0:T(8,128)(2,1)}, u32[]{:S(2)}, u32[]{:S(2)}) collective-permute-start(bf16[2,384,1536]{2,1,0:T(8,128)(2,1)} %shard_map.337), channel_id=1, source_target_pairs={{0,2},{2,0},{4,6},{6,4},{8,10},{10,8},{12,14},{14,12},{16,18},{18,... | collective-permute-start | bytes 7077896 | tf_op jit(solution)/shard_map/ppermute | solution.py:31
  423.6 19.4 %collective-permute-start.19 = (bf16[192,1536]{1,0:T(8,128)(2,1)}, bf16[192,1536]{1,0:T(8,128)(2,1)S(1)}, u32[]{:S(2)}, u32[]{:S(2)}) collective-permute-start(bf16[192,1536]{1,0:T(8,128)(2,1)} %fusion.7), channel_id=1, source_target_pairs={{0,1},{1,0},{2,3},{3,2},{4,5},{5,4},{6,7},{7,6},{8,9},{9,8},{10,11... | collective-permute-start | bytes 1769480 | tf_op jit(solution)/shard_map/ppermute | solution.py:21
  424.7 18.4 %collective-permute-start.18 = (bf16[192,1536]{1,0:T(8,128)(2,1)}, bf16[192,1536]{1,0:T(8,128)(2,1)S(1)}, u32[]{:S(2)}, u32[]{:S(2)}) collective-permute-start(bf16[192,1536]{1,0:T(8,128)(2,1)} %slice.736), channel_id=1, source_target_pairs={{0,4},{2,6},{4,0},{6,2},{8,12},{10,14},{12,8},{14,10},{16,20},{18,... | collective-permute-start | bytes 1769480 | tf_op jit(solution)/shard_map/ppermute | solution.py:26
  427.0 15.0 %collective-permute-start.20 = (bf16[48,2304]{1,0:T(8,128)(2,1)S(1)}, bf16[48,2304]{1,0:T(8,128)(2,1)S(1)}, u32[]{:S(2)}, u32[]{:S(2)}) collective-permute-start(bf16[48,2304]{1,0:T(8,128)(2,1)S(1)} %fusion.26), channel_id=1, source_target_pairs={{0,8},{2,10},{4,12},{6,14},{16,0},{18,2},{20,4},{22,6},{24,16},{26... | collective-permute-start | bytes 663560 | tf_op jit(solution)/shard_map/ppermute | solution.py:41
  427.8 13.2 %collective-permute-start.21 = (f32[16128]{0:T(1024)S(1)}, f32[16128]{0:T(1024)S(1)}, u32[]{:S(2)}, u32[]{:S(2)}) collective-permute-start(f32[16128]{0:T(1024)S(1)} %constant_dynamic-update-slice_fusion), channel_id=1, source_target_pairs={{0,1},{1,0},{2,3},{3,2},{4,5},{5,4},{6,7},{7,6},{8,9},{9,8},{10,11... | collective-permute-start | bytes 193544 | tf_op jit(solution)/shard_map/ppermute | solution.py:21
  428.7 14.3 %copy-start.61 = (f32[2,192,1536]{2,1,0:T(8,128)S(1)}, f32[2,192,1536]{2,1,0:T(8,128)}, u32[]{:S(2)}) copy-start(f32[2,192,1536]{2,1,0:T(8,128)} %copy-done.60) | copy-start | bytes 7077892
  441.0 16.7 %collective-permute-start.12 = (bf16[256,768]{1,0:T(8,128)(2,1)}, bf16[256,768]{1,0:T(8,128)(2,1)S(1)}, u32[]{:S(2)}, u32[]{:S(2)}) collective-permute-start(bf16[256,768]{1,0:T(8,128)(2,1)} %slice.738), channel_id=1, source_target_pairs={{0,1},{1,0},{2,3},{3,2},{4,5},{5,4},{6,7},{7,6},{8,9},{9,8},{10,11... | collective-permute-start | bytes 1179656 | tf_op jit(solution)/shard_map/ppermute | solution.py:21
  442.0 19.7 %collective-permute-start.13 = (bf16[256,768]{1,0:T(8,128)(2,1)S(1)}, bf16[256,768]{1,0:T(8,128)(2,1)S(1)}, u32[]{:S(2)}, u32[]{:S(2)}) collective-permute-start(bf16[256,768]{1,0:T(8,128)(2,1)S(1)} %get-tuple-element.197), channel_id=1, source_target_pairs={{0,1},{1,0},{2,3},{3,2},{4,5},{5,4},{6,7},{7,6},{8,9},{9,8},{10,11... | collective-permute-start | bytes 1179656 | tf_op jit(solution)/shard_map/ppermute | solution.py:21
  454.8 9.3 %collective-permute-start.25 = (bf16[48,2304]{1,0:T(8,128)(2,1)S(1)}, bf16[48,2304]{1,0:T(8,128)(2,1)S(1)}, u32[]{:S(2)}, u32[]{:S(2)}) collective-permute-start(bf16[48,2304]{1,0:T(8,128)(2,1)S(1)} %fusion.21), channel_id=1, source_target_pairs={{0,8},{2,10},{4,12},{6,14},{16,0},{18,2},{20,4},{22,6},{24,16},{26... | collective-permute-start | bytes 663560 | tf_op jit(solution)/shard_map/ppermute | solution.py:41
  455.6 17.4 %collective-permute-start.22 = (bf16[384,768]{1,0:T(8,128)(2,1)S(1)}, bf16[384,768]{1,0:T(8,128)(2,1)S(1)}, u32[]{:S(2)}, u32[]{:S(2)}) collective-permute-start(bf16[384,768]{1,0:T(8,128)(2,1)S(1)} %get-tuple-element.219), channel_id=1, source_target_pairs={{0,1},{1,0},{2,3},{3,2},{4,5},{5,4},{6,7},{7,6},{8,9},{9,8},{10,11... | collective-permute-start | bytes 1769480 | tf_op jit(solution)/shard_map/ppermute | solution.py:21
  456.6 16.4 %collective-permute-start.23 = (bf16[2,192,768]{2,1,0:T(8,128)(2,1)S(1)}, bf16[2,192,768]{2,1,0:T(8,128)(2,1)S(1)}, u32[]{:S(2)}, u32[]{:S(2)}) collective-permute-start(bf16[2,192,768]{2,1,0:T(8,128)(2,1)S(1)} %get-tuple-element.220), channel_id=1, source_target_pairs={{0,4},{2,6},{4,0},{6,2},{8,12},{10,14},{12,8},{14,10},{16,20},{18,... | collective-permute-start | bytes 1769480 | tf_op jit(solution)/shard_map/ppermute | solution.py:26
  457.8 10.8 %collective-permute-start.24 = (bf16[48,3072]{1,0:T(8,128)(2,1)S(1)}, bf16[48,3072]{1,0:T(8,128)(2,1)S(1)}, u32[]{:S(2)}, u32[]{:S(2)}) collective-permute-start(bf16[48,3072]{1,0:T(8,128)(2,1)S(1)} %fusion.12), channel_id=1, source_target_pairs={{0,8},{2,10},{4,12},{6,14},{16,0},{18,2},{20,4},{22,6},{24,16},{26... | collective-permute-start | bytes 884744 | tf_op jit(solution)/shard_map/ppermute | solution.py:41
  461.9 1.6 collective-permute-start.26
  473.4 9.7 %collective-permute-start.29 = (bf16[48,3072]{1,0:T(8,128)(2,1)S(1)}, bf16[48,3072]{1,0:T(8,128)(2,1)S(1)}, u32[]{:S(2)}, u32[]{:S(2)}) collective-permute-start(bf16[48,3072]{1,0:T(8,128)(2,1)S(1)} %fusion.15), channel_id=1, source_target_pairs={{0,8},{2,10},{4,12},{6,14},{16,0},{18,2},{20,4},{22,6},{24,16},{26... | collective-permute-start | bytes 884744 | tf_op jit(solution)/shard_map/ppermute | solution.py:41
  474.2 8.8 %collective-permute-start.27 = (bf16[192,768]{1,0:T(8,128)(2,1)S(1)}, bf16[192,768]{1,0:T(8,128)(2,1)S(1)}, u32[]{:S(2)}, u32[]{:S(2)}) collective-permute-start(bf16[192,768]{1,0:T(8,128)(2,1)S(1)} %slice.740), channel_id=1, source_target_pairs={{0,4},{2,6},{4,0},{6,2},{8,12},{10,14},{12,8},{14,10},{16,20},{18,... | collective-permute-start | bytes 884744 | tf_op jit(solution)/shard_map/ppermute | solution.py:26
  475.2 7.9 %collective-permute-start.28 = (bf16[192,768]{1,0:T(8,128)(2,1)S(1)}, bf16[192,768]{1,0:T(8,128)(2,1)S(1)}, u32[]{:S(2)}, u32[]{:S(2)}) collective-permute-start(bf16[192,768]{1,0:T(8,128)(2,1)S(1)} %fusion.28), channel_id=1, source_target_pairs={{0,1},{1,0},{2,3},{3,2},{4,5},{5,4},{6,7},{7,6},{8,9},{9,8},{10,11... | collective-permute-start | bytes 884744 | tf_op jit(solution)/shard_map/ppermute | solution.py:21
  476.4 6.7 %collective-permute-start.30 = (f32[16128]{0:T(1024)S(1)}, f32[16128]{0:T(1024)S(1)}, u32[]{:S(2)}, u32[]{:S(2)}) collective-permute-start(f32[16128]{0:T(1024)S(1)} %add.233), channel_id=1, source_target_pairs={{0,4},{2,6},{4,0},{6,2},{8,12},{10,14},{12,8},{14,10},{16,20},{18,... | collective-permute-start | bytes 193544 | tf_op jit(solution)/shard_map/ppermute | solution.py:802
  483.2 12.0 %collective-permute-start.31 = (bf16[48,1536]{1,0:T(8,128)(2,1)S(1)}, bf16[48,1536]{1,0:T(8,128)(2,1)S(1)}, u32[]{:S(2)}, u32[]{:S(2)}) collective-permute-start(bf16[48,1536]{1,0:T(8,128)(2,1)S(1)} %fusion.37), channel_id=1, source_target_pairs={{0,8},{2,10},{4,12},{6,14},{16,0},{18,2},{20,4},{22,6},{24,16},{26... | collective-permute-start | bytes 442376 | tf_op jit(solution)/shard_map/ppermute | solution.py:41
  484.9 10.4 %collective-permute-start.32 = (bf16[48,3072]{1,0:T(8,128)(2,1)S(1)}, bf16[48,3072]{1,0:T(8,128)(2,1)S(1)}, u32[]{:S(2)}, u32[]{:S(2)}) collective-permute-start(bf16[48,3072]{1,0:T(8,128)(2,1)S(1)} %fusion.10), channel_id=1, source_target_pairs={{0,8},{2,10},{4,12},{6,14},{16,0},{18,2},{20,4},{22,6},{24,16},{26... | collective-permute-start | bytes 884744 | tf_op jit(solution)/shard_map/ppermute | solution.py:41
  487.1 8.2 %collective-permute-start.33 = (f32[16128]{0:T(1024)S(1)}, f32[16128]{0:T(1024)S(1)}, u32[]{:S(2)}, u32[]{:S(2)}) collective-permute-start(f32[16128]{0:T(1024)S(1)} %add.237), channel_id=1, source_target_pairs={{0,8},{2,10},{4,12},{6,14},{8,0},{10,2},{12,4},{14,6},{16,24},{18,... | collective-permute-start | bytes 193544 | tf_op jit(solution)/shard_map/ppermute | solution.py:802
  495.4 6.6 %collective-permute-start.35 = (f32[16128]{0:T(1024)S(1)}, f32[16128]{0:T(1024)S(1)}, u32[]{:S(2)}, u32[]{:S(2)}) collective-permute-start(f32[16128]{0:T(1024)S(1)} %add.239), channel_id=1, source_target_pairs={{0,16},{2,18},{4,20},{6,22},{8,24},{10,26},{12,28},{14,30},{16,0},... | collective-permute-start | bytes 193544 | tf_op jit(solution)/shard_map/ppermute | solution.py:802
  496.7 8.0 %collective-permute-start.34 = (bf16[48,1536]{1,0:T(8,128)(2,1)S(1)}, bf16[48,1536]{1,0:T(8,128)(2,1)S(1)}, u32[]{:S(2)}, u32[]{:S(2)}) collective-permute-start(bf16[48,1536]{1,0:T(8,128)(2,1)S(1)} %fusion.31), channel_id=1, source_target_pairs={{0,8},{2,10},{4,12},{6,14},{16,0},{18,2},{20,4},{22,6},{24,16},{26... | collective-permute-start | bytes 442376 | tf_op jit(solution)/shard_map/ppermute | solution.py:41
  504.9 6.4 %collective-permute-start.36 = (bf16[48,1536]{1,0:T(8,128)(2,1)S(1)}, bf16[48,1536]{1,0:T(8,128)(2,1)S(1)}, u32[]{:S(2)}, u32[]{:S(2)}) collective-permute-start(bf16[48,1536]{1,0:T(8,128)(2,1)S(1)} %fusion.36), channel_id=1, source_target_pairs={{0,8},{2,10},{4,12},{6,14},{16,0},{18,2},{20,4},{22,6},{24,16},{26... | collective-permute-start | bytes 442376 | tf_op jit(solution)/shard_map/ppermute | solution.py:41
  (65 other events, 212.3 us)
Sparse Core Ops, SparseCore 0:
  11.9 143.4 all-gather.1
